TPU v7x, 32 devices: a whole 2x2x4 slice. The times are simulated.
32 devices in a mesh: rep: 2 (over x), shard: 16 (over z, y, core).
Axes of the slice: x: 2, y: 2, z: 4, core: 2. Of those that a mesh axis runs over, the one named last changes fastest.
Arguments:
- hidden_in: bfloat16 [8192, 768], P(('rep', 'shard')), may hold values from -6 to 6
- gate_in: float32 [8192, 8], P(('rep', 'shard')), may hold values from -4 to 4
- routes: int32 [2, 8192, 2], P(None, ('rep', 'shard')), may hold values from 0 to 7, all different within a row
- priority: int32 [2, 32, 512], P(None, ('rep', 'shard')), may hold values from 0 to 511, each once within a row
- segments: int32 [32, 256], P(('rep', 'shard')), may hold values from 0 to 3, never falling along the last dimension, each value on 1 to 128 neighbouring positions
- norm_attn: bfloat16 [2, 768], P(None, 'shard'), may hold values from 0.25 to 1.75
- w_qkv: bfloat16 [2, 768, 2304], P(None, 'shard'), may hold values from -0.21875 to 0.21875
- w_out: bfloat16 [2, 768, 768], P(None, 'shard'), may hold values from -0.875 to 0.875
- norm_moe: bfloat16 [2, 768], P(None, 'shard'), may hold values from 0.25 to 1.75
- w_router: bfloat16 [2, 768, 8], P(None, 'shard'), may hold values from -0.109375 to 0.109375
- w_const: bfloat16 [2, 768, 4], P(None, 'shard'), may hold values from -0.21875 to 0.21875
- const_vec: bfloat16 [2, 2, 768], P(None, None, 'shard'), may hold values from -5 to 5
- w_gate_up: bfloat16 [2, 4, 768, 4096], P(None, None, 'shard'), may hold values from -0.21875 to 0.21875
- w_down: bfloat16 [2, 4, 2048, 768], P(None, None, 'shard'), may hold values from -0.25 to 0.25
- grad_out: float32 [8192, 768], P(('rep', 'shard')), may hold values from -6 to 6
Outputs:
- hidden_out: bfloat16 [8192, 768], P(('rep', 'shard'))
- grad_hidden: float32 [8192, 768], P(('rep', 'shard'))
- grad_gate: float32 [8192, 8], P(('rep', 'shard'))
- grad_norm_attn: float32 [2, 768], P(None, 'shard')
- grad_qkv: float32 [2, 768, 2304], P(None, 'shard')
- grad_out_proj: float32 [2, 768, 768], P(None, 'shard')
- grad_norm_moe: float32 [2, 768], P(None, 'shard')
- grad_router: float32 [2, 768, 8], P(None, 'shard')
- grad_const_mix: float32 [2, 768, 4], P(None, 'shard')
- grad_const_vec: float32 [2, 2, 768], P(None, None, 'shard')
- grad_gate_up: float32 [2, 4, 768, 4096], P(None, None, 'shard')
- grad_down: float32 [2, 4, 2048, 768], P(None, None, 'shard')
Inputs may be any that keep to these rules, and one draw needn't show every extreme that they name: Each token's 2 routes name different experts; experts below 4 have feed-forward weights, 4 is the zero expert, 5 the copy expert, the rest constant experts. `priority`: for each layer and device the 512 ranks are a permutation; rank of pair t * 2 + k belongs to the device's token t and its k-th route. `segments`: document numbers never fall along a device's row; each document has 1 to 128 tokens and one has exactly that many.
All inputs are finite; a program needn't handle non-finite values.
Results may differ from a plain program's by a relative error of at most 0.02.
Values may be sent and summed in bfloat16 or wider, within the bound.
No kernel may reach another device: no remote copies, remote signals or barrier semaphores. Data moves between devices by JAX's collectives and lax.ppermute only.
A program may use at most 448 MiB of HBM per device.

v0:
```python
import math

import jax
import jax.numpy as jnp
from jax import lax
from jax.sharding import PartitionSpec as P

HEAD_DIM = 64
EF = 4
NCONST = 2
TOP = 2
EXPERTS = 8
CAP = 80


EPSILON = 1e-06
SCALE = 0.125
MASKED = -1000000000.0
HIGHEST_PRECISION = lax.Precision.HIGHEST


def rope_tables(tokens, head_size):
    half = head_size // 2
    places = jnp.arange(tokens, dtype=jnp.int32).astype(jnp.float32)[:, None]
    powers = jnp.arange(half, dtype=jnp.int32).astype(jnp.float32) / half
    angles = places * jnp.exp(-math.log(10000.0) * powers)[None, :]
    return (jnp.cos(angles)[:, None, :], jnp.sin(angles)[:, None, :])


def rotate(source, cosine, sine):
    half = source.shape[-1] // 2
    first, second = (source[..., :half], source[..., half:])
    return jnp.concatenate(
        [first * cosine - second * sine, second * cosine + first * sine], axis=-1
    )


def rotate_back(grad_rows, cosine, sine):
    half = grad_rows.shape[-1] // 2
    first, second = (grad_rows[..., :half], grad_rows[..., half:])
    return jnp.concatenate(
        [first * cosine + second * sine, second * cosine - first * sine], axis=-1
    )


def softmax_rows(scores):
    shifted = jnp.exp(scores - jnp.max(scores, axis=-1, keepdims=True))
    return shifted / jnp.sum(shifted, axis=-1, keepdims=True)


def place_pairs(routes_now, order_now, ffn_count, capacity):
    flat_routes = routes_now.reshape(-1)
    pair_count = flat_routes.shape[0]
    numbers = jnp.arange(pair_count, dtype=jnp.int32)
    pair_at_rank = jnp.zeros((pair_count,), jnp.int32).at[order_now].set(numbers)
    route_by_rank = flat_routes[pair_at_rank]
    expert_ids = jnp.arange(EXPERTS, dtype=jnp.int32)
    hot_rank = (route_by_rank[:, None] == expert_ids[None, :]).astype(jnp.int32)
    before = jnp.cumsum(hot_rank, axis=0) - hot_rank
    place_by_rank = jnp.sum(before * hot_rank, axis=1)
    position = place_by_rank[order_now]
    accepted = (flat_routes < ffn_count) & (position < capacity)
    sink = ffn_count * capacity
    slot_of_pair = jnp.where(accepted, flat_routes * capacity + position, sink)
    token_of_slot = (
        jnp.full((sink + 1,), routes_now.shape[0], jnp.int32)
        .at[slot_of_pair]
        .set(numbers // routes_now.shape[1])[:sink]
    )
    pair_of_slot = jnp.full((sink + 1,), pair_count, jnp.int32).at[slot_of_pair].set(numbers)[:sink]
    return (slot_of_pair, token_of_slot, pair_of_slot)


def doc_mask(segment, row_start, row_stop):
    rows = jnp.arange(row_start, row_stop, dtype=jnp.int32)
    columns = jnp.arange(row_stop, dtype=jnp.int32)
    same_doc = segment[row_start:row_stop, None] == segment[None, :row_stop]
    return same_doc & (columns[None, :] <= rows[:, None])


def norm_back(grad_rows, source, inverse, gain):
    scaled = grad_rows * gain
    gain_grad = jnp.sum(grad_rows * source * inverse, axis=0)
    source_grad = inverse * scaled - source * inverse**3 * jnp.mean(
        scaled * source, axis=-1, keepdims=True
    )
    return (source_grad, gain_grad)


def swiglu_back(d_activated, gate_up, hidden_units):
    gate_part, up_part = (gate_up[..., :hidden_units], gate_up[..., hidden_units:])
    sigmoid_gate = jax.nn.sigmoid(gate_part)
    return jnp.concatenate(
        [
            d_activated * up_part * sigmoid_gate * (1.0 + gate_part * (1.0 - sigmoid_gate)),
            d_activated * gate_part * sigmoid_gate,
        ],
        axis=-1,
    ).astype(jnp.bfloat16)


def experts_forward(inputs, w_gate_up, w_down):
    features = inputs.shape[-1]
    hidden_units = w_down.shape[1]
    gate_up = jnp.einsum("ecd,edf->ecf", inputs, w_gate_up, preferred_element_type=jnp.float32)
    gate_part = gate_up[..., :hidden_units]
    activated = (gate_part * jax.nn.sigmoid(gate_part) * gate_up[..., hidden_units:]).astype(
        jnp.bfloat16
    )
    expert_out = jnp.einsum(
        "ecf,efd->ecd", activated, w_down, preferred_element_type=jnp.float32
    ).reshape(EF * CAP, features)
    return (expert_out, (inputs, gate_up, activated))


def experts_backward(d_expert, saved, w_gate_up, w_down):
    features = d_expert.shape[-1]
    hidden_units = w_down.shape[1]
    source_rows, gate_up, activated = saved
    d_activated = jnp.einsum("ecd,efd->ecf", d_expert, w_down, preferred_element_type=jnp.float32)
    grad_down = jnp.einsum("ecf,ecd->efd", activated, d_expert, preferred_element_type=jnp.float32)
    d_gate_up = swiglu_back(d_activated, gate_up, hidden_units)
    grad_gate_up = jnp.einsum(
        "ecd,ecf->edf", source_rows, d_gate_up, preferred_element_type=jnp.float32
    )
    d_inputs = jnp.einsum(
        "ecf,edf->ecd", d_gate_up, w_gate_up, preferred_element_type=jnp.float32
    ).reshape(EF * CAP, features)
    return (d_inputs, grad_gate_up, grad_down)


def forward_layer(full, hidden, previous, routes_now, order_now, segment, cosine, sine):
    gain_attn, w_qkv, w_out, gain_moe, w_router, w_const, const_vec, w_gate_up, w_down = full
    tokens, features = hidden.shape
    head_count = features // HEAD_DIM
    ffn_count = EF
    inv_attn = lax.rsqrt(jnp.mean(hidden * hidden, axis=-1, keepdims=True) + EPSILON)
    normed = (hidden * inv_attn * gain_attn.astype(jnp.float32)).astype(jnp.bfloat16)
    projected = jnp.dot(normed, w_qkv, preferred_element_type=jnp.float32).reshape(
        tokens, 3, head_count, HEAD_DIM
    )
    query = rotate(projected[:, 0], cosine, sine).astype(jnp.bfloat16)
    keys = rotate(projected[:, 1], cosine, sine).astype(jnp.bfloat16)
    values = projected[:, 2].astype(jnp.bfloat16)
    block_rows = min(512, tokens)
    scores = jnp.einsum("qhd,khd->hqk", query, keys, preferred_element_type=jnp.float32) * SCALE
    scores = jnp.where(doc_mask(segment, 0, block_rows)[None], scores, MASKED)
    row_max = jnp.max(scores, axis=-1, keepdims=True)
    weight = jnp.exp(scores - row_max)
    total = jnp.sum(weight, axis=-1, keepdims=True)
    probs = (weight / total).astype(jnp.bfloat16)
    outputs = jnp.einsum("hqk,khd->qhd", probs, values, preferred_element_type=jnp.float32)
    totals = row_max + jnp.log(total)
    attended = outputs.reshape(tokens, features).astype(jnp.bfloat16)
    middle = hidden + jnp.dot(attended, w_out, preferred_element_type=jnp.float32)
    inv_moe = lax.rsqrt(jnp.mean(middle * middle, axis=-1, keepdims=True) + EPSILON)
    mixed_in = middle * inv_moe * gain_moe.astype(jnp.float32)
    mixed_low = mixed_in.astype(jnp.bfloat16)
    logits = jnp.dot(mixed_low, w_router, preferred_element_type=jnp.float32) + previous
    route_hot = (
        routes_now[:, :, None] == jnp.arange(EXPERTS, dtype=jnp.int32)[None, None, :]
    ).astype(jnp.float32)
    gate_probs = softmax_rows(jnp.sum(route_hot * logits[:, None, :], axis=-1))
    shares = softmax_rows(
        jnp.dot(mixed_low, w_const, preferred_element_type=jnp.float32).reshape(tokens, NCONST, 2)
    )
    constant = (
        shares[..., 0:1] * mixed_in[:, None, :]
        + shares[..., 1:2] * const_vec.astype(jnp.float32)[None]
    )
    slot_of_pair, token_of_slot, pair_of_slot = place_pairs(routes_now, order_now, ffn_count, CAP)
    padded = jnp.concatenate([mixed_low, jnp.zeros((1, features), jnp.bfloat16)], axis=0)
    inputs = padded[token_of_slot].reshape(ffn_count, CAP, features)
    expert_out, saved = experts_forward(inputs, w_gate_up, w_down)
    out_padded = jnp.concatenate([expert_out, jnp.zeros((1, features), jnp.float32)], axis=0)
    pair_out = out_padded[slot_of_pair].reshape(tokens, TOP, features)
    copy_flag = (routes_now == ffn_count + 1).astype(jnp.float32)
    const_flag = (
        routes_now[:, :, None] == ffn_count + 2 + jnp.arange(NCONST, dtype=jnp.int32)[None, None, :]
    ).astype(jnp.float32)
    pair_value = (
        pair_out
        + copy_flag[..., None] * mixed_in[:, None, :]
        + jnp.sum(const_flag[..., None] * constant[:, None, :, :], axis=2)
    )
    result = middle + jnp.sum(gate_probs[..., None] * pair_value, axis=1)
    kept = (
        hidden,
        inv_attn,
        normed,
        query,
        keys,
        values,
        totals,
        attended,
        middle,
        inv_moe,
        mixed_in,
        mixed_low,
        route_hot,
        gate_probs,
        shares,
        pair_value,
        slot_of_pair,
        pair_of_slot,
        saved,
        copy_flag,
        const_flag,
    )
    return (result, logits, kept)


def backward_layer(full, kept, grad_result, grad_next, segment, cosine, sine):
    (
        hidden,
        inv_attn,
        normed,
        query,
        keys,
        values,
        log_totals,
        attended,
        middle,
        inv_moe,
        mixed_in,
        mixed_low,
        route_hot,
        gate_probs,
        shares,
        pair_value,
        slot_of_pair,
        pair_of_slot,
        saved,
        copy_flag,
        const_flag,
    ) = kept
    gain_attn, w_qkv, w_out, gain_moe, w_router, w_const, const_vec, w_gate_up, w_down = full
    tokens, features = hidden.shape
    head_count = features // HEAD_DIM
    ffn_count = EF
    d_value = gate_probs[..., None] * grad_result[:, None, :]
    d_gates = jnp.sum(pair_value * grad_result[:, None, :], axis=-1)
    d_chosen = gate_probs * (d_gates - jnp.sum(gate_probs * d_gates, axis=-1, keepdims=True))
    d_logits = jnp.sum(route_hot * d_chosen[..., None], axis=1) + grad_next
    pair_grads = jnp.concatenate(
        [d_value.reshape(tokens * TOP, features), jnp.zeros((1, features), jnp.float32)], axis=0
    )
    d_expert = pair_grads[pair_of_slot].reshape(ffn_count, CAP, features).astype(jnp.bfloat16)
    d_inputs, grad_gate_up, grad_down = experts_backward(d_expert, saved, w_gate_up, w_down)
    d_padded = jnp.concatenate([d_inputs, jnp.zeros((1, features), jnp.float32)], axis=0)
    d_mixed_low = jnp.sum(d_padded[slot_of_pair].reshape(tokens, TOP, features), axis=1)
    const_grads = jnp.sum(const_flag[..., None] * d_value[:, :, None, :], axis=1)
    vector_wide = const_vec.astype(jnp.float32)
    d_shares = jnp.stack(
        [
            jnp.sum(const_grads * mixed_in[:, None, :], axis=-1),
            jnp.sum(const_grads * vector_wide[None], axis=-1),
        ],
        axis=-1,
    )
    d_mix = (shares * (d_shares - jnp.sum(shares * d_shares, axis=-1, keepdims=True))).reshape(
        tokens, 2 * NCONST
    )
    grad_const_vec = jnp.sum(shares[..., 1:2] * const_grads, axis=0)
    d_mixed = jnp.sum(copy_flag[..., None] * d_value, axis=1) + jnp.sum(
        shares[..., 0:1] * const_grads, axis=1
    )
    mixed_wide = mixed_low.astype(jnp.float32)
    d_mixed_low = (
        d_mixed_low
        + jnp.dot(d_mix, w_const.astype(jnp.float32).T, precision=HIGHEST_PRECISION)
        + jnp.dot(d_logits, w_router.astype(jnp.float32).T, precision=HIGHEST_PRECISION)
    )
    grad_const = jnp.dot(mixed_wide.T, d_mix, precision=HIGHEST_PRECISION)
    grad_router = jnp.dot(mixed_wide.T, d_logits, precision=HIGHEST_PRECISION)
    d_middle, grad_gain_moe = norm_back(
        d_mixed + d_mixed_low, middle, inv_moe, gain_moe.astype(jnp.float32)
    )
    d_middle = d_middle + grad_result
    d_branch = d_middle.astype(jnp.bfloat16)
    grad_out_proj = jnp.einsum("td,te->de", attended, d_branch, preferred_element_type=jnp.float32)
    d_attended = (
        jnp.einsum("te,de->td", d_branch, w_out, preferred_element_type=jnp.float32)
        .astype(jnp.bfloat16)
        .reshape(tokens, head_count, HEAD_DIM)
    )
    block_rows = min(512, tokens)
    d_keys = jnp.zeros((tokens, head_count, HEAD_DIM), jnp.float32)
    d_values = jnp.zeros((tokens, head_count, HEAD_DIM), jnp.float32)
    scores = jnp.einsum("qhd,khd->hqk", query, keys, preferred_element_type=jnp.float32) * SCALE
    scores = jnp.where(doc_mask(segment, 0, block_rows)[None], scores, MASKED)
    probs = jnp.exp(scores - log_totals)
    probs_low = probs.astype(jnp.bfloat16)
    d_values = d_values.at[:block_rows].add(
        jnp.einsum("hqk,qhd->khd", probs_low, d_attended, preferred_element_type=jnp.float32)
    )
    d_probs = jnp.einsum("qhd,khd->hqk", d_attended, values, preferred_element_type=jnp.float32)
    d_scores = (probs * (d_probs - jnp.sum(d_probs * probs, axis=-1, keepdims=True))).astype(
        jnp.bfloat16
    )
    query_parts = (
        jnp.einsum("hqk,khd->qhd", d_scores, keys, preferred_element_type=jnp.float32) * SCALE
    )
    d_keys = d_keys.at[:block_rows].add(
        jnp.einsum("hqk,qhd->khd", d_scores, query, preferred_element_type=jnp.float32) * SCALE
    )
    d_projected = (
        jnp.stack(
            [rotate_back(query_parts, cosine, sine), rotate_back(d_keys, cosine, sine), d_values],
            axis=1,
        )
        .reshape(tokens, 3 * features)
        .astype(jnp.bfloat16)
    )
    grad_qkv = jnp.einsum("td,te->de", normed, d_projected, preferred_element_type=jnp.float32)
    d_normed = jnp.einsum("te,de->td", d_projected, w_qkv, preferred_element_type=jnp.float32)
    d_hidden, grad_gain_attn = norm_back(d_normed, hidden, inv_attn, gain_attn.astype(jnp.float32))
    d_hidden = d_hidden + d_middle
    return (
        d_hidden,
        d_logits,
        (
            grad_gain_attn,
            grad_qkv,
            grad_out_proj,
            grad_gain_moe,
            grad_router,
            grad_const,
            grad_const_vec,
            grad_gate_up,
            grad_down,
        ),
    )


def local(
    hidden_in,
    gate_in,
    routes,
    priority,
    segments,
    norm_attn,
    w_qkv,
    w_out,
    norm_moe,
    w_router,
    w_const,
    const_vec,
    w_gate_up,
    w_down,
    grad_out,
):
    layer_count = w_qkv.shape[0]
    segment = segments[0]
    cosine, sine = rope_tables(hidden_in.shape[0], HEAD_DIM)
    hidden = hidden_in.astype(jnp.float32)
    previous = gate_in
    kept_layers = []
    full_layers = []
    for layer_index in range(layer_count):
        full = (
            lax.all_gather(norm_attn[layer_index], "shard", axis=0, tiled=True),
            lax.all_gather(w_qkv[layer_index], "shard", axis=0, tiled=True),
            lax.all_gather(w_out[layer_index], "shard", axis=0, tiled=True),
            lax.all_gather(norm_moe[layer_index], "shard", axis=0, tiled=True),
            lax.all_gather(w_router[layer_index], "shard", axis=0, tiled=True),
            lax.all_gather(w_const[layer_index], "shard", axis=0, tiled=True),
            lax.all_gather(const_vec[layer_index], "shard", axis=1, tiled=True),
            lax.all_gather(w_gate_up[layer_index], "shard", axis=1, tiled=True),
            lax.all_gather(w_down[layer_index], "shard", axis=1, tiled=True),
        )
        hidden, previous, kept = forward_layer(
            full,
            hidden,
            previous,
            routes[layer_index],
            priority[layer_index, 0],
            segment,
            cosine,
            sine,
        )
        kept_layers.append(kept)
        full_layers.append(full)
    grad_hidden = grad_out
    grad_gate = jnp.zeros_like(gate_in)
    summed_layers = [0] * layer_count
    for layer_index in reversed(range(layer_count)):
        full = (
            lax.all_gather(norm_attn[layer_index], "shard", axis=0, tiled=True),
            lax.all_gather(w_qkv[layer_index], "shard", axis=0, tiled=True),
            lax.all_gather(w_out[layer_index], "shard", axis=0, tiled=True),
            lax.all_gather(norm_moe[layer_index], "shard", axis=0, tiled=True),
            lax.all_gather(w_router[layer_index], "shard", axis=0, tiled=True),
            lax.all_gather(w_const[layer_index], "shard", axis=0, tiled=True),
            lax.all_gather(const_vec[layer_index], "shard", axis=1, tiled=True),
            lax.all_gather(w_gate_up[layer_index], "shard", axis=1, tiled=True),
            lax.all_gather(w_down[layer_index], "shard", axis=1, tiled=True),
        )
        grad_hidden, grad_gate, terms = backward_layer(
            full, kept_layers[layer_index], grad_hidden, grad_gate, segment, cosine, sine
        )
        (
            term_attn,
            term_qkv,
            term_proj,
            term_moe,
            term_router,
            term_const,
            term_vec,
            term_gate_up,
            term_down,
        ) = terms
        pieces = (
            lax.psum_scatter(term_attn, "shard", scatter_dimension=0, tiled=True),
            lax.psum_scatter(term_qkv, "shard", scatter_dimension=0, tiled=True),
            lax.psum_scatter(term_proj, "shard", scatter_dimension=0, tiled=True),
            lax.psum_scatter(term_moe, "shard", scatter_dimension=0, tiled=True),
            lax.psum_scatter(term_router, "shard", scatter_dimension=0, tiled=True),
            lax.psum_scatter(term_const, "shard", scatter_dimension=0, tiled=True),
            lax.psum_scatter(term_vec, "shard", scatter_dimension=1, tiled=True),
            lax.psum_scatter(term_gate_up, "shard", scatter_dimension=1, tiled=True),
            lax.psum_scatter(term_down, "shard", scatter_dimension=1, tiled=True),
        )
        summed = (
            lax.psum(pieces[0].astype(jnp.bfloat16), "rep").astype(jnp.float32),
            lax.psum(pieces[1].astype(jnp.bfloat16), "rep").astype(jnp.float32),
            lax.psum(pieces[2].astype(jnp.bfloat16), "rep").astype(jnp.float32),
            lax.psum(pieces[3].astype(jnp.bfloat16), "rep").astype(jnp.float32),
            lax.psum(pieces[4].astype(jnp.bfloat16), "rep").astype(jnp.float32),
            lax.psum(pieces[5].astype(jnp.bfloat16), "rep").astype(jnp.float32),
            lax.psum(pieces[6].astype(jnp.bfloat16), "rep").astype(jnp.float32),
            lax.psum(pieces[7].astype(jnp.bfloat16), "rep").astype(jnp.float32),
            lax.psum(pieces[8].astype(jnp.bfloat16), "rep").astype(jnp.float32),
        )
        summed_layers[layer_index] = summed
    stacked = [
        jnp.stack([summed_layers[layer_index][member] for layer_index in range(layer_count)])
        for member in range(9)
    ]
    return (
        hidden.astype(jnp.bfloat16),
        grad_hidden,
        grad_gate,
        stacked[0],
        stacked[1],
        stacked[2],
        stacked[3],
        stacked[4],
        stacked[5],
        stacked[6],
        stacked[7],
        stacked[8],
    )


def solution(mesh):
    return jax.shard_map(
        local,
        mesh=mesh,
        in_specs=(
            P(("rep", "shard"), None),
            P(("rep", "shard"), None),
            P(None, ("rep", "shard"), None),
            P(None, ("rep", "shard"), None),
            P(("rep", "shard"), None),
            P(None, "shard"),
            P(None, "shard", None),
            P(None, "shard", None),
            P(None, "shard"),
            P(None, "shard", None),
            P(None, "shard", None),
            P(None, None, "shard"),
            P(None, None, "shard", None),
            P(None, None, "shard", None),
            P(("rep", "shard"), None),
        ),
        out_specs=(
            P(("rep", "shard"), None),
            P(("rep", "shard"), None),
            P(("rep", "shard"), None),
            P(None, "shard"),
            P(None, "shard", None),
            P(None, "shard", None),
            P(None, "shard"),
            P(None, "shard", None),
            P(None, "shard", None),
            P(None, None, "shard"),
            P(None, None, "shard", None),
            P(None, None, "shard", None),
        ),
        check_vma=False,
    )
```

profile of v0, /device:TPU:8, one launch (start us, length us, event | category | flops | bytes accessed | tf_op | source)
XLA Modules:
  0.0 3010.7 jit_solution(5413974284276612052)
XLA Ops:
  22.3 26.3 all-reduce.17
  48.8 23.7 all-gather.8
  73.2 21.0 all-gather.7
  103.1 19.6 all-gather.4
  146.5 22.5 all-gather.13
  169.4 20.6 all-gather.17
  191.3 22.0 all-gather.16
  259.0 87.1 %all-gather.33.cloned.1.call-done = bf16[1,4,2048,768]{3,2,1,0:T(8,128)(2,1)} async-done(((bf16[1,4,128,768]{3,2,1,0:T(8,128)(2,1)}), bf16[1,4,2048,768]{3,2,1,0:T(8,128)(2,1)}) %all-gather.33.cloned.1.call-update) | async-done | bytes 12582928 | tf_op jit(solution)/shard_map/all_gather | solution.py:370
  361.9 34.2 %all-gather.35.cloned.1.call-done = bf16[1,768,2304]{2,1,0:T(8,128)(2,1)} async-done(((bf16[1,48,2304]{2,1,0:T(8,128)(2,1)}), bf16[1,768,2304]{2,1,0:T(8,128)(2,1)}) %all-gather.35.cloned.1.call-update) | async-done | bytes 3538960 | tf_op jit(solution)/shard_map/all_gather | solution.py:363
  403.6 30.6 %all-gather.37.cloned.1.call-done = bf16[1,768,768]{2,1,0:T(8,128)(2,1)} async-done(((bf16[1,48,768]{2,1,0:T(8,128)(2,1)}), bf16[1,768,768]{2,1,0:T(8,128)(2,1)}) %all-gather.37.cloned.1.call-update) | async-done | bytes 1179664 | tf_op jit(solution)/shard_map/all_gather | solution.py:364
  445.8 118.8 %all-gather.39.cloned.1.call-done = bf16[1,4,768,4096]{3,2,1,0:T(8,128)(2,1)} async-done(((bf16[1,4,48,4096]{3,2,1,0:T(8,128)(2,1)}), bf16[1,4,768,4096]{3,2,1,0:T(8,128)(2,1)}) %all-gather.39.cloned.1.call-update) | async-done | bytes 25165840 | tf_op jit(solution)/shard_map/all_gather | solution.py:369
  564.7 15.1 fusion.2
  579.7 87.3 %all-gather.41.cloned.1.call-done = bf16[1,4,2048,768]{3,2,1,0:T(8,128)(2,1)} async-done(((bf16[1,4,128,768]{3,2,1,0:T(8,128)(2,1)}), bf16[1,4,2048,768]{3,2,1,0:T(8,128)(2,1)}) %all-gather.41.cloned.1.call-update) | async-done | bytes 12582928 | tf_op jit(solution)/shard_map/all_gather | solution.py:370
  667.0 14.4 multiply_convert_fusion.5
  681.4 14.0 fusion
  756.4 12.2 multiply_convert_fusion.3
  768.5 14.3 fusion.4
  852.3 20.0 fusion.29
  874.1 20.2 fusion.28
  905.9 70.2 %reduce-scatter.29.cloned.1.call-done = f32[48,2304]{1,0:T(8,128)} async-done(((f32[768,2304]{1,0:T(8,128)}), f32[48,2304]{1,0:T(8,128)}) %reduce-scatter.29.cloned.1.call-update) | async-done | bytes 442384 | tf_op jit(solution)/shard_map/reduce_scatter | solution.py:415
  977.8 92.3 %reduce-scatter.27.cloned.1.call-done = f32[48,2304]{1,0:T(8,128)} async-done(((f32[768,2304]{1,0:T(8,128)}), f32[48,2304]{1,0:T(8,128)}) %reduce-scatter.27.cloned.1.call-update) | async-done | bytes 442384 | tf_op jit(solution)/shard_map/reduce_scatter | solution.py:415
  1071.8 243.8 %reduce-scatter.41.cloned.1.call-done = f32[4,128,768]{2,1,0:T(8,128)} async-done(((f32[4,2048,768]{2,1,0:T(8,128)}), f32[4,128,768]{2,1,0:T(8,128)}) %reduce-scatter.41.cloned.1.call-update) | async-done | bytes 1572880 | tf_op jit(solution)/shard_map/reduce_scatter | solution.py:422
  1318.0 244.6 %reduce-scatter.39.cloned.1.call-done = f32[4,128,768]{2,1,0:T(8,128)} async-done(((f32[4,2048,768]{2,1,0:T(8,128)}), f32[4,128,768]{2,1,0:T(8,128)}) %reduce-scatter.39.cloned.1.call-update) | async-done | bytes 1572880 | tf_op jit(solution)/shard_map/reduce_scatter | solution.py:422
  1564.9 468.6 %reduce-scatter.37.cloned.1.call-done = f32[4,48,4096]{2,1,0:T(8,128)} async-done(((f32[4,768,4096]{2,1,0:T(8,128)}), f32[4,48,4096]{2,1,0:T(8,128)}) %reduce-scatter.37.cloned.1.call-update) | async-done | bytes 3145744 | tf_op jit(solution)/shard_map/reduce_scatter | solution.py:421
  2036.7 467.8 %reduce-scatter.35.cloned.1.call-done = f32[4,48,4096]{2,1,0:T(8,128)} async-done(((f32[4,768,4096]{2,1,0:T(8,128)}), f32[4,48,4096]{2,1,0:T(8,128)}) %reduce-scatter.35.cloned.1.call-update) | async-done | bytes 3145744 | tf_op jit(solution)/shard_map/reduce_scatter | solution.py:421
  2512.4 53.6 %all-reduce.16 = (bf16[768]{0:T(1024)(128)(2,1)S(1)}, bf16[768]{0:T(1024)(128)(2,1)S(1)}, bf16[768]{0:T(1024)(128)(2,1)S(1)}, bf16[768]{0:T(1024)(128)(2,1)S(1)}) all-reduce(f32[768]{0:T(1024)S(1)} %copy-done.174, f32[768]{0:T(1024)S(1)} %get-tuple-element.108, ...), channel_id=21, replica_groups=mesh['rep'=2,'shard'=16] {'shard'}, use_global_device_ids=true, to_apply=%region_64.65.clone | all-reduce | flops 3072 | bytes 18432
  2568.2 54.5 %reduce-scatter.51.cloned.1.call-done = f32[48,2]{1,0:T(8,128)} async-done(((f32[768,2]{1,0:T(8,128)}), f32[48,2]{1,0:T(8,128)}) %reduce-scatter.51.cloned.1.call-update) | async-done | bytes 400
  2623.5 57.3 %reduce-scatter.49.cloned.1.call-done = f32[48,4]{1,0:T(8,128)} async-done(((f32[768,4]{1,0:T(8,128)}), f32[48,4]{1,0:T(8,128)}) %reduce-scatter.49.cloned.1.call-update) | async-done | bytes 784
  2681.6 57.5 %reduce-scatter.47.cloned.1.call-done = f32[48,4]{1,0:T(8,128)} async-done(((f32[768,4]{1,0:T(8,128)}), f32[48,4]{1,0:T(8,128)}) %reduce-scatter.47.cloned.1.call-update) | async-done | bytes 784
  2739.9 57.3 %reduce-scatter.45.cloned.1.call-done = f32[48,8]{1,0:T(8,128)} async-done(((f32[768,8]{1,0:T(8,128)}), f32[48,8]{1,0:T(8,128)}) %reduce-scatter.45.cloned.1.call-update) | async-done | bytes 1552
  2798.0 57.7 %reduce-scatter.43.cloned.1.call-done = f32[48,8]{1,0:T(8,128)} async-done(((f32[768,8]{1,0:T(8,128)}), f32[48,8]{1,0:T(8,128)}) %reduce-scatter.43.cloned.1.call-update) | async-done | bytes 1552
  2864.5 129.0 %all-reduce.22.cloned.1.call-done = (bf16[1,48,2304]{2,1,0:T(8,128)(2,1)}, bf16[1,48,2304]{2,1,0:T(8,128)(2,1)}, bf16[1,48,768]{2,1,0:T(8,128)(2,1)}, bf16[1,48,...) async-done(((bf16[1,48,2304]{2,1,0:T(8,128)(2,1)}, ...) | async-done | bytes 5308432 | tf_op jit(solution)/shard_map/psum | solution.py:426
  (725 shorter events, 314.3 us)
Async XLA Ops:
  7.2 218.8 %all-gather.27.cloned.1.call-start = ((), (), s32[]{:S(2)}) async-start(), calls=%async_computation.22 | async-start | bytes 3760128 | tf_op jit(solution)/shard_map/all_gather | solution.py:363
  9.1 224.2 %all-gather.29.cloned.1.call-start = ((), (), s32[]{:S(2)}) async-start(), calls=%async_computation.23 | async-start | bytes 1253376 | tf_op jit(solution)/shard_map/all_gather | solution.py:364
  10.8 232.8 %all-gather.31.cloned.1.call-start = ((), (), s32[]{:S(2)}) async-start(), calls=%async_computation.24 | async-start | bytes 26738688 | tf_op jit(solution)/shard_map/all_gather | solution.py:369
  14.7 331.3 %all-gather.33.cloned.1.call-start = ((), (), s32[]{:S(2)}) async-start(), calls=%async_computation.25 | async-start | bytes 13369344 | tf_op jit(solution)/shard_map/all_gather | solution.py:370
  17.4 378.6 %all-gather.35.cloned.1.call-start = ((), (), s32[]{:S(2)}) async-start(), calls=%async_computation.26 | async-start | bytes 3760128 | tf_op jit(solution)/shard_map/all_gather | solution.py:363
  18.0 416.2 %all-gather.37.cloned.1.call-start = ((), (), s32[]{:S(2)}) async-start(), calls=%async_computation.27 | async-start | bytes 1253376 | tf_op jit(solution)/shard_map/all_gather | solution.py:364
  18.6 546.1 %all-gather.39.cloned.1.call-start = ((), (), s32[]{:S(2)}) async-start(), calls=%async_computation.28 | async-start | bytes 26738688 | tf_op jit(solution)/shard_map/all_gather | solution.py:369
  19.3 647.7 %all-gather.41.cloned.1.call-start = ((), (), s32[]{:S(2)}) async-start(), calls=%async_computation.29 | async-start | bytes 13369344 | tf_op jit(solution)/shard_map/all_gather | solution.py:370
  20.1 882.7 %reduce-scatter.33.cloned.1.call-start = ((), (), s32[]{:S(2)}) async-start(), calls=%async_computation.17 | async-start | bytes 2506752 | tf_op jit(solution)/shard_map/reduce_scatter | solution.py:416
  48.7 177.4 %copy-start.88 = (f32[768]{0:T(1024)}, f32[768]{0:T(1024)S(1)}, u32[]{:S(2)}) copy-start(f32[768]{0:T(1024)S(1)} %convert_element_type.468) | copy-start | bytes 9220
  73.1 169.5 %copy-start.118 = (f32[2,768]{1,0:T(2,128)}, f32[2,768]{1,0:T(2,128)S(1)}, u32[]{:S(2)}) copy-start(f32[2,768]{1,0:T(2,128)S(1)} %copy.230) | copy-start | bytes 18436
  73.1 162.8 %copy-start.109 = (f32[768]{0:T(1024)}, f32[768]{0:T(1024)S(1)}, u32[]{:S(2)}) copy-start(f32[768]{0:T(1024)S(1)} %convert_element_type.469) | copy-start | bytes 9220
  94.6 142.7 %copy-start.136 = (s32[256,2]{0,1:T(2,128)}, s32[256,2]{0,1:T(2,128)S(1)}, u32[]{:S(2)}) copy-start(s32[256,2]{0,1:T(2,128)S(1)} %get-tuple-element.198) | copy-start | bytes 6148
  122.9 313.1 %copy-start.111 = (f32[768]{0:T(1024)}, f32[768]{0:T(1024)S(1)}, u32[]{:S(2)}) copy-start(f32[768]{0:T(1024)S(1)} %convert_element_type.471) | copy-start | bytes 9220
  225.8 173.9 %copy-start.64 = (f32[256,32]{0,1:T(8,128)}, f32[256,32]{0,1:T(8,128)S(1)}, u32[]{:S(2)}) copy-start(f32[256,32]{0,1:T(8,128)S(1)} %get-tuple-element.213) | copy-start | bytes 98308
  225.9 173.9 %copy-start.67 = (f32[256,32]{0,1:T(8,128)}, f32[256,32]{0,1:T(8,128)S(1)}, u32[]{:S(2)}) copy-start(f32[256,32]{0,1:T(8,128)S(1)} %get-tuple-element.214) | copy-start | bytes 98308
  437.2 267.2 %copy-start.15 = (bf16[256,768]{1,0:T(8,128)(2,1)}, bf16[256,768]{1,0:T(8,128)(2,1)S(1)}, u32[]{:S(2)}) copy-start(bf16[256,768]{1,0:T(8,128)(2,1)S(1)} %get-tuple-element.144) | copy-start | bytes 1179652
  443.8 223.2 %copy-start.53 = (bf16[320,768]{1,0:T(8,128)(2,1)}, bf16[320,768]{1,0:T(8,128)(2,1)S(1)}, u32[]{:S(2)}) copy-start(bf16[320,768]{1,0:T(8,128)(2,1)S(1)} %gather_fusion.8) | copy-start | bytes 1474564
  753.5 150.8 %reduce-scatter.31.cloned.1.call-start = ((), (), s32[]{:S(2)}) async-start(), calls=%async_computation.16 | async-start | bytes 2506752 | tf_op jit(solution)/shard_map/reduce_scatter | solution.py:416
  805.5 170.6 %reduce-scatter.29.cloned.1.call-start = ((), (), s32[]{:S(2)}) async-start(), calls=%async_computation.15 | async-start | bytes 7520256 | tf_op jit(solution)/shard_map/reduce_scatter | solution.py:415
  809.7 260.4 %reduce-scatter.27.cloned.1.call-start = ((), (), s32[]{:S(2)}) async-start(), calls=%async_computation.14 | async-start | bytes 7520256 | tf_op jit(solution)/shard_map/reduce_scatter | solution.py:415
  826.5 489.1 %reduce-scatter.41.cloned.1.call-start = ((), (), s32[]{:S(2)}) async-start(), calls=%async_computation.21 | async-start | bytes 26738688 | tf_op jit(solution)/shard_map/reduce_scatter | solution.py:422
  838.6 724.0 %reduce-scatter.39.cloned.1.call-start = ((), (), s32[]{:S(2)}) async-start(), calls=%async_computation.20 | async-start | bytes 26738688 | tf_op jit(solution)/shard_map/reduce_scatter | solution.py:422
  850.4 1183.1 %reduce-scatter.37.cloned.1.call-start = ((), (), s32[]{:S(2)}) async-start(), calls=%async_computation.19 | async-start | bytes 53477376 | tf_op jit(solution)/shard_map/reduce_scatter | solution.py:421
  872.3 1632.2 %reduce-scatter.35.cloned.1.call-start = ((), (), s32[]{:S(2)}) async-start(), calls=%async_computation.18 | async-start | bytes 53477376 | tf_op jit(solution)/shard_map/reduce_scatter | solution.py:421
  894.4 1673.0 %reduce-scatter.53.cloned.1.call-start = ((), (), s32[]{:S(2)}) async-start(), calls=%async_computation.35 | async-start | bytes 417792
  896.0 1726.7 %reduce-scatter.51.cloned.1.call-start = ((), (), s32[]{:S(2)}) async-start(), calls=%async_computation.34 | async-start | bytes 417792
  897.0 1783.8 %reduce-scatter.49.cloned.1.call-start = ((), (), s32[]{:S(2)}) async-start(), calls=%async_computation.33 | async-start | bytes 417792
  898.4 1840.7 %reduce-scatter.47.cloned.1.call-start = ((), (), s32[]{:S(2)}) async-start(), calls=%async_computation.32 | async-start | bytes 417792
  899.8 1897.4 %reduce-scatter.45.cloned.1.call-start = ((), (), s32[]{:S(2)}) async-start(), calls=%async_computation.31 | async-start | bytes 417792
  901.3 1954.5 %reduce-scatter.43.cloned.1.call-start = ((), (), s32[]{:S(2)}) async-start(), calls=%async_computation.30 | async-start | bytes 417792
  902.7 2090.8 %all-reduce.22.cloned.1.call-start = ((), (), s32[]{:S(2)}) async-start(), calls=%async_computation.36 | async-start | bytes 10616832 | tf_op jit(solution)/shard_map/psum | solution.py:426
  (171 other events, 2168.3 us)
Sparse Core Ops, SparseCore 0:
  10.9 50.0 all-gather.26
  63.2 36.0 all-gather.28
  101.4 134.4 all-gather.30
  238.6 107.3 all-gather.32
  348.7 47.2 all-gather.34
  398.2 35.9 all-gather.36
  436.3 128.3 all-gather.38
  567.5 99.4 all-gather.40
  753.6 62.3 reduce-scatter.32
  820.7 62.0 reduce-scatter.30
  886.7 89.3 reduce-scatter.28
  980.5 89.5 reduce-scatter.26
  1074.2 241.3 reduce-scatter.40
  1319.5 242.9 reduce-scatter.38
  1566.6 466.8 reduce-scatter.36
  2037.6 466.8 reduce-scatter.34
  2507.8 56.3 reduce-scatter.52
  2568.0 54.6 reduce-scatter.50
  2626.2 54.5 reduce-scatter.48
  2684.5 54.5 reduce-scatter.46
  2742.6 54.5 reduce-scatter.44
  2801.1 54.5 reduce-scatter.42
  2859.9 133.5 all-reduce.21
where the time goes:
time: 3020 us; the launch traced here: 3010 us
  waiting for transfers between devices  2360 us (78%)
  blocking collectives  214 us (7%)
  matrix products  214 us (7%)
  local copies, waits for them, and re-layouts  128 us (4%)
  other arithmetic  73.4 us (2%)
    reduce_scatter x2, waiting for transfers between devices, local(): lax.psum_scatter(term_gate_up, 'shard', scatter_dimension=1, tiled=True)  936 us
    reduce_scatter x2, waiting for transfers between devices, local(): lax.psum_scatter(term_down, 'shard', scatter_dimension=1, tiled=True)  488 us
    unnamed x29, waiting for transfers between devices  287 us
    all_gather x2, waiting for transfers between devices, local(): lax.all_gather(w_down[layer_index], 'shard', axis=1, tiled=True)  174 us
    reduce_scatter x2, waiting for transfers between devices, local(): lax.psum_scatter(term_qkv, 'shard', scatter_dimension=0, tiled=True)  162 us
    psum x1, waiting for transfers between devices, local(): lax.psum(pieces[1].astype(jnp.bfloat16), 'rep').astype(jnp.float32)  129 us
    all_gather x2, waiting for transfers between devices, local(): lax.all_gather(w_gate_up[layer_index], 'shard', axis=1, tiled=True)  119 us
    unnamed x2, blocking collectives  79.9 us
  transfers between devices with their start and end apart: 23, of which 17 were waited for; matrix products, arithmetic and copies ran while one was open for 10% of the time, Pallas kernels for 0%

commit v1 on v0

v1 whole, which is shorter than its diff:
```python
import functools
import math

import jax
import jax.numpy as jnp
from jax import lax
from jax.sharding import PartitionSpec as P

HEAD_DIM = 64
EF = 4
NCONST = 2
TOP = 2
EXPERTS = 8
CAP = 80
SMALL = 2 + EXPERTS + 2 * NCONST + NCONST
LANES = 128

EPSILON = 1e-06
SCALE = 0.125
MASKED = -1000000000.0
EXACT = lax.Precision.HIGHEST
AXES = ("rep", "shard")
BF16 = jnp.bfloat16
F32 = jnp.float32


def dot(a, b, dims=((1,), (0,))):
    return lax.dot_general(a, b, (dims, ((), ())), preferred_element_type=F32)


def rope_tables(tokens, head_size):
    half = head_size // 2
    places = jnp.arange(tokens, dtype=jnp.int32).astype(F32)[:, None]
    powers = jnp.arange(half, dtype=jnp.int32).astype(F32) / half
    angles = places * jnp.exp(-math.log(10000.0) * powers)[None, :]
    return (jnp.cos(angles)[:, None, :], jnp.sin(angles)[:, None, :])


def rotate(source, cosine, sine):
    half = source.shape[-1] // 2
    first, second = (source[..., :half], source[..., half:])
    return jnp.concatenate(
        [first * cosine - second * sine, second * cosine + first * sine], axis=-1
    )


def rotate_back(grad_rows, cosine, sine):
    return rotate(grad_rows, cosine, -sine)


def softmax_rows(scores):
    shifted = jnp.exp(scores - jnp.max(scores, axis=-1, keepdims=True))
    return shifted / jnp.sum(shifted, axis=-1, keepdims=True)


def norm_back(grad_rows, source, inverse, gain):
    scaled = grad_rows * gain
    gain_grad = jnp.sum(grad_rows * source * inverse, axis=0)
    source_grad = inverse * scaled - source * inverse**3 * jnp.mean(
        scaled * source, axis=-1, keepdims=True
    )
    return (source_grad, gain_grad)


class Layout:
    def __init__(self, mesh):
        self.reps, self.shards = mesh.shape["rep"], mesh.shape["shard"]
        self.lines = self.shards // EF
        assert self.shards % EF == 0 and EF % self.reps == 0

    def pairs(self, move):
        found = []
        for rep in range(self.reps):
            for shard in range(self.shards):
                r, z, j = move(rep, shard // EF, shard % EF)
                found.append((rep * self.shards + shard, r * self.shards + z * EF + j))
        return found

    def send(self, x, move):
        return lax.ppermute(x, AXES, self.pairs(move))

    def expert_move(self, mask, shift):
        def move(r, z, j):
            number = r * EF + j
            e, f = (number // self.reps) ^ mask, (number % self.reps + shift) % self.reps
            number = e * self.reps + f
            return number // EF, z, number % EF

        return move

    def place(self):
        rep, shard = lax.axis_index("rep"), lax.axis_index("shard")
        j = shard % EF
        return rep, j, (rep * EF + j) // self.reps

    def quad_exchange(self, blocks, j):
        got = lax.dynamic_update_slice_in_dim(
            jnp.zeros_like(blocks), lax.dynamic_slice_in_dim(blocks, j, 1, 0), j, 0
        )
        for mask in range(1, EF):
            other = j ^ mask
            block = lax.dynamic_slice_in_dim(blocks, other, 1, 0)
            block = self.send(block, lambda r, z, q: (r, z, q ^ mask))
            got = lax.dynamic_update_slice_in_dim(got, block, other, 0)
        return got

    def part_exchange(self, blocks, j):
        count = EF // self.reps
        mine = j // self.reps
        got = lax.dynamic_update_slice_in_dim(
            jnp.zeros_like(blocks), lax.dynamic_slice_in_dim(blocks, mine, 1, 0), mine, 0
        )
        for mask in range(1, count):
            other = mine ^ mask
            block = lax.dynamic_slice_in_dim(blocks, other, 1, 0)
            block = self.send(block, lambda r, z, q: (r, z, q ^ (mask * self.reps)))
            got = lax.dynamic_update_slice_in_dim(got, block, other, 0)
        return got

    def rep_gather(self, x, rep):
        got = lax.dynamic_update_slice_in_dim(
            jnp.zeros((self.reps,) + x.shape, x.dtype), x[None], rep, 0
        )
        for shift in range(1, self.reps):
            block = self.send(x, lambda r, z, q: ((r + shift) % self.reps, z, q))
            got = lax.dynamic_update_slice_in_dim(
                got, block[None], (rep + self.reps - shift) % self.reps, 0
            )
        return got

    def line_groups(self):
        return [[z * EF + j for z in range(self.lines)] for j in range(EF)]

    def line_gather(self, x):
        return lax.all_gather(
            x, "shard", axis=0, tiled=True, axis_index_groups=self.line_groups()
        )

    def line_sum(self, x):
        return lax.psum_scatter(
            x, "shard", scatter_dimension=0, tiled=True, axis_index_groups=self.line_groups()
        )

    def dispatch(self, rows):
        blocks = rows.reshape(EF, CAP, -1)
        own = jnp.stack(
            [blocks[0]] + [self.send(blocks[m], self.expert_move(m, 0)) for m in range(1, EF)]
        )
        parts = [own] + [self.send(own, self.expert_move(0, g)) for g in range(1, self.reps)]
        return jnp.concatenate(parts).reshape(self.reps * EF * CAP, -1)

    def collect(self, rows):
        blocks = rows.reshape(self.reps, EF * CAP, -1)
        total = blocks[0]
        for g in range(1, self.reps):
            total = total + self.send(
                blocks[g].astype(BF16), self.expert_move(0, self.reps - g)
            ).astype(F32)
        total = total.astype(BF16).reshape(EF, CAP, -1)
        return jnp.concatenate(
            [total[0]] + [self.send(total[m], self.expert_move(m, 0)) for m in range(1, EF)]
        )


def split_columns(array, layout):
    width = array.shape[-1] // (2 * layout.shards)
    return array.reshape(array.shape[:-1] + (2, layout.shards // layout.reps, layout.reps, width))


def expert_weights(layout, w_gate_up, w_down, rep, j):
    features = w_gate_up.shape[1]
    blocks = split_columns(w_gate_up, layout)
    blocks = jnp.transpose(blocks, (0, 4, 1, 2, 3, 5)).reshape(EF * layout.reps, features, -1)
    mine = lax.dynamic_slice_in_dim(blocks, rep * EF, EF, 0)
    mine = layout.quad_exchange(mine, j).reshape(EF * features, -1)
    gate_up = layout.line_gather(mine)
    count = EF // layout.reps
    down = lax.dynamic_slice_in_dim(w_down, rep * count, count, 0)
    down = layout.part_exchange(down, j).reshape(count * w_down.shape[1], -1)
    return gate_up, layout.line_gather(down)


def expert_grads(layout, grad_gate_up, grad_down, rep, j):
    down = layout.line_sum(grad_down)
    count = EF // layout.reps
    down = layout.part_exchange(down.reshape(count, -1, down.shape[-1]), j)
    down = layout.rep_gather(down, rep).reshape((EF,) + down.shape[1:]).astype(F32)
    mine = layout.line_sum(grad_gate_up)
    mine = layout.quad_exchange(mine.reshape(EF, -1, mine.shape[-1]), j)
    full = layout.rep_gather(mine, rep)
    features = mine.shape[1]
    full = full.reshape(EF, layout.reps, features, 2, layout.shards // layout.reps, -1)
    full = jnp.transpose(full, (0, 2, 3, 4, 1, 5)).reshape(EF, features, -1)
    return full.astype(F32), down


def place_pairs(routes, priority, expert):
    flat = routes.reshape(-1)
    ahead = (flat[:, None] == flat[None, :]) & (priority[:, None] < priority[None, :])
    position = jnp.sum(ahead.astype(jnp.int32), axis=0)
    kept = (flat < EF) & (position < CAP)
    slot = jnp.where(kept, (flat ^ expert) * CAP + position, EF * CAP).reshape(-1, TOP)
    places = jnp.arange(EF * CAP, dtype=jnp.int32)[:, None]
    return [(places == slot[:, k][None, :]).astype(BF16) for k in range(TOP)]


def attention_forward(weights, hidden, allowed, cosine, sine):
    gain, w_qkv, w_out = weights
    tokens, features = hidden.shape
    heads = features // HEAD_DIM
    inverse = lax.rsqrt(jnp.mean(hidden * hidden, axis=-1, keepdims=True) + EPSILON)
    normed = (hidden * inverse * gain).astype(BF16)
    projected = dot(normed, w_qkv).reshape(tokens, 3, heads, HEAD_DIM)
    query = rotate(projected[:, 0], cosine, sine).astype(BF16)
    keys = rotate(projected[:, 1], cosine, sine).astype(BF16)
    values = projected[:, 2].astype(BF16)
    scores = jnp.einsum("qhd,khd->hqk", query, keys, preferred_element_type=F32) * SCALE
    scores = jnp.where(allowed[None], scores, MASKED)
    row_max = jnp.max(scores, axis=-1, keepdims=True)
    weight = jnp.exp(scores - row_max)
    total = jnp.sum(weight, axis=-1, keepdims=True)
    probs = (weight / total).astype(BF16)
    outputs = jnp.einsum("hqk,khd->qhd", probs, values, preferred_element_type=F32)
    attended = outputs.reshape(tokens, features).astype(BF16)
    middle = hidden + dot(attended, w_out)
    log_total = row_max + jnp.log(total)
    return middle, (hidden, inverse, normed, query, keys, values, log_total, attended)


def attention_backward(weights, kept, d_middle, allowed, cosine, sine):
    gain, w_qkv, w_out = weights
    hidden, inverse, normed, query, keys, values, log_total, attended = kept
    tokens, features = hidden.shape
    heads = features // HEAD_DIM
    d_branch = d_middle.astype(BF16)
    grad_out = dot(attended, d_branch, ((0,), (0,)))
    d_attended = dot(d_branch, w_out, ((1,), (1,))).astype(BF16)
    d_attended = d_attended.reshape(tokens, heads, HEAD_DIM)
    scores = jnp.einsum("qhd,khd->hqk", query, keys, preferred_element_type=F32) * SCALE
    scores = jnp.where(allowed[None], scores, MASKED)
    probs = jnp.exp(scores - log_total)
    d_values = jnp.einsum(
        "hqk,qhd->khd", probs.astype(BF16), d_attended, preferred_element_type=F32
    )
    d_probs = jnp.einsum("qhd,khd->hqk", d_attended, values, preferred_element_type=F32)
    d_scores = (probs * (d_probs - jnp.sum(d_probs * probs, axis=-1, keepdims=True))).astype(BF16)
    d_query = jnp.einsum("hqk,khd->qhd", d_scores, keys, preferred_element_type=F32) * SCALE
    d_keys = jnp.einsum("hqk,qhd->khd", d_scores, query, preferred_element_type=F32) * SCALE
    d_projected = (
        jnp.stack(
            [rotate_back(d_query, cosine, sine), rotate_back(d_keys, cosine, sine), d_values],
            axis=1,
        )
        .reshape(tokens, 3 * features)
        .astype(BF16)
    )
    grad_qkv = dot(normed, d_projected, ((0,), (0,)))
    d_normed = dot(d_projected, w_qkv, ((1,), (1,)))
    d_hidden, grad_gain = norm_back(d_normed, hidden, inverse, gain)
    return d_hidden + d_middle, grad_gain, grad_qkv, grad_out


def moe_forward(layout, small, w_gate_up, w_down, middle, previous, routes, onehots):
    gain, w_router, w_const, const_vec = small
    tokens, features = middle.shape
    inverse = lax.rsqrt(jnp.mean(middle * middle, axis=-1, keepdims=True) + EPSILON)
    mixed = middle * inverse * gain
    mixed_low = mixed.astype(BF16)
    rows = dot(onehots[0] + onehots[1], mixed_low).astype(BF16)
    inputs = layout.dispatch(rows)
    logits = dot(mixed_low, w_router) + previous
    ids = jnp.arange(EXPERTS, dtype=jnp.int32)
    hot = (routes[:, :, None] == ids[None, None, :]).astype(F32)
    gates = softmax_rows(jnp.sum(hot * logits[:, None, :], axis=-1))
    shares = softmax_rows(dot(mixed_low, w_const).reshape(tokens, NCONST, 2))
    const_flag = hot[:, :, EF + 2 :]
    copy_flag = hot[:, :, EF + 1]
    mixed_part = copy_flag + jnp.sum(const_flag * shares[:, None, :, 0], axis=-1)
    vector_part = const_flag * shares[:, None, :, 1]
    gate_up = dot(inputs, w_gate_up)
    hidden_units = gate_up.shape[-1] // 2
    gate_part = gate_up[:, :hidden_units]
    activated = (gate_part * jax.nn.sigmoid(gate_part) * gate_up[:, hidden_units:]).astype(BF16)
    outputs = layout.collect(dot(activated, w_down))
    values = [
        dot(onehots[k], outputs, ((0,), (0,)))
        + mixed_part[:, k : k + 1] * mixed
        + sum(vector_part[:, k, c : c + 1] * const_vec[c][None] for c in range(NCONST))
        for k in range(TOP)
    ]
    result = middle + sum(gates[:, k : k + 1] * values[k] for k in range(TOP))
    kept = (middle, inverse, mixed, mixed_low, hot, gates, shares, values, inputs, gate_up, activated)
    return result, logits, kept


def moe_backward(layout, small, w_gate_up, w_down, kept, onehots, d_result, d_next):
    gain, w_router, w_const, const_vec = small
    middle, inverse, mixed, mixed_low, hot, gates, shares, values, inputs, gate_up, activated = kept
    tokens, features = middle.shape
    rows = sum(
        dot(onehots[k], (gates[:, k : k + 1] * d_result).astype(BF16)) for k in range(TOP)
    ).astype(BF16)
    d_expert = layout.dispatch(rows)
    d_gates = jnp.stack([jnp.sum(v * d_result, axis=-1) for v in values], axis=-1)
    d_chosen = gates * (d_gates - jnp.sum(gates * d_gates, axis=-1, keepdims=True))
    d_logits = jnp.sum(hot * d_chosen[..., None], axis=1) + d_next
    const_weight = jnp.sum(hot[:, :, EF + 2 :] * gates[..., None], axis=1)
    d_shares = jnp.stack(
        [
            const_weight * jnp.sum(d_result * mixed, axis=-1, keepdims=True),
            const_weight
            * jnp.stack(
                [jnp.sum(d_result * const_vec[c][None], axis=-1) for c in range(NCONST)], axis=-1
            ),
        ],
        axis=-1,
    )
    d_mix = (shares * (d_shares - jnp.sum(shares * d_shares, axis=-1, keepdims=True))).reshape(
        tokens, 2 * NCONST
    )
    terms = jnp.concatenate([d_logits, d_mix], axis=-1)
    grad_terms = lax.dot_general(
        mixed_low.astype(F32), terms, (((0,), (0,)), ((), ())), precision=EXACT
    )
    grad_vec = lax.dot_general(
        d_result, shares[..., 1] * const_weight, (((0,), (0,)), ((), ())), precision=EXACT
    )
    direct = jnp.sum(hot[:, :, EF + 1] * gates, axis=-1, keepdims=True) + jnp.sum(
        shares[..., 0] * const_weight, axis=-1, keepdims=True
    )
    both = jnp.concatenate([w_router, w_const], axis=-1).astype(F32)
    d_mixed = direct * d_result + lax.dot_general(
        terms, both, (((1,), (1,)), ((), ())), precision=EXACT
    )
    hidden_units = gate_up.shape[-1] // 2
    gate_part, up_part = gate_up[:, :hidden_units], gate_up[:, hidden_units:]
    d_activated = dot(d_expert, w_down, ((1,), (1,)))
    grad_down = dot(activated, d_expert, ((0,), (0,))).astype(BF16)
    sigmoid = jax.nn.sigmoid(gate_part)
    d_gate_up = jnp.concatenate(
        [
            d_activated * up_part * sigmoid * (1.0 + gate_part * (1.0 - sigmoid)),
            d_activated * gate_part * sigmoid,
        ],
        axis=-1,
    ).astype(BF16)
    d_rows = layout.collect(dot(d_gate_up, w_gate_up, ((1,), (1,))))
    grad_gate_up = dot(inputs, d_gate_up, ((0,), (0,))).astype(BF16)
    d_mixed = d_mixed + dot(onehots[0] + onehots[1], d_rows, ((0,), (0,)))
    d_middle, grad_gain = norm_back(d_mixed, middle, inverse, gain)
    small_grads = (grad_gain, grad_terms, grad_vec)
    return d_middle + d_result, d_logits, small_grads, grad_gate_up, grad_down


def local(
    layout,
    hidden_in,
    gate_in,
    routes,
    priority,
    segments,
    norm_attn,
    w_qkv,
    w_out,
    norm_moe,
    w_router,
    w_const,
    const_vec,
    w_gate_up,
    w_down,
    grad_out,
):
    layers = w_qkv.shape[0]
    tokens, features = hidden_in.shape
    rep, j, expert = layout.place()
    slim = w_qkv.shape[1]
    small = jnp.concatenate(
        [
            piece
            for l in range(layers)
            for piece in (
                norm_attn[l][:, None],
                norm_moe[l][:, None],
                w_router[l],
                w_const[l],
                const_vec[l].T,
            )
        ]
        + [jnp.zeros((slim, LANES - layers * SMALL), BF16)],
        axis=-1,
    )
    dense = []
    moe = []
    for l in range(layers):
        packed = [w_qkv[l], w_out[l]] + ([small] if l == 0 else [])
        dense.append(lax.all_gather(jnp.concatenate(packed, axis=-1), "shard", axis=0, tiled=True))
        moe.append(expert_weights(layout, w_gate_up[l], w_down[l], rep, j))
    wide = 3 * features
    small_full = dense[0][:, wide + features :].astype(F32)
    attn_weights, small_weights = [], []
    for l in range(layers):
        part = small_full[:, l * SMALL : (l + 1) * SMALL]
        router = part[:, 2 : 2 + EXPERTS].astype(BF16)
        const = part[:, 2 + EXPERTS : 2 + EXPERTS + 2 * NCONST].astype(BF16)
        attn_weights.append((part[:, 0][None], dense[l][:, :wide], dense[l][:, wide : wide + features]))
        small_weights.append((part[:, 1][None], router, const, part[:, SMALL - NCONST :].T))

    segment = segments[0]
    places = jnp.arange(tokens, dtype=jnp.int32)
    allowed = (segment[:, None] == segment[None, :]) & (places[None, :] <= places[:, None])
    cosine, sine = rope_tables(tokens, HEAD_DIM)
    onehots = [place_pairs(routes[l], priority[l, 0], expert) for l in range(layers)]

    hidden = hidden_in.astype(F32)
    previous = gate_in
    attn_kept, moe_kept = [], []
    for l in range(layers):
        middle, kept = attention_forward(attn_weights[l], hidden, allowed, cosine, sine)
        attn_kept.append(kept)
        hidden, previous, kept = moe_forward(
            layout, small_weights[l], *moe[l], middle, previous, routes[l], onehots[l]
        )
        moe_kept.append(kept)

    grad_hidden = grad_out
    grad_gate = jnp.zeros_like(gate_in)
    dense_grads, moe_grads = [None] * layers, [None] * layers
    for l in reversed(range(layers)):
        d_middle, grad_gate, small_grads, grad_gate_up, grad_down = moe_backward(
            layout, small_weights[l], *moe[l], moe_kept[l], onehots[l], grad_hidden, grad_gate
        )
        moe_grads[l] = expert_grads(layout, grad_gate_up, grad_down, rep, j)
        grad_hidden, grad_gain, grad_qkv, grad_proj = attention_backward(
            attn_weights[l], attn_kept[l], d_middle, allowed, cosine, sine
        )
        packed = jnp.concatenate(
            [
                grad_qkv,
                grad_proj,
                grad_gain[:, None],
                small_grads[0][:, None],
                small_grads[1],
                small_grads[2],
                jnp.zeros((features, LANES - SMALL), F32),
            ],
            axis=-1,
        ).astype(BF16)
        piece = lax.psum_scatter(packed, "shard", scatter_dimension=0, tiled=True)
        dense_grads[l] = jnp.sum(layout.rep_gather(piece, rep).astype(F32), axis=0)

    dense_all = jnp.stack(dense_grads)
    base = wide + features
    return (
        hidden.astype(BF16),
        grad_hidden,
        grad_gate,
        dense_all[:, :, base],
        dense_all[:, :, :wide],
        dense_all[:, :, wide:base],
        dense_all[:, :, base + 1],
        dense_all[:, :, base + 2 : base + 2 + EXPERTS],
        dense_all[:, :, base + 2 + EXPERTS : base + SMALL - NCONST],
        jnp.transpose(dense_all[:, :, base + SMALL - NCONST : base + SMALL], (0, 2, 1)),
        jnp.stack([g[0] for g in moe_grads]),
        jnp.stack([g[1] for g in moe_grads]),
    )


def solution(mesh):
    return jax.shard_map(
        functools.partial(local, Layout(mesh)),
        mesh=mesh,
        in_specs=(
            P(("rep", "shard"), None),
            P(("rep", "shard"), None),
            P(None, ("rep", "shard"), None),
            P(None, ("rep", "shard"), None),
            P(("rep", "shard"), None),
            P(None, "shard"),
            P(None, "shard", None),
            P(None, "shard", None),
            P(None, "shard"),
            P(None, "shard", None),
            P(None, "shard", None),
            P(None, None, "shard"),
            P(None, None, "shard", None),
            P(None, None, "shard", None),
            P(("rep", "shard"), None),
        ),
        out_specs=(
            P(("rep", "shard"), None),
            P(("rep", "shard"), None),
            P(("rep", "shard"), None),
            P(None, "shard"),
            P(None, "shard", None),
            P(None, "shard", None),
            P(None, "shard"),
            P(None, "shard", None),
            P(None, "shard", None),
            P(None, None, "shard"),
            P(None, None, "shard", None),
            P(None, None, "shard", None),
        ),
        check_vma=False,
    )
```

time: 3020 us -> 766 us (0.25)
  waiting for transfers between devices: 2360 us -> 349 us
  blocking collectives: 214 us -> 0 us
  matrix products: 214 us -> 124 us
  starting transfers between devices: 0.94 us -> 51.9 us
    reduce_scatter x8 -> x6, waiting for transfers between devices: 1590 us -> 111 us  [the longest x2 105 us: local(): piece = lax.psum_scatter(packed, 'shard', scatter_dimension=0, tiled=True)]
    unnamed x29 -> x12, waiting for transfers between devices: 287 us -> 0.2 us
    all_gather x8 -> x6, waiting for transfers between devices: 358 us -> 130 us  [the longest x4 90.2 us: line_gather(): lax.all_gather(x, 'shard', axis=0, tiled=True, axis_index_groups=self.lin...]
    all_gather x6 -> x0, blocking collectives: 129 us -> none  [the longest x2 44.3 us: local(): lax.all_gather(const_vec[layer_index], 'shard', axis=1, tiled=True)]
    psum x1 -> x0, waiting for transfers between devices: 129 us -> none  [local(): lax.psum(pieces[1].astype(jnp.bfloat16), 'rep').astype(jnp.float32)]
    ppermute x0 -> x54, waiting for transfers between devices: none -> 108 us  [send(): return lax.ppermute(x, AXES, self.pairs(move))]
    dot_general x44 -> x58, matrix products: 209 us -> 124 us  [the longest x40 102 us: dot(): return lax.dot_general(a, b, (dims, ((), ())), preferred_element_type=F32)]
    unnamed x2 -> x0, blocking collectives: 79.9 us -> none
  transfers between devices with their start and end apart: 23 -> 66, of which waited for: 17 -> 38; matrix products, arithmetic and copies ran while one was open for 10% -> 39% of each run, Pallas kernels for 0% -> 0%
where the time goes in v1:
time: 766 us; the launch traced here: 755 us
  waiting for transfers between devices  349 us (46%)
  local copies, waits for them, and re-layouts  155 us (20%)
  matrix products  124 us (16%)
  other arithmetic  57.5 us (8%)
  starting transfers between devices  51.9 us (7%)
  between operations  17.6 us (2%)
    ppermute x54, waiting for transfers between devices, send(): return lax.ppermute(x, AXES, self.pairs(move))  108 us
    reduce_scatter x2, waiting for transfers between devices, local(): piece = lax.psum_scatter(packed, 'shard', scatter_dimension=0, tiled=True)  105 us
    dot_general x40, matrix products, dot(): return lax.dot_general(a, b, (dims, ((), ())), preferred_element_type=F32)  102 us
    all_gather x4, waiting for transfers between devices, line_gather(): lax.all_gather(x, 'shard', axis=0, tiled=True, axis_index_groups=self.lin...  90.2 us
    ppermute x54, starting transfers between devices, send(): return lax.ppermute(x, AXES, self.pairs(move))  50.6 us
    unnamed x403, local copies, waits for them, and re-layouts  40.2 us
    all_gather x2, waiting for transfers between devices, local(): lax.all_gather(jnp.concatenate(packed, axis=-1), 'shard', axis=0, tiled=T...  40.2 us
    concatenate x2, local copies, waits for them, and re-layouts, local(): jnp.concatenate([grad_qkv, grad_proj, grad_gain[:, None], small_grads[0][...  16.7 us
  transfers between devices with their start and end apart: 66, of which 38 were waited for; matrix products, arithmetic and copies ran while one was open for 39% of the time, Pallas kernels for 0%

profile of v1, /device:TPU:8, one launch (start us, length us, event | category | flops | bytes accessed | tf_op | source)
XLA Modules:
  0.0 754.8 jit_solution(9919632000045659638)
XLA Ops:
  22.4 7.3 collective-permute-done.5
  29.7 5.2 collective-permute-done.6
  40.0 5.7 collective-permute-done.7
  51.7 10.1 %collective-permute-done.17 = bf16[1,48,2048]{2,1,0:T(8,128)(2,1)S(1)} collective-permute-done((bf16[1,48,2048]{2,1,0:T(8,128)(2,1)S(1)}, bf16[1,48,2048]{2,1,0:T(8,128)(2,1)S(1)}, u32[]{:S(2)}, u32[]{:S(2)}) %collective-permute-start.17) | collective-permute-done | bytes 196640 | tf_op jit(solution)/shard_map/ppermute | solution.py:80
  61.8 7.7 %collective-permute-done.18 = bf16[1,48,2048]{2,1,0:T(8,128)(2,1)S(1)} collective-permute-done((bf16[1,48,2048]{2,1,0:T(8,128)(2,1)S(1)}, bf16[1,48,2048]{2,1,0:T(8,128)(2,1)S(1)}, u32[]{:S(2)}, u32[]{:S(2)}) %collective-permute-start.18) | collective-permute-done | bytes 196640 | tf_op jit(solution)/shard_map/ppermute | solution.py:80
  120.9 22.5 %all-gather.9.cloned.1.call-done = bf16[768,2048]{1,0:T(8,128)(2,1)} async-done(((bf16[192,2048]{1,0:T(8,128)(2,1)}), bf16[768,2048]{1,0:T(8,128)(2,1)}) %all-gather.9.cloned.1.call-update) | async-done | bytes 3145744 | tf_op jit(solution)/shard_map/all_gather | solution.py:135
  143.4 4.4 fusion.203
  152.0 30.1 %all-gather.11.cloned.1.call-done = bf16[1024,768]{1,0:T(8,128)(2,1)} async-done(((bf16[256,768]{1,0:T(8,128)(2,1)}), bf16[1024,768]{1,0:T(8,128)(2,1)}) %all-gather.11.cloned.1.call-update) | async-done | bytes 1572880 | tf_op jit(solution)/shard_map/all_gather | solution.py:135
  201.0 37.8 %all-gather.13.cloned.1.call-done = bf16[768,3072]{1,0:T(8,128)(2,1)} async-done(((bf16[48,3072]{1,0:T(8,128)(2,1)}), bf16[768,3072]{1,0:T(8,128)(2,1)}) %all-gather.13.cloned.1.call-update) | async-done | bytes 4718608 | tf_op jit(solution)/shard_map/all_gather | solution.py:396
  294.7 5.8 all-gather.15.cloned.1.call-done
  300.5 6.8 fusion.205
  307.3 31.8 %all-gather.17.cloned.1.call-done = bf16[1024,768]{1,0:T(8,128)(2,1)} async-done(((bf16[256,768]{1,0:T(8,128)(2,1)}), bf16[1024,768]{1,0:T(8,128)(2,1)}) %all-gather.17.cloned.1.call-update) | async-done | bytes 1572880 | tf_op jit(solution)/shard_map/all_gather | solution.py:135
  339.0 5.5 multiply_convert_fusion.5
  413.7 6.3 convolution_convert_fusion.2
  420.1 5.3 multiply_convert_fusion.3
  426.8 4.1 convolution_convert_fusion.3
  456.4 8.5 %concatenate.141 = bf16[768,3200]{1,0:T(8,128)(2,1)} concatenate(bf16[768,2304]{1,0:T(8,128)(2,1)} %convolution_convert_fusion, bf16[768,768]{1,0:T(8,128)(2,1)} %convolution_convert_fusion.6, bf16[768,1]{1,0:T(8,128)(2,1)} %broadcast_in_dim.158, bf16[768,1]{1,0:T(8,128)(2,1)} %broadcast_in_dim.159, bf16[768,12]{1,0:T(8,128)(2,1)} %copy.358, bf16[768,2]{1,0:T(8,128)(2,1)} %copy.359, ...), dimensions={1} | concatenate | bytes 9830400 | tf_op jit(solution)/shard_map/concatenate | solution.py:436
  471.5 5.0 fusion.14
  517.1 8.1 %concatenate.140 = bf16[768,3200]{1,0:T(8,128)(2,1)} concatenate(bf16[768,2304]{1,0:T(8,128)(2,1)S(1)} %convolution_convert_fusion.1, bf16[768,768]{1,0:T(8,128)(2,1)} %convolution_convert_fusion.7, bf16[768,1]{1,0:T(8,128)(2,1)} %broadcast_in_dim.156, bf16[768,1]{1,0:T(8,128)(2,1)} %broadcast_in_dim.157, bf16[768,12]{1,0:T(8,128)(2,1)} %copy.353, bf16[768,2]{1,0:T(8,128)(2,1)} %copy.354, ...), dimensions={1} | concatenate | bytes 9830400 | tf_op jit(solution)/shard_map/concatenate | solution.py:436
  528.1 5.2 collective-permute-done.52
  538.9 4.6 collective-permute-done.53
  548.1 4.8 collective-permute-done.51
  555.7 4.1 collective-permute-done.47
  567.7 5.2 reduce-scatter.11.cloned.1.call-done
  575.0 8.5 %collective-permute-done.49 = bf16[4,48,2048]{2,1,0:T(8,128)(2,1)} collective-permute-done((bf16[4,48,2048]{2,1,0:T(8,128)(2,1)}, bf16[4,48,2048]{2,1,0:T(8,128)(2,1)}, u32[]{:S(2)}, u32[]{:S(2)}) %collective-permute-start.49) | collective-permute-done | bytes 786464 | tf_op jit(solution)/shard_map/ppermute | solution.py:80
  594.1 5.5 collective-permute-done.43
  605.6 48.8 %reduce-scatter.9.cloned.1.call-done = bf16[48,3200]{1,0:T(8,128)(2,1)} async-done(((bf16[768,3200]{1,0:T(8,128)(2,1)}), bf16[48,3200]{1,0:T(8,128)(2,1)}) %reduce-scatter.9.cloned.1.call-update) | async-done | bytes 307216 | tf_op jit(solution)/shard_map/reduce_scatter | solution.py:448
  656.9 5.3 collective-permute-done.41
  669.9 4.0 convert_element_type.455
  673.9 4.6 maximum_convert_fusion
  678.5 56.6 %reduce-scatter.7.cloned.1.call-done = bf16[48,3200]{1,0:T(8,128)(2,1)} async-done(((bf16[768,3200]{1,0:T(8,128)(2,1)}), bf16[48,3200]{1,0:T(8,128)(2,1)}) %reduce-scatter.7.cloned.1.call-update) | async-done | bytes 307216 | tf_op jit(solution)/shard_map/reduce_scatter | solution.py:448
  737.6 5.3 collective-permute-done.40
  (826 shorter events, 356.6 us)
Async XLA Ops:
  7.2 74.2 %all-gather.7.cloned.1.call-start = ((), (), s32[]{:S(2)}) async-start(), calls=%async_computation.6 | async-start | bytes 5222400 | tf_op jit(solution)/shard_map/all_gather | solution.py:396
  14.7 128.7 %all-gather.9.cloned.1.call-start = ((), (), s32[]{:S(2)}) async-start(), calls=%async_computation.7 | async-start | bytes 3932160 | tf_op jit(solution)/shard_map/all_gather | solution.py:135
  22.1 12.8 %collective-permute-start.6 = (bf16[1,48,2048]{2,1,0:T(8,128)(2,1)S(1)}, bf16[1,48,2048]{2,1,0:T(8,128)(2,1)S(1)}, u32[]{:S(2)}, u32[]{:S(2)}) collective-permute-start(bf16[1,48,2048]{2,1,0:T(8,128)(2,1)S(1)} %get-tuple-element.157), channel_id=1, source_target_pairs={{0,3},{1,2},{2,1},{3,0},{4,7},{5,6},{6,5},{7,4},{8,11},{9,10},{10,... | collective-permute-start | bytes 589832 | tf_op jit(solution)/shard_map/ppermute | solution.py:80
  35.8 146.3 %all-gather.11.cloned.1.call-start = ((), (), s32[]{:S(2)}) async-start(), calls=%async_computation.8 | async-start | bytes 1966080 | tf_op jit(solution)/shard_map/all_gather | solution.py:135
  46.5 192.3 %all-gather.13.cloned.1.call-start = ((), (), s32[]{:S(2)}) async-start(), calls=%async_computation.9 | async-start | bytes 5013504 | tf_op jit(solution)/shard_map/all_gather | solution.py:396
  47.3 253.2 %all-gather.15.cloned.1.call-start = ((), (), s32[]{:S(2)}) async-start(), calls=%async_computation.10 | async-start | bytes 3932160 | tf_op jit(solution)/shard_map/all_gather | solution.py:135
  49.8 12.0 %collective-permute-start.17 = (bf16[1,48,2048]{2,1,0:T(8,128)(2,1)S(1)}, bf16[1,48,2048]{2,1,0:T(8,128)(2,1)S(1)}, u32[]{:S(2)}, u32[]{:S(2)}) collective-permute-start(bf16[1,48,2048]{2,1,0:T(8,128)(2,1)S(1)} %get-tuple-element.154), channel_id=1, source_target_pairs={{0,2},{1,3},{2,0},{3,1},{4,6},{5,7},{6,4},{7,5},{8,10},{9,11},{10,... | collective-permute-start | bytes 589832 | tf_op jit(solution)/shard_map/ppermute | solution.py:80
  51.6 17.9 %collective-permute-start.18 = (bf16[1,48,2048]{2,1,0:T(8,128)(2,1)S(1)}, bf16[1,48,2048]{2,1,0:T(8,128)(2,1)S(1)}, u32[]{:S(2)}, u32[]{:S(2)}) collective-permute-start(bf16[1,48,2048]{2,1,0:T(8,128)(2,1)S(1)} %get-tuple-element.153), channel_id=1, source_target_pairs={{0,3},{1,2},{2,1},{3,0},{4,7},{5,6},{6,5},{7,4},{8,11},{9,10},{10,... | collective-permute-start | bytes 589832 | tf_op jit(solution)/shard_map/ppermute | solution.py:80
  70.4 268.6 %all-gather.17.cloned.1.call-start = ((), (), s32[]{:S(2)}) async-start(), calls=%async_computation.11 | async-start | bytes 1966080 | tf_op jit(solution)/shard_map/all_gather | solution.py:135
  78.8 446.5 %reduce-scatter.17.cloned.1.call-start = ((), (), s32[]{:S(2)}) async-start(), calls=%async_computation.17 | async-start | bytes 1966080 | tf_op jit(solution)/shard_map/reduce_scatter | solution.py:140
  265.0 12.5 %collective-permute-start.12 = (bf16[80,768]{1,0:T(8,128)(2,1)}, bf16[80,768]{1,0:T(8,128)(2,1)}, u32[]{:S(2)}, u32[]{:S(2)}) collective-permute-start(bf16[80,768]{1,0:T(8,128)(2,1)} %get-tuple-element.208), channel_id=1, source_target_pairs={{0,2},{1,3},{2,0},{3,1},{4,6},{5,7},{6,4},{7,5},{8,10},{9,11},{10,... | collective-permute-start | bytes 368648 | tf_op jit(solution)/shard_map/ppermute | solution.py:80
  265.5 13.5 %collective-permute-start.13 = (bf16[80,768]{1,0:T(8,128)(2,1)}, bf16[80,768]{1,0:T(8,128)(2,1)}, u32[]{:S(2)}, u32[]{:S(2)}) collective-permute-start(bf16[80,768]{1,0:T(8,128)(2,1)} %get-tuple-element.207), channel_id=1, source_target_pairs={{0,16},{1,17},{2,18},{3,19},{4,20},{5,21},{6,22},{7,23},{8,24},{9,... | collective-permute-start | bytes 368648 | tf_op jit(solution)/shard_map/ppermute | solution.py:80
  266.9 12.0 %collective-permute-start.14 = (bf16[80,768]{1,0:T(8,128)(2,1)}, bf16[80,768]{1,0:T(8,128)(2,1)}, u32[]{:S(2)}, u32[]{:S(2)}) collective-permute-start(bf16[80,768]{1,0:T(8,128)(2,1)} %get-tuple-element.206), channel_id=1, source_target_pairs={{0,18},{1,19},{2,16},{3,17},{4,22},{5,23},{6,20},{7,21},{8,26},{9,... | collective-permute-start | bytes 368648 | tf_op jit(solution)/shard_map/ppermute | solution.py:80
  269.8 10.5 %collective-permute-start.24 = (bf16[80,768]{1,0:T(8,128)(2,1)}, bf16[80,768]{1,0:T(8,128)(2,1)}, u32[]{:S(2)}, u32[]{:S(2)}) collective-permute-start(bf16[80,768]{1,0:T(8,128)(2,1)} %get-tuple-element.200), channel_id=1, source_target_pairs={{0,2},{1,3},{2,0},{3,1},{4,6},{5,7},{6,4},{7,5},{8,10},{9,11},{10,... | collective-permute-start | bytes 368648 | tf_op jit(solution)/shard_map/ppermute | solution.py:80
  270.2 10.0 %collective-permute-start.25 = (bf16[80,768]{1,0:T(8,128)(2,1)}, bf16[80,768]{1,0:T(8,128)(2,1)}, u32[]{:S(2)}, u32[]{:S(2)}) collective-permute-start(bf16[80,768]{1,0:T(8,128)(2,1)} %get-tuple-element.199), channel_id=1, source_target_pairs={{0,16},{1,17},{2,18},{3,19},{4,20},{5,21},{6,22},{7,23},{8,24},{9,... | collective-permute-start | bytes 368648 | tf_op jit(solution)/shard_map/ppermute | solution.py:80
  280.1 12.9 %collective-permute-start.15 = (bf16[4,80,768]{2,1,0:T(8,128)(2,1)S(1)}, bf16[4,80,768]{2,1,0:T(8,128)(2,1)S(1)}, u32[]{:S(2)}, u32[]{:S(2)}) collective-permute-start(bf16[4,80,768]{2,1,0:T(8,128)(2,1)S(1)} %pad_maximum_fusion.10), channel_id=1, source_target_pairs={{0,1},{1,0},{2,3},{3,2},{4,5},{5,4},{6,7},{7,6},{8,9},{9,8},{10,11... | collective-permute-start | bytes 1474568 | tf_op jit(solution)/shard_map/ppermute | solution.py:80
  284.5 9.3 %collective-permute-start.27 = (bf16[4,80,768]{2,1,0:T(8,128)(2,1)S(1)}, bf16[4,80,768]{2,1,0:T(8,128)(2,1)S(1)}, u32[]{:S(2)}, u32[]{:S(2)}) collective-permute-start(bf16[4,80,768]{2,1,0:T(8,128)(2,1)S(1)} %pad_maximum_fusion.12), channel_id=1, source_target_pairs={{0,1},{1,0},{2,3},{3,2},{4,5},{5,4},{6,7},{7,6},{8,9},{9,8},{10,11... | collective-permute-start | bytes 1474568 | tf_op jit(solution)/shard_map/ppermute | solution.py:80
  346.6 10.2 %collective-permute-start.20 = (bf16[320,768]{1,0:T(8,128)(2,1)}, bf16[320,768]{1,0:T(8,128)(2,1)}, u32[]{:S(2)}, u32[]{:S(2)}) collective-permute-start(bf16[320,768]{1,0:T(8,128)(2,1)} %slice.976), channel_id=1, source_target_pairs={{0,1},{1,0},{2,3},{3,2},{4,5},{5,4},{6,7},{7,6},{8,9},{9,8},{10,11... | collective-permute-start | bytes 1474568 | tf_op jit(solution)/shard_map/ppermute | solution.py:80
  356.7 179.4 %reduce-scatter.15.cloned.1.call-start = ((), (), s32[]{:S(2)}) async-start(), calls=%async_computation.16 | async-start | bytes 1966080 | tf_op jit(solution)/shard_map/reduce_scatter | solution.py:140
  364.0 13.6 %collective-permute-start.31 = (bf16[80,768]{1,0:T(8,128)(2,1)}, bf16[80,768]{1,0:T(8,128)(2,1)}, u32[]{:S(2)}, u32[]{:S(2)}) collective-permute-start(bf16[80,768]{1,0:T(8,128)(2,1)} %get-tuple-element.194), channel_id=1, source_target_pairs={{0,18},{1,19},{2,16},{3,17},{4,22},{5,23},{6,20},{7,21},{8,26},{9,... | collective-permute-start | bytes 368648 | tf_op jit(solution)/shard_map/ppermute | solution.py:80
  366.4 11.2 %collective-permute-start.30 = (bf16[80,768]{1,0:T(8,128)(2,1)}, bf16[80,768]{1,0:T(8,128)(2,1)}, u32[]{:S(2)}, u32[]{:S(2)}) collective-permute-start(bf16[80,768]{1,0:T(8,128)(2,1)} %get-tuple-element.195), channel_id=1, source_target_pairs={{0,16},{1,17},{2,18},{3,19},{4,20},{5,21},{6,22},{7,23},{8,24},{9,... | collective-permute-start | bytes 368648 | tf_op jit(solution)/shard_map/ppermute | solution.py:80
  366.9 10.7 %collective-permute-start.29 = (bf16[80,768]{1,0:T(8,128)(2,1)}, bf16[80,768]{1,0:T(8,128)(2,1)}, u32[]{:S(2)}, u32[]{:S(2)}) collective-permute-start(bf16[80,768]{1,0:T(8,128)(2,1)} %get-tuple-element.196), channel_id=1, source_target_pairs={{0,2},{1,3},{2,0},{3,1},{4,6},{5,7},{6,4},{7,5},{8,10},{9,11},{10,... | collective-permute-start | bytes 368648 | tf_op jit(solution)/shard_map/ppermute | solution.py:80
  413.4 131.7 %reduce-scatter.13.cloned.1.call-start = ((), (), s32[]{:S(2)}) async-start(), calls=%async_computation.15 | async-start | bytes 3932160 | tf_op jit(solution)/shard_map/reduce_scatter | solution.py:140
  420.0 152.9 %reduce-scatter.11.cloned.1.call-start = ((), (), s32[]{:S(2)}) async-start(), calls=%async_computation.14 | async-start | bytes 3932160 | tf_op jit(solution)/shard_map/reduce_scatter | solution.py:140
  431.0 223.5 %reduce-scatter.9.cloned.1.call-start = ((), (), s32[]{:S(2)}) async-start(), calls=%async_computation.13 | async-start | bytes 5222400 | tf_op jit(solution)/shard_map/reduce_scatter | solution.py:448
  465.0 270.1 %reduce-scatter.7.cloned.1.call-start = ((), (), s32[]{:S(2)}) async-start(), calls=%async_computation.12 | async-start | bytes 5222400 | tf_op jit(solution)/shard_map/reduce_scatter | solution.py:448
  533.3 10.2 %collective-permute-start.53 = (bf16[2,128,768]{2,1,0:T(8,128)(2,1)S(1)}, bf16[2,128,768]{2,1,0:T(8,128)(2,1)S(1)}, u32[]{:S(2)}, u32[]{:S(2)}) collective-permute-start(bf16[2,128,768]{2,1,0:T(8,128)(2,1)S(1)} %constant_dynamic-update-slice_fusion.32), channel_id=1, source_target_pairs={{0,16},{1,17},{2,18},{3,19},{4,20},{5,21},{6,22},{7,23},{8,24},{9,... | collective-permute-start | bytes 1179656 | tf_op jit(solution)/shard_map/ppermute | solution.py:80
  543.5 9.3 %collective-permute-start.51 = (bf16[2,128,768]{2,1,0:T(8,128)(2,1)S(1)}, bf16[2,128,768]{2,1,0:T(8,128)(2,1)S(1)}, u32[]{:S(2)}, u32[]{:S(2)}) collective-permute-start(bf16[2,128,768]{2,1,0:T(8,128)(2,1)S(1)} %constant_dynamic-update-slice_fusion.20), channel_id=1, source_target_pairs={{0,16},{1,17},{2,18},{3,19},{4,20},{5,21},{6,22},{7,23},{8,24},{9,... | collective-permute-start | bytes 1179656 | tf_op jit(solution)/shard_map/ppermute | solution.py:80
  562.9 20.6 %collective-permute-start.49 = (bf16[4,48,2048]{2,1,0:T(8,128)(2,1)}, bf16[4,48,2048]{2,1,0:T(8,128)(2,1)}, u32[]{:S(2)}, u32[]{:S(2)}) collective-permute-start(bf16[4,48,2048]{2,1,0:T(8,128)(2,1)} %constant_dynamic-update-slice_fusion.21), channel_id=1, source_target_pairs={{0,16},{1,17},{2,18},{3,19},{4,20},{5,21},{6,22},{7,23},{8,24},{9,... | collective-permute-start | bytes 2359304 | tf_op jit(solution)/shard_map/ppermute | solution.py:80
  575.0 18.1 %collective-permute-start.42 = (bf16[1,48,2048]{2,1,0:T(8,128)(2,1)}, bf16[1,48,2048]{2,1,0:T(8,128)(2,1)}, u32[]{:S(2)}, u32[]{:S(2)}) collective-permute-start(bf16[1,48,2048]{2,1,0:T(8,128)(2,1)} %get-tuple-element.179), channel_id=1, source_target_pairs={{0,1},{1,0},{2,3},{3,2},{4,5},{5,4},{6,7},{7,6},{8,9},{9,8},{10,11... | collective-permute-start | bytes 589832 | tf_op jit(solution)/shard_map/ppermute | solution.py:80
  592.0 9.8 %collective-permute-start.44 = (bf16[1,48,2048]{2,1,0:T(8,128)(2,1)S(1)}, bf16[1,48,2048]{2,1,0:T(8,128)(2,1)S(1)}, u32[]{:S(2)}, u32[]{:S(2)}) collective-permute-start(bf16[1,48,2048]{2,1,0:T(8,128)(2,1)S(1)} %get-tuple-element.177), channel_id=1, source_target_pairs={{0,3},{1,2},{2,1},{3,0},{4,7},{5,6},{6,5},{7,4},{8,11},{9,10},{10,... | collective-permute-start | bytes 589832 | tf_op jit(solution)/shard_map/ppermute | solution.py:80
  601.8 60.5 %collective-permute-start.45 = (bf16[4,48,2048]{2,1,0:T(8,128)(2,1)S(1)}, bf16[4,48,2048]{2,1,0:T(8,128)(2,1)}, u32[]{:S(2)}, u32[]{:S(2)}) collective-permute-start(bf16[4,48,2048]{2,1,0:T(8,128)(2,1)S(1)} %constant_dynamic-update-slice_fusion.24), channel_id=1, source_target_pairs={{0,16},{1,17},{2,18},{3,19},{4,20},{5,21},{6,22},{7,23},{8,24},{9,... | collective-permute-start | bytes 2359304 | tf_op jit(solution)/shard_map/ppermute | solution.py:80
  (223 other events, 1247.1 us)
Sparse Core Ops, SparseCore 0:
  14.8 66.4 all-gather.6
  83.5 59.8 all-gather.8
  145.0 37.0 all-gather.10
  184.8 53.9 all-gather.12
  240.8 59.6 all-gather.14
  301.9 37.0 all-gather.16
  356.8 34.1 reduce-scatter.16
  413.5 34.0 reduce-scatter.14
  450.6 59.8 reduce-scatter.12
  512.6 60.2 reduce-scatter.10
  577.5 76.9 reduce-scatter.8
  658.8 76.2 reduce-scatter.6

commit v2 on v1

v2 whole, which is shorter than its diff:
```python
import functools
import math

import jax
import jax.numpy as jnp
from jax import lax
from jax.experimental import pallas as pl
from jax.experimental.pallas import tpu as pltpu
from jax.sharding import PartitionSpec as P

HEAD_DIM = 64
EF = 4
NCONST = 2
TOP = 2
EXPERTS = 8
CAP = 80
SMALL = 2 + EXPERTS + 2 * NCONST + NCONST
ROWS = 16
LANES = 128

EPSILON = 1e-06
SCALE = 0.125
MASKED = -1000000000.0
AXES = ("rep", "shard")
BF16 = jnp.bfloat16
F32 = jnp.float32


def dot(a, b, dims=((1,), (0,))):
    return lax.dot_general(a, b, (dims, ((), ())), preferred_element_type=F32)


def rope_tables(tokens):
    half = HEAD_DIM // 2
    places = jnp.arange(tokens, dtype=jnp.int32).astype(F32)[:, None]
    powers = jnp.arange(half, dtype=jnp.int32).astype(F32) / half
    angles = places * jnp.exp(-math.log(10000.0) * powers)[None, :]
    cosine, sine = jnp.cos(angles), jnp.sin(angles)
    heads = LANES // HEAD_DIM
    return jnp.tile(cosine, (1, 2 * heads)), jnp.tile(
        jnp.concatenate([-sine, sine], axis=-1), (1, heads)
    )


def turn(block, cosine, sine):
    half = HEAD_DIM // 2
    lane = lax.broadcasted_iota(jnp.int32, block.shape, 1)
    width = block.shape[1]
    partner = jnp.where(
        lane % HEAD_DIM < half,
        pltpu.roll(block, width - half, 1),
        pltpu.roll(block, half, 1),
    )
    return block * cosine + partner * sine


def lane_pick(array, lane, index):
    return jnp.sum(jnp.where(lane == index, array, 0.0), axis=-1, keepdims=True)


def inverse_rms(x):
    return lax.rsqrt(jnp.mean(x * x, axis=-1, keepdims=True) + EPSILON)


def attention_bias(seg_col, seg_row):
    shape = (seg_col.shape[0], seg_row.shape[1])
    rows = lax.broadcasted_iota(jnp.int32, shape, 0)
    columns = lax.broadcasted_iota(jnp.int32, shape, 1)
    allowed = (seg_col[...] == seg_row[...]) & (columns <= rows)
    return jnp.where(allowed, 0.0, MASKED)


def head_masks(shape):
    lane = lax.broadcasted_iota(jnp.int32, shape, 1)
    return [(lane // HEAD_DIM) == half for half in range(LANES // HEAD_DIM)]


def columns_of(step, width):
    return pl.ds(pl.multiple_of(step * width, width), width)


def attention_forward_kernel(
    hidden, gains, weights, cosine, sine, seg_col, seg_row, mixing, previous, routes, gather,
    normed, query, keys, values, log_total, attended, middle, mixed_low, logits, coefs, rows,
    bias,
):
    tokens, features = hidden.shape
    h = hidden[...].astype(F32)
    normed[...] = (h * inverse_rms(h) * gains[0:1]).astype(BF16)
    bias[...] = attention_bias(seg_col, seg_row)
    wide = 2 * LANES
    for block, out in ((0, query), (1, keys)):

        @pl.loop(0, features // wide)
        def _(step):
            part = dot(normed[...], weights[block, :, columns_of(step, wide)])
            for k in range(2):
                turned = turn(part[:, k * LANES : (k + 1) * LANES], cosine[...], sine[...])
                out[:, columns_of(2 * step + k, LANES)] = turned.astype(BF16)

    @pl.loop(0, features // wide)
    def _(step):
        at = columns_of(step, wide)
        values[:, at] = dot(normed[...], weights[2, :, at]).astype(BF16)

    log_total[...] = jnp.zeros_like(log_total)

    @pl.loop(0, features // LANES)
    def _(step):
        at = columns_of(step, LANES)
        q, k, v = query[:, at], keys[:, at], values[:, at]
        lane = lax.broadcasted_iota(jnp.int32, log_total.shape, 1)
        total_out = jnp.zeros((tokens, LANES), F32)
        for half, mask in enumerate(head_masks(q.shape)):
            scores = dot(jnp.where(mask, q, 0), k, ((1,), (1,))) * SCALE + bias[...]
            top = jnp.max(scores, axis=-1, keepdims=True)
            weight = jnp.exp(scores - top)
            total = jnp.sum(weight, axis=-1, keepdims=True)
            probs = (weight * (1.0 / total)).astype(BF16)
            total_out += dot(probs, jnp.where(mask, v, 0))
            log_total[...] = jnp.where(
                lane == step * (LANES // HEAD_DIM) + half, top + jnp.log(total), log_total[...]
            )
        attended[:, at] = total_out.astype(BF16)

    @pl.loop(0, features // wide)
    def _(step):
        at = columns_of(step, wide)
        middle[:, at] = hidden[:, at].astype(F32) + dot(attended[...], weights[3, :, at])

    m = middle[...]
    low = (m * inverse_rms(m) * gains[1:2]).astype(BF16)
    mixed_low[...] = low
    rows[...] = dot(gather[...], low).astype(BF16)
    raw = dot(low, mixing[...])
    lane = lax.broadcasted_iota(jnp.int32, raw.shape, 1)
    now = jnp.where(lane < EXPERTS, raw + previous[...], 0.0)
    logits[...] = now
    route = [routes[:, k : k + 1] for k in range(TOP)]
    chosen = [lane_pick(now, lane, route[k]) for k in range(TOP)]
    best = jnp.maximum(chosen[0], chosen[1])
    chosen = [jnp.exp(c - best) for c in chosen]
    gates = [c / (chosen[0] + chosen[1]) for c in chosen]
    shares = []
    for c in range(NCONST):
        pair = [lane_pick(raw, lane, EXPERTS + 2 * c + i) for i in range(2)]
        best = jnp.maximum(pair[0], pair[1])
        pair = [jnp.exp(p - best) for p in pair]
        shares.append([p / (pair[0] + pair[1]) for p in pair])
    copies = [(route[k] == EF + 1).astype(F32) for k in range(TOP)]
    consts = [[(route[k] == EF + 2 + c).astype(F32) for c in range(NCONST)] for k in range(TOP)]
    weight = [sum(consts[k][c] * gates[k] for k in range(TOP)) for c in range(NCONST)]
    columns = list(gates)
    columns += [
        copies[k] + sum(consts[k][c] * shares[c][0] for c in range(NCONST)) for k in range(TOP)
    ]
    columns += [consts[k][c] * shares[c][1] for k in range(TOP) for c in range(NCONST)]
    columns += [shares[c][i] for c in range(NCONST) for i in range(2)]
    columns += weight
    columns += [
        sum(copies[k] * gates[k] for k in range(TOP))
        + sum(shares[c][0] * weight[c] for c in range(NCONST))
    ]
    columns += [shares[c][1] * weight[c] for c in range(NCONST)]
    packed = jnp.zeros_like(raw)
    for index, column in enumerate(columns):
        packed = jnp.where(lane == index, column, packed)
    coefs[...] = packed


GATE, MIXED, VECTOR, SHARE, WEIGHT, DIRECT, CONST = 0, 2, 4, 8, 12, 14, 15


def combine_kernel(coefs, middle, gains, scatter, outputs, vectors, result):
    coef = coefs[...]
    m = middle[...]
    total = m + coef[:, DIRECT : DIRECT + 1] * (m * inverse_rms(m) * gains[1:2])
    for k in range(TOP):
        total += coef[:, GATE + k : GATE + k + 1] * dot(scatter[k], outputs[...])
    for c in range(NCONST):
        total += coef[:, CONST + c : CONST + c + 1] * vectors[c : c + 1]
    result[...] = total


def value_rows_kernel(coefs, gather, d_result, rows):
    coef = coefs[...]
    rows[...] = sum(
        dot(gather[k], (coef[:, GATE + k : GATE + k + 1] * d_result[...]).astype(BF16))
        for k in range(TOP)
    ).astype(BF16)


def two_parts(x):
    high = x.astype(BF16)
    return high, (x - high.astype(F32)).astype(BF16)


def gate_backward_kernel(
    coefs, middle, gains, scatter, outputs, vectors, routes, mixed_low, mixing_t, d_result, d_next,
    d_logits, d_mixed, grads,
):
    coef = coefs[...]
    m = middle[...]
    dh = d_result[...]
    lane = lax.broadcasted_iota(jnp.int32, coef.shape, 1)

    def column(index):
        return coef[:, index : index + 1]

    along = jnp.sum(m * inverse_rms(m) * gains[1:2] * dh, axis=-1, keepdims=True)
    with_vector = [
        jnp.sum(dh * vectors[c : c + 1], axis=-1, keepdims=True) for c in range(NCONST)
    ]
    d_gates = []
    for k in range(TOP):
        value = jnp.sum(dot(scatter[k], outputs[...]) * dh, axis=-1, keepdims=True)
        value += column(MIXED + k) * along
        value += sum(column(VECTOR + k * NCONST + c) * with_vector[c] for c in range(NCONST))
        d_gates.append(value)
    mean = sum(column(GATE + k) * d_gates[k] for k in range(TOP))
    terms = d_next[...]
    for k in range(TOP):
        chosen = column(GATE + k) * (d_gates[k] - mean)
        terms += jnp.where(lane == routes[:, k : k + 1], chosen, 0.0)
    d_logits[...] = terms
    vector_terms = jnp.zeros_like(terms)
    for c in range(NCONST):
        share = [column(SHARE + 2 * c + i) for i in range(2)]
        d_share = [column(WEIGHT + c) * along, column(WEIGHT + c) * with_vector[c]]
        mean = share[0] * d_share[0] + share[1] * d_share[1]
        for i in range(2):
            terms = jnp.where(
                lane == EXPERTS + 2 * c + i, share[i] * (d_share[i] - mean), terms
            )
        vector_terms = jnp.where(
            lane == EXPERTS + 2 * NCONST + c, column(CONST + c), vector_terms
        )
    high, lowest = two_parts(terms)
    d_mixed[...] = column(DIRECT) * dh + dot(high, mixing_t[...]) + dot(lowest, mixing_t[...])
    both = ((0,), (0,))
    total = dot(high, mixed_low[...], both) + dot(lowest, mixed_low[...], both)
    high, lowest = two_parts(vector_terms)
    dh_high, dh_low = two_parts(dh)
    total += dot(high, dh_high, both) + dot(lowest, dh_high, both) + dot(high, dh_low, both)
    grads[...] = total[: grads.shape[0]]


def expert_forward_kernel(inputs, w_gate_up, w_down, gate_up, activated, own, others):
    units = w_down.shape[0]
    wide = min(2 * LANES, units)
    kept = own.shape[0]

    @pl.loop(0, units // wide)
    def _(step):
        at = columns_of(step, wide)
        gate = dot(inputs[...], w_gate_up[:, at])
        up_at = pl.ds(pl.multiple_of(units + step * wide, wide), wide)
        up = dot(inputs[...], w_gate_up[:, up_at])
        gate_up[:, at] = gate
        gate_up[:, up_at] = up
        activated[:, at] = (gate / (1.0 + jnp.exp(-gate)) * up).astype(BF16)

    @pl.loop(0, w_down.shape[1] // (2 * LANES))
    def _(step):
        at = columns_of(step, 2 * LANES)
        out = dot(activated[...], w_down[:, at])
        own[:, at] = out[:kept]
        others[:, at] = out[kept:].astype(BF16)


def expert_backward_kernel(d_expert, w_gate_up, w_down, gate_up, d_gate_up, own, others):
    units = w_down.shape[0]
    wide = min(2 * LANES, units)
    kept = own.shape[0]

    @pl.loop(0, units // wide)
    def _(step):
        at = columns_of(step, wide)
        up_at = pl.ds(pl.multiple_of(units + step * wide, wide), wide)
        d_active = dot(d_expert[...], w_down[at, :], ((1,), (1,)))
        gate, up = gate_up[:, at], gate_up[:, up_at]
        sigmoid = 1.0 / (1.0 + jnp.exp(-gate))
        d_gate_up[:, at] = (
            d_active * up * sigmoid * (1.0 + gate * (1.0 - sigmoid))
        ).astype(BF16)
        d_gate_up[:, up_at] = (d_active * gate * sigmoid).astype(BF16)

    @pl.loop(0, w_gate_up.shape[0] // (2 * LANES))
    def _(step):
        at = columns_of(step, 2 * LANES)
        out = dot(d_gate_up[...], w_gate_up[at, :], ((1,), (1,)))
        own[:, at] = out[:kept]
        others[:, at] = out[kept:].astype(BF16)


def norm_backward(grad, source, gain):
    inverse = inverse_rms(source)
    scaled = grad * gain
    gain_grad = jnp.sum(grad * source * inverse, axis=0, keepdims=True)
    mean = jnp.mean(scaled * source, axis=-1, keepdims=True)
    return inverse * scaled - source * (inverse * inverse * inverse * mean), gain_grad


def attention_backward_kernel(
    d_result, d_mixed, d_rows, scatter, middle, hidden, gains, weights, cosine, sine, seg_col,
    seg_row, query, keys, values, log_total,
    d_hidden, d_branch, d_projected, gain_grads,
    bias, d_attended, d_normed,
):
    tokens, features = hidden.shape
    wide = 2 * LANES
    total = d_mixed[...] + dot(scatter[...], d_rows[...])
    d_middle, gain_grad = norm_backward(total, middle[...], gains[1:2])
    d_middle = d_middle + d_result[...]
    gain_grads[1:2] = gain_grad
    d_hidden[...] = d_middle
    d_branch[...] = d_middle.astype(BF16)
    bias[...] = attention_bias(seg_col, seg_row)

    @pl.loop(0, features // wide)
    def _(step):
        at = columns_of(step, wide)
        d_attended[:, at] = dot(d_branch[...], weights[3, at, :], ((1,), (1,))).astype(BF16)

    @pl.loop(0, features // LANES)
    def _(step):
        at = columns_of(step, LANES)
        q, k, v, da = query[:, at], keys[:, at], values[:, at], d_attended[:, at]
        lane = lax.broadcasted_iota(jnp.int32, log_total.shape, 1)
        zero = jnp.zeros((tokens, LANES), F32)
        dq, dk, dv = zero, zero, zero
        for half, mask in enumerate(head_masks(q.shape)):
            q_half, da_half = jnp.where(mask, q, 0), jnp.where(mask, da, 0)
            scores = dot(q_half, k, ((1,), (1,))) * SCALE + bias[...]
            shift = lane_pick(log_total[...], lane, step * (LANES // HEAD_DIM) + half)
            probs = jnp.exp(scores - shift)
            dv += dot(probs.astype(BF16), da_half, ((0,), (0,)))
            d_probs = dot(da_half, v, ((1,), (1,)))
            mean = jnp.sum(d_probs * probs, axis=-1, keepdims=True)
            d_scores = (probs * (d_probs - mean)).astype(BF16)
            dq += dot(d_scores, jnp.where(mask, k, 0))
            dk += dot(d_scores, q_half, ((0,), (0,)))
        d_projected[0, :, at] = turn(dq * SCALE, cosine[...], -sine[...]).astype(BF16)
        d_projected[1, :, at] = turn(dk * SCALE, cosine[...], -sine[...]).astype(BF16)
        d_projected[2, :, at] = dv.astype(BF16)

    @pl.loop(0, features // wide)
    def _(step):
        at = columns_of(step, wide)
        d_normed[:, at] = sum(
            dot(d_projected[b], weights[b, at, :], ((1,), (1,))) for b in range(3)
        )

    d_input, gain_grad = norm_backward(d_normed[...], hidden[...].astype(F32), gains[0:1])
    gain_grads[0:1] = gain_grad
    d_hidden[...] += d_input


def call(kernel, outs, args, scratch=(), megabytes=32):
    return pl.pallas_call(
        kernel,
        out_shape=[jax.ShapeDtypeStruct(shape, dtype) for shape, dtype in outs],
        scratch_shapes=[pltpu.VMEM(shape, dtype) for shape, dtype in scratch],
        compiler_params=pltpu.CompilerParams(vmem_limit_bytes=megabytes * 1024 * 1024),
    )(*args)


class Layout:
    def __init__(self, mesh):
        self.reps, self.shards = mesh.shape["rep"], mesh.shape["shard"]
        self.lines = self.shards // EF
        assert self.shards % EF == 0 and EF % self.reps == 0

    def pairs(self, move):
        found = []
        for rep in range(self.reps):
            for shard in range(self.shards):
                r, z, j = move(rep, shard // EF, shard % EF)
                found.append((rep * self.shards + shard, r * self.shards + z * EF + j))
        return found

    def send(self, x, move):
        return lax.ppermute(x, AXES, self.pairs(move))

    def expert_move(self, mask, shift):
        def move(r, z, j):
            number = r * EF + j
            e, f = (number // self.reps) ^ mask, (number % self.reps + shift) % self.reps
            number = e * self.reps + f
            return number // EF, z, number % EF

        return move

    def place(self):
        rep, shard = lax.axis_index("rep"), lax.axis_index("shard")
        j = shard % EF
        return rep, j, (rep * EF + j) // self.reps

    def quad_exchange(self, blocks, j):
        got = lax.dynamic_update_slice_in_dim(
            jnp.zeros_like(blocks), lax.dynamic_slice_in_dim(blocks, j, 1, 0), j, 0
        )
        for mask in range(1, EF):
            other = j ^ mask
            block = lax.dynamic_slice_in_dim(blocks, other, 1, 0)
            block = self.send(block, lambda r, z, q: (r, z, q ^ mask))
            got = lax.dynamic_update_slice_in_dim(got, block, other, 0)
        return got

    def part_exchange(self, blocks, j):
        count = EF // self.reps
        mine = j // self.reps
        got = lax.dynamic_update_slice_in_dim(
            jnp.zeros_like(blocks), lax.dynamic_slice_in_dim(blocks, mine, 1, 0), mine, 0
        )
        for mask in range(1, count):
            other = mine ^ mask
            block = lax.dynamic_slice_in_dim(blocks, other, 1, 0)
            block = self.send(block, lambda r, z, q: (r, z, q ^ (mask * self.reps)))
            got = lax.dynamic_update_slice_in_dim(got, block, other, 0)
        return got

    def rep_gather(self, x, rep):
        got = lax.dynamic_update_slice_in_dim(
            jnp.zeros((self.reps,) + x.shape, x.dtype), x[None], rep, 0
        )
        for shift in range(1, self.reps):
            block = self.send(x, lambda r, z, q: ((r + shift) % self.reps, z, q))
            got = lax.dynamic_update_slice_in_dim(
                got, block[None], (rep + self.reps - shift) % self.reps, 0
            )
        return got

    def line_groups(self):
        return [[z * EF + j for z in range(self.lines)] for j in range(EF)]

    def line_gather(self, x):
        return lax.all_gather(
            x, "shard", axis=0, tiled=True, axis_index_groups=self.line_groups()
        )

    def line_sum(self, x):
        return lax.psum_scatter(
            x, "shard", scatter_dimension=0, tiled=True, axis_index_groups=self.line_groups()
        )

    def dense_gather(self, x, rep, j):
        z = lax.axis_index("shard") // EF
        reps, lines = self.reps, self.lines
        line = lax.dynamic_update_slice_in_dim(
            jnp.zeros((lines,) + x.shape, x.dtype), x[None], z, 0
        )
        for shift in range(1, lines):
            block = self.send(x, lambda r, q, k: (r, (q + shift) % lines, k))
            line = lax.dynamic_update_slice_in_dim(
                line, block[None], (z + lines - shift) % lines, 0
            )
        cut = lines // 2
        high, core = j // 2, j % 2
        full = jnp.zeros((reps, lines, 2, 2) + x.shape, x.dtype)

        def put(full, block, r, at, hi, lo):
            return lax.dynamic_update_slice(full, block[None, :, None, None], (r, at, hi, lo, 0, 0))

        def over_rep(block, shift):
            return self.send(block, lambda r, q, k: ((r + shift) % reps, q, k))

        def over_high(block):
            return self.send(block, lambda r, q, k: (r, q, k ^ 2))

        sides = [(shift, over_rep(line, shift)) for shift in range(1, reps)]
        flip = over_high(line)
        full = put(full, line, rep, 0, high, core)
        full = put(full, flip, rep, 0, 1 - high, core)
        for shift, block in sides:
            source = (rep + reps - shift) % reps
            full = put(full, block, source, 0, high, core)
            full = put(full, over_high(block[:cut]), source, 0, 1 - high, core)
            full = put(full, over_rep(flip[cut:], shift), source, cut, 1 - high, core)
        half = lax.dynamic_slice_in_dim(full, core, 1, 3)
        half = self.send(half, lambda r, q, k: (r, q, k ^ 1))
        return lax.dynamic_update_slice_in_dim(full, half, 1 - core, 3)

    def dense_sum(self, parts, rep, j):
        z = lax.axis_index("shard") // EF
        reps, lines = self.reps, self.lines
        high, core = j // 2, j % 2

        def over_rep(block, shift):
            return self.send(block, lambda r, q, k: ((r + shift) % reps, q, k))

        def over_high(block):
            return self.send(block, lambda r, q, k: (r, q, k ^ 2))

        def rep_step(x):
            total = lax.dynamic_slice_in_dim(x, rep, 1, 0)[0].astype(F32)
            for shift in range(1, reps):
                block = lax.dynamic_slice_in_dim(x, (rep + shift) % reps, 1, 0)[0]
                total = total + over_rep(block, shift).astype(F32)
            return total.astype(BF16)

        def high_step(x, axis):
            mine = lax.dynamic_slice_in_dim(x, high, 1, axis)
            other = over_high(lax.dynamic_slice_in_dim(x, 1 - high, 1, axis))
            return jnp.squeeze(mine.astype(F32) + other.astype(F32), axis).astype(BF16)

        other = self.send(parts(1 - core), lambda r, q, k: (r, q, k ^ 1))
        both = (parts(core).astype(F32) + other.astype(F32)).astype(BF16)
        cut = lines // 2
        first = rep_step(high_step(both[:, :cut], 2))
        second = high_step(rep_step(both[:, cut:]), 1)
        line = jnp.concatenate([first, second])
        total = lax.dynamic_slice_in_dim(line, z, 1, 0)[0].astype(F32)
        for shift in range(1, lines):
            block = lax.dynamic_slice_in_dim(line, (z + shift) % lines, 1, 0)[0]
            block = self.send(block, lambda r, q, k: (r, (q + shift) % lines, k))
            total = total + block.astype(F32)
        return self.rep_gather(total.astype(BF16), rep)

    def dispatch(self, rows):
        blocks = rows.reshape(EF, CAP, -1)
        own = jnp.stack(
            [blocks[0]] + [self.send(blocks[m], self.expert_move(m, 0)) for m in range(1, EF)]
        )
        parts = [own] + [self.send(own, self.expert_move(0, g)) for g in range(1, self.reps)]
        return jnp.concatenate(parts).reshape(self.reps * EF * CAP, -1)

    def collect(self, own, others):
        total = own
        for g in range(1, self.reps):
            block = others[(g - 1) * EF * CAP : g * EF * CAP]
            total = total + self.send(block, self.expert_move(0, self.reps - g)).astype(F32)
        total = total.astype(BF16).reshape(EF, CAP, -1)
        return jnp.concatenate(
            [total[0]] + [self.send(total[m], self.expert_move(m, 0)) for m in range(1, EF)]
        )


def split_columns(array, layout):
    width = array.shape[-1] // (2 * layout.shards)
    return array.reshape(array.shape[:-1] + (2, layout.shards // layout.reps, layout.reps, width))


def expert_weights(layout, w_gate_up, w_down, rep, j):
    features = w_gate_up.shape[1]
    blocks = split_columns(w_gate_up, layout)
    blocks = jnp.transpose(blocks, (0, 4, 1, 2, 3, 5)).reshape(EF * layout.reps, features, -1)
    mine = lax.dynamic_slice_in_dim(blocks, rep * EF, EF, 0)
    mine = layout.quad_exchange(mine, j).reshape(EF * features, -1)
    gate_up = layout.line_gather(mine)
    count = EF // layout.reps
    down = lax.dynamic_slice_in_dim(w_down, rep * count, count, 0)
    down = layout.part_exchange(down, j).reshape(count * w_down.shape[1], -1)
    return gate_up, layout.line_gather(down)


def expert_grads(layout, grad_gate_up, grad_down, rep, j):
    down = layout.line_sum(grad_down)
    count = EF // layout.reps
    down = layout.part_exchange(down.reshape(count, -1, down.shape[-1]), j)
    down = layout.rep_gather(down, rep).reshape((EF,) + down.shape[1:]).astype(F32)
    mine = layout.line_sum(grad_gate_up)
    mine = layout.quad_exchange(mine.reshape(EF, -1, mine.shape[-1]), j)
    full = layout.rep_gather(mine, rep)
    features = mine.shape[1]
    full = full.reshape(EF, layout.reps, features, 2, layout.shards // layout.reps, -1)
    full = jnp.transpose(full, (0, 2, 3, 4, 1, 5)).reshape(EF, features, -1)
    return full.astype(F32), down


def place_pairs(routes, priority, expert):
    flat = routes.reshape(-1)
    ahead = (flat[:, None] == flat[None, :]) & (priority[:, None] < priority[None, :])
    position = jnp.sum(ahead.astype(jnp.int32), axis=0)
    kept = (flat < EF) & (position < CAP)
    slot = jnp.where(kept, (flat ^ expert) * CAP + position, EF * CAP).reshape(-1, TOP).T
    places = jnp.arange(EF * CAP, dtype=jnp.int32)
    gather = (places[None, :, None] == slot[:, None, :]).astype(BF16)
    scatter = (places[None, None, :] == slot[:, :, None]).astype(BF16)
    return gather, scatter


def attention_forward(shared, dense, hidden, previous, routes, gather):
    gains, weights, mixing = dense
    tokens, features = hidden.shape
    cosine, sine, seg_col, seg_row = shared
    low = ((tokens, features), BF16)
    lanes = ((tokens, LANES), F32)
    return call(
        attention_forward_kernel,
        [low, low, low, low, lanes, low, ((tokens, features), F32), low, lanes, lanes]
        + [((EF * CAP, features), BF16)],
        (hidden, gains, weights, cosine, sine, seg_col, seg_row, mixing, previous, routes)
        + (gather[0] + gather[1],),
        [((tokens, tokens), F32)],
    )


def expert_forward(layout, inputs, w_gate_up, w_down):
    count, features = inputs.shape
    units = w_down.shape[0]
    return call(
        expert_forward_kernel,
        [((count, 2 * units), F32), ((count, units), BF16)]
        + [((EF * CAP, features), F32), ((count - EF * CAP, features), BF16)],
        (inputs, w_gate_up, w_down),
    )


def expert_backward(layout, d_expert, w_gate_up, w_down, gate_up):
    count, features = d_expert.shape
    units = w_down.shape[0]
    return call(
        expert_backward_kernel,
        [((count, 2 * units), BF16)]
        + [((EF * CAP, features), F32), ((count - EF * CAP, features), BF16)],
        (d_expert, w_gate_up, w_down, gate_up),
    )


def local(
    layout,
    hidden_in,
    gate_in,
    routes,
    priority,
    segments,
    norm_attn,
    w_qkv,
    w_out,
    norm_moe,
    w_router,
    w_const,
    const_vec,
    w_gate_up,
    w_down,
    grad_out,
):
    layers = w_qkv.shape[0]
    tokens, features = hidden_in.shape
    rep, j, expert = layout.place()
    slim = w_qkv.shape[1]
    small = [
        jnp.concatenate(
            [norm_attn[l][:, None], norm_moe[l][:, None], w_router[l], w_const[l], const_vec[l].T],
            axis=-1,
        ).reshape(1, -1)
        for l in range(layers)
    ]
    small = jnp.concatenate(small, axis=-1)
    extra = ROWS * features
    small = jnp.pad(small, ((0, 0), (0, extra - small.shape[1]))).reshape(ROWS, features)
    count = EF // layout.reps
    dense, moe = [], []
    small_full = None
    for l in range(layers):
        blocks = jnp.concatenate(
            [jnp.transpose(w_qkv[l].reshape(slim, 3, features), (1, 0, 2)), w_out[l][None]]
        )
        mine = lax.dynamic_slice_in_dim(blocks, rep * count, count, 0).reshape(count * slim, features)
        if l == 0:
            mine = jnp.concatenate([mine, small])
        full = layout.dense_gather(mine, rep, j)
        if l == 0:
            small_full = full[0, :, :, :, count * slim :].reshape(layout.shards, -1)
        full = full[:, :, :, :, : count * slim].reshape(
            layout.reps, layout.shards, count, slim, features
        )
        dense.append(jnp.transpose(full, (0, 2, 1, 3, 4)).reshape(4, features, features))
        moe.append(expert_weights(layout, w_gate_up[l], w_down[l], rep, j))
    packs, vectors, mixing_t = [], [], []
    for l in range(layers):
        part = small_full[:, l * slim * SMALL : (l + 1) * slim * SMALL]
        part = part.reshape(features, SMALL)
        mixing = part[:, 2 : SMALL - NCONST]
        mixing = jnp.pad(mixing, ((0, 0), (0, LANES - mixing.shape[1])))
        packs.append((part[:, :2].T.astype(F32), dense[l], mixing))
        mixing_t.append(mixing.T)
        vectors.append(part[:, SMALL - NCONST :].T.astype(F32))

    shared = (*rope_tables(tokens), segments.reshape(-1, 1), segments)
    pairs = [place_pairs(routes[l], priority[l, 0], expert) for l in range(layers)]

    hidden = hidden_in
    previous = jnp.pad(gate_in, ((0, 0), (0, LANES - EXPERTS)))
    kept = []
    for l in range(layers):
        gather, scatter = pairs[l]
        state = attention_forward(shared, packs[l], hidden, previous, routes[l], gather)
        normed, query, keys, values, log_total, attended, middle, low, logits, coefs, rows = state
        inputs = layout.dispatch(rows)
        gate_up, activated, own, others = expert_forward(layout, inputs, *moe[l])
        outputs = layout.collect(own, others)
        (result,) = call(
            combine_kernel,
            [((tokens, features), F32)],
            (coefs, middle, packs[l][0], scatter, outputs, vectors[l]),
        )
        kept.append((hidden, state, inputs, gate_up, activated, outputs))
        hidden, previous = result, logits

    grad_hidden = grad_out
    grad_gate = jnp.zeros_like(previous)
    dense_grads, moe_grads = [None] * layers, [None] * layers
    for l in reversed(range(layers)):
        gather, scatter = pairs[l]
        source, state, inputs, gate_up, activated, outputs = kept[l]
        normed, query, keys, values, log_total, attended, middle, low, logits, coefs, _ = state
        (rows,) = call(
            value_rows_kernel,
            [((EF * CAP, features), BF16)],
            (coefs, gather, grad_hidden),
        )
        d_expert = layout.dispatch(rows)
        grad_gate, d_mixed, mix_grads = call(
            gate_backward_kernel,
            [((tokens, LANES), F32), ((tokens, features), F32), ((SMALL - 2, features), F32)],
            (coefs, middle, packs[l][0], scatter, outputs, vectors[l], routes[l], low)
            + (mixing_t[l], grad_hidden, grad_gate),
        )
        grad_down = dot(activated, d_expert, ((0,), (0,))).astype(BF16)
        d_gate_up, own, others = expert_backward(layout, d_expert, *moe[l], gate_up)
        d_rows = layout.collect(own, others)
        grad_gate_up = dot(inputs, d_gate_up, ((0,), (0,))).astype(BF16)
        moe_grads[l] = expert_grads(layout, grad_gate_up, grad_down, rep, j)
        grad_hidden, d_branch, d_projected, gain_grads = call(
            attention_backward_kernel,
            [((tokens, features), F32), ((tokens, features), BF16)]
            + [((3, tokens, features), BF16), ((2, features), F32)],
            (grad_hidden, d_mixed, d_rows, scatter[0] + scatter[1], middle, source)
            + (packs[l][0], packs[l][1], *shared, query, keys, values, log_total),
            [((tokens, tokens), F32), ((tokens, features), BF16), ((tokens, features), F32)],
        )
        grad_dense = jnp.stack(
            [dot(normed, d_projected[b], ((0,), (0,))).astype(BF16) for b in range(3)]
            + [dot(attended, d_branch, ((0,), (0,))).astype(BF16)]
        )
        small_grads = jnp.concatenate([gain_grads, mix_grads]).T.astype(BF16)
        lines = layout.lines
        blocks = grad_dense.reshape(layout.reps, count, lines, 2, 2, slim, features)
        small_grads = small_grads.reshape(lines, 2, 2, slim * SMALL)
        small_grads = jnp.pad(
            small_grads, ((0, 0),) * 3 + ((0, ROWS * features - slim * SMALL),)
        ).reshape(lines, 2, 2, ROWS, features)

        def parts(c):
            chosen = lax.dynamic_slice_in_dim(blocks, c, 1, 4)[:, :, :, :, 0]
            chosen = jnp.transpose(chosen, (0, 2, 3, 1, 4, 5)).reshape(
                layout.reps, lines, 2, count * slim, features
            )
            extra = lax.dynamic_slice_in_dim(small_grads, c, 1, 2)[:, :, 0]
            extra = jnp.broadcast_to(extra[None], (layout.reps,) + extra.shape)
            return jnp.concatenate([chosen, extra], axis=3)

        dense_grads[l] = layout.dense_sum(parts, rep, j)

    dense_all = jnp.stack(dense_grads).astype(F32)
    small_all = dense_all[:, 0, count * slim :].reshape(layers, -1)[:, : slim * SMALL]
    small_all = small_all.reshape(layers, slim, SMALL)
    dense_all = dense_all[:, :, : count * slim].reshape(layers, 4, slim, features)
    qkv_all = jnp.transpose(dense_all[:, :3], (0, 2, 1, 3)).reshape(layers, slim, 3 * features)
    return (
        hidden.astype(BF16),
        grad_hidden,
        grad_gate[:, :EXPERTS],
        small_all[:, :, 0],
        qkv_all,
        dense_all[:, 3],
        small_all[:, :, 1],
        small_all[:, :, 2 : 2 + EXPERTS],
        small_all[:, :, 2 + EXPERTS : SMALL - NCONST],
        jnp.transpose(small_all[:, :, SMALL - NCONST :], (0, 2, 1)),
        jnp.stack([g[0] for g in moe_grads]),
        jnp.stack([g[1] for g in moe_grads]),
    )


def solution(mesh):
    return jax.shard_map(
        functools.partial(local, Layout(mesh)),
        mesh=mesh,
        in_specs=(
            P(("rep", "shard"), None),
            P(("rep", "shard"), None),
            P(None, ("rep", "shard"), None),
            P(None, ("rep", "shard"), None),
            P(("rep", "shard"), None),
            P(None, "shard"),
            P(None, "shard", None),
            P(None, "shard", None),
            P(None, "shard"),
            P(None, "shard", None),
            P(None, "shard", None),
            P(None, None, "shard"),
            P(None, None, "shard", None),
            P(None, None, "shard", None),
            P(("rep", "shard"), None),
        ),
        out_specs=(
            P(("rep", "shard"), None),
            P(("rep", "shard"), None),
            P(("rep", "shard"), None),
            P(None, "shard"),
            P(None, "shard", None),
            P(None, "shard", None),
            P(None, "shard"),
            P(None, "shard", None),
            P(None, "shard", None),
            P(None, None, "shard"),
            P(None, None, "shard", None),
            P(None, None, "shard", None),
        ),
        check_vma=False,
    )
```

time: 766 us -> 619 us (0.81)
  the two profiles are of different devices: /device:TPU:8 before, /device:TPU:0 now
where the time goes in v2:
time: 619 us; the launch traced here: 609 us
  local copies, waits for them, and re-layouts  185 us (30%)
  waiting for transfers between devices  179 us (29%)
  starting transfers between devices  101 us (16%)
  Pallas kernels  67.6 us (11%)
  other arithmetic  33.2 us (5%)
  matrix products  24.3 us (4%)
  between operations  17.7 us (3%)
    ppermute x86, waiting for transfers between devices, send(): return lax.ppermute(x, AXES, self.pairs(move))  165 us
    ppermute x86, starting transfers between devices, send(): return lax.ppermute(x, AXES, self.pairs(move))  101 us
    pallas_call x14, Pallas kernels, call(): pl.pallas_call(kernel, out_shape=[jax.ShapeDtypeStruct(shape, dtype) for...  67.6 us
    unnamed x348, local copies, waits for them, and re-layouts  48.7 us
    dot_general x12, matrix products, dot(): return lax.dot_general(a, b, (dims, ((), ())), preferred_element_type=F32)  24.3 us
    all_gather x4, waiting for transfers between devices, line_gather(): lax.all_gather(x, 'shard', axis=0, tiled=True, axis_index_groups=self.lin...  13.8 us
    dynamic_update_slice x10, local copies, waits for them, and re-layouts, put(): lax.dynamic_update_slice(full, block[None, :, None, None], (r, at, hi, lo...  13.7 us
    convert_element_type x4, local copies, waits for them, and re-layouts, expert_grads(): return (full.astype(F32), down)  12.9 us
  transfers between devices with their start and end apart: 94, of which 44 were waited for; matrix products, arithmetic and copies ran while one was open for 29% of the time, Pallas kernels for 11%

profile of v2, /device:TPU:0, one launch (start us, length us, event | category | flops | bytes accessed | tf_op | source)
XLA Modules:
  0.0 608.6 jit_solution(5136744048833250338)
XLA Ops:
  21.6 9.2 %collective-permute-done.15 = bf16[1,128,768]{2,1,0:T(8,128)(2,1)S(1)} collective-permute-done((bf16[1,128,768]{2,1,0:T(8,128)(2,1)}, bf16[1,128,768]{2,1,0:T(8,128)(2,1)S(1)}, u32[]{:S(2)}, u32[]{:S(2)}) %collective-permute-start.15) | collective-permute-done | bytes 196640 | tf_op jit(solution)/shard_map/ppermute | solution.py:383
  75.8 14.6 %collective-permute-start.22 = (bf16[96,768]{1,0:T(8,128)(2,1)}, bf16[96,768]{1,0:T(8,128)(2,1)}, u32[]{:S(2)}, u32[]{:S(2)}) collective-permute-start(bf16[96,768]{1,0:T(8,128)(2,1)} %bitcast.52), channel_id=1, source_target_pairs={{0,12},{1,13},{2,14},{3,15},{4,0},{5,1},{6,2},{7,3},{8,4},{9,5},{1... | collective-permute-start | bytes 442376 | tf_op jit(solution)/shard_map/ppermute | solution.py:383
  118.0 13.0 %collective-permute-done.24 = bf16[4,96,768]{2,1,0:T(8,128)(2,1)} collective-permute-done((bf16[4,96,768]{2,1,0:T(8,128)(2,1)S(1)}, bf16[4,96,768]{2,1,0:T(8,128)(2,1)}, u32[]{:S(2)}, u32[]{:S(2)}) %collective-permute-start.24) | collective-permute-done | bytes 589856 | tf_op jit(solution)/shard_map/ppermute | solution.py:383
  149.6 4.9 slice.441
  156.0 5.0 copy.178
  163.7 8.9 %shard_map.238 = (bf16[256,768]{1,0:T(8,128)(2,1)S(1)}, bf16[256,768]{1,0:T(8,128)(2,1)S(1)}, bf16[256,768]{1,0:T(8,128)(2,1)S(1)}, bf16[256,768]{1,0:T(8,128)(2...) custom-call(bf16[256,768]{1,0:T(8,128)(2,1)S(1)} %copy-done.51, ...), custom_call_target="tpu_custom_call" | custom-call | tf_op jit(solution)/shard_map/pallas_call | solution.py:360
  189.5 5.3 shard_map.239
  198.1 3.8 constant_dynamic-update-slice_fusion.32
  202.0 5.1 copy.198
  223.6 9.2 %shard_map.241 = (bf16[256,768]{1,0:T(8,128)(2,1)S(1)}, bf16[256,768]{1,0:T(8,128)(2,1)S(1)}, bf16[256,768]{1,0:T(8,128)(2,1)S(1)}, bf16[256,768]{1,0:T(8,128)(2...) custom-call(f32[256,768]{1,0:T(8,128)S(1)} %shard_map.240.hidden, ...), custom_call_target="tpu_custom_call" | custom-call | tf_op jit(solution)/shard_map/pallas_call | solution.py:360
  247.5 13.8 %all-gather.9.cloned.1.call-done.w_gate_up = bf16[768,2048]{1,0:T(8,128)(2,1)} async-done(((bf16[192,2048]{1,0:T(8,128)(2,1)}), bf16[768,2048]{1,0:T(8,128)(2,1)}) %all-gather.9.cloned.1.call-update) | async-done | bytes 3145744 | tf_op jit(solution)/shard_map/all_gather | solution.py:438
  264.5 5.5 shard_map.242
  273.6 3.9 convolution_convert_fusion.2
  287.1 5.1 shard_map.246
  311.6 9.3 %shard_map.247 = (f32[256,768]{1,0:T(8,128)S(1)}, bf16[256,768]{1,0:T(8,128)(2,1)S(1)}, bf16[3,256,768]{2,1,0:T(8,128)(2,1)S(1)}, f32[2,768]{1,0:T(2,128)S(1)}) custom-call(f32[256,768]{1,0:T(8,128)S(1)} %copy-done.8, f32[256,768]{1,0:T(8,128)S(1)} %get-tuple-element.73.d_mixed, bf16[320,768]{1,0:T(8,128)(2,1)S(1)} %pad_maximum_fusion.10.d_rows, ...), custom_call_target="tpu_custom_call" | custom-call | tf_op jit(solution)/shard_map/pallas_call | solution.py:360
  335.7 5.8 convolution_convert_fusion
  348.4 5.3 shard_map.250
  374.6 10.2 %shard_map.251 = (f32[256,768]{1,0:T(8,128)}, bf16[256,768]{1,0:T(8,128)(2,1)S(1)}, bf16[3,256,768]{2,1,0:T(8,128)(2,1)S(1)}, f32[2,768]{1,0:T(2,128)S(1)}) custom-call(f32[256,768]{1,0:T(8,128)S(1)} %copy-done.10, f32[256,768]{1,0:T(8,128)S(1)} %get-tuple-element.84.d_mixed, bf16[320,768]{1,0:T(8,128)(2,1)S(1)} %pad_maximum_fusion.12.d_rows, ...), custom_call_target="tpu_custom_call" | custom-call | tf_op jit(solution)/shard_map/pallas_call | solution.py:360
  406.4 3.9 collective-permute-done.84
  411.2 5.7 convolution_convert_fusion.1
  442.7 8.6 %collective-permute-done.66 = bf16[2,2,1,112,768]{4,3,1,2,0:T(8,128)(2,1)S(1)} collective-permute-done((bf16[2,2,1,112,768]{4,3,1,2,0:T(8,128)(2,1)S(1)}, bf16[2,2,1,112,768]{4,3,1,2,0:T(8,128)(2,1)S(1)}, u32[]{:S(2)}, u32[]{:S(2)}) %collective-permute-start.66) | collective-permute-done | bytes 688160 | tf_op jit(solution)/shard_map/ppermute | solution.py:383
  457.2 8.9 %collective-permute-done.57 = bf16[2,2,1,112,768]{4,3,1,2,0:T(8,128)(2,1)S(1)} collective-permute-done((bf16[2,2,1,112,768]{4,3,1,2,0:T(8,128)(2,1)S(1)}, bf16[2,2,1,112,768]{4,3,1,2,0:T(8,128)(2,1)S(1)}, u32[]{:S(2)}, u32[]{:S(2)}) %collective-permute-start.57) | collective-permute-done | bytes 688160 | tf_op jit(solution)/shard_map/ppermute | solution.py:383
  472.0 5.7 collective-permute-done.67
  484.8 9.2 %collective-permute-done.72 = bf16[112,768]{1,0:T(8,128)(2,1)S(1)} collective-permute-done((bf16[112,768]{1,0:T(8,128)(2,1)S(1)}, bf16[112,768]{1,0:T(8,128)(2,1)S(1)}, u32[]{:S(2)}, u32[]{:S(2)}) %collective-permute-start.72) | collective-permute-done | bytes 172064 | tf_op jit(solution)/shard_map/ppermute | solution.py:383
  494.0 5.4 collective-permute-start.61
  499.4 11.6 %collective-permute-done.71 = bf16[112,768]{1,0:T(8,128)(2,1)S(1)} collective-permute-done((bf16[112,768]{1,0:T(8,128)(2,1)S(1)}, bf16[112,768]{1,0:T(8,128)(2,1)S(1)}, u32[]{:S(2)}, u32[]{:S(2)}) %collective-permute-start.71) | collective-permute-done | bytes 172064 | tf_op jit(solution)/shard_map/ppermute | solution.py:383
  512.8 9.6 %collective-permute-done.62 = bf16[112,768]{1,0:T(8,128)(2,1)S(1)} collective-permute-done((bf16[112,768]{1,0:T(8,128)(2,1)S(1)}, bf16[112,768]{1,0:T(8,128)(2,1)S(1)}, u32[]{:S(2)}, u32[]{:S(2)}) %collective-permute-start.62) | collective-permute-done | bytes 172064 | tf_op jit(solution)/shard_map/ppermute | solution.py:383
  524.1 3.9 collective-permute-done.64
  538.6 5.1 collective-permute-done.79
  550.9 6.3 %collective-permute-done.75 = bf16[1,48,2048]{2,1,0:T(8,128)(2,1)S(1)} collective-permute-done((bf16[1,48,2048]{2,1,0:T(8,128)(2,1)S(1)}, bf16[1,48,2048]{2,1,0:T(8,128)(2,1)S(1)}, u32[]{:S(2)}, u32[]{:S(2)}) %collective-permute-start.75) | collective-permute-done | bytes 196640 | tf_op jit(solution)/shard_map/ppermute | solution.py:383
  561.6 6.9 %collective-permute-done.81 = bf16[4,48,2048]{2,1,0:T(8,128)(2,1)S(1)} collective-permute-done((bf16[4,48,2048]{2,1,0:T(8,128)(2,1)}, bf16[4,48,2048]{2,1,0:T(8,128)(2,1)S(1)}, u32[]{:S(2)}, u32[]{:S(2)}) %collective-permute-start.81) | collective-permute-done | bytes 786464 | tf_op jit(solution)/shard_map/ppermute | solution.py:383
  568.5 16.1 %collective-permute-done.77 = bf16[4,48,2048]{2,1,0:T(8,128)(2,1)S(1)} collective-permute-done((bf16[4,48,2048]{2,1,0:T(8,128)(2,1)S(1)}, bf16[4,48,2048]{2,1,0:T(8,128)(2,1)S(1)}, u32[]{:S(2)}, u32[]{:S(2)}) %collective-permute-start.77) | collective-permute-done | bytes 786464 | tf_op jit(solution)/shard_map/ppermute | solution.py:383
  (786 shorter events, 345.8 us)
Async XLA Ops:
  7.2 178.7 %all-gather.7.cloned.1.call-start = ((), (), s32[]{:S(2)}) async-start(), calls=%async_computation.5 | async-start | bytes 1966080 | tf_op jit(solution)/shard_map/all_gather | solution.py:438
  13.6 22.9 %collective-permute-start.12 = (bf16[1,48,2048]{2,1,0:T(8,128)(2,1)}, bf16[1,48,2048]{2,1,0:T(8,128)(2,1)S(1)}, u32[]{:S(2)}, u32[]{:S(2)}) collective-permute-start(bf16[1,48,2048]{2,1,0:T(8,128)(2,1)} %get-tuple-element.182), channel_id=1, source_target_pairs={{0,1},{1,0},{2,3},{3,2},{4,5},{5,4},{6,7},{7,6},{8,9},{9,8},{10,11... | collective-permute-start | bytes 589832 | tf_op jit(solution)/shard_map/ppermute | solution.py:383
  14.1 22.5 %collective-permute-start.13 = (bf16[1,48,2048]{2,1,0:T(8,128)(2,1)}, bf16[1,48,2048]{2,1,0:T(8,128)(2,1)S(1)}, u32[]{:S(2)}, u32[]{:S(2)}) collective-permute-start(bf16[1,48,2048]{2,1,0:T(8,128)(2,1)} %get-tuple-element.181), channel_id=1, source_target_pairs={{0,2},{1,3},{2,0},{3,1},{4,6},{5,7},{6,4},{7,5},{8,10},{9,11},{10,... | collective-permute-start | bytes 589832 | tf_op jit(solution)/shard_map/ppermute | solution.py:383
  31.6 154.3 %all-gather.5.cloned.1.call-start = ((), (), s32[]{:S(2)}) async-start(), calls=%async_computation.4 | async-start | bytes 3932160 | tf_op jit(solution)/shard_map/all_gather | solution.py:438
  37.6 209.9 %all-gather.11.cloned.1.call-start = ((), (), s32[]{:S(2)}) async-start(), calls=%async_computation.7 | async-start | bytes 1966080 | tf_op jit(solution)/shard_map/all_gather | solution.py:438
  37.8 25.5 %collective-permute-start = (bf16[112,768]{1,0:T(8,128)(2,1)S(1)}, bf16[112,768]{1,0:T(8,128)(2,1)S(1)}, u32[]{:S(2)}, u32[]{:S(2)}) collective-permute-start(bf16[112,768]{1,0:T(8,128)(2,1)S(1)} %pad_maximum_fusion.13), channel_id=1, source_target_pairs={{0,4},{1,5},{2,6},{3,7},{4,8},{5,9},{6,10},{7,11},{8,12},{9,13},{1... | collective-permute-start | bytes 516104 | tf_op jit(solution)/shard_map/ppermute | solution.py:383
  39.6 26.0 %collective-permute-start.1 = (bf16[112,768]{1,0:T(8,128)(2,1)S(1)}, bf16[112,768]{1,0:T(8,128)(2,1)S(1)}, u32[]{:S(2)}, u32[]{:S(2)}) collective-permute-start(bf16[112,768]{1,0:T(8,128)(2,1)S(1)} %pad_maximum_fusion.13), channel_id=1, source_target_pairs={{0,8},{1,9},{2,10},{3,11},{4,12},{5,13},{6,14},{7,15},{8,0},{9,1},... | collective-permute-start | bytes 516104 | tf_op jit(solution)/shard_map/ppermute | solution.py:383
  42.2 24.1 %collective-permute-start.2 = (bf16[112,768]{1,0:T(8,128)(2,1)S(1)}, bf16[112,768]{1,0:T(8,128)(2,1)S(1)}, u32[]{:S(2)}, u32[]{:S(2)}) collective-permute-start(bf16[112,768]{1,0:T(8,128)(2,1)S(1)} %pad_maximum_fusion.13), channel_id=1, source_target_pairs={{0,12},{1,13},{2,14},{3,15},{4,0},{5,1},{6,2},{7,3},{8,4},{9,5},{1... | collective-permute-start | bytes 516104 | tf_op jit(solution)/shard_map/ppermute | solution.py:383
  45.0 62.3 %collective-permute-start.20 = (bf16[96,768]{1,0:T(8,128)(2,1)}, bf16[96,768]{1,0:T(8,128)(2,1)}, u32[]{:S(2)}, u32[]{:S(2)}) collective-permute-start(bf16[96,768]{1,0:T(8,128)(2,1)} %bitcast.52), channel_id=1, source_target_pairs={{0,4},{1,5},{2,6},{3,7},{4,8},{5,9},{6,10},{7,11},{8,12},{9,13},{1... | collective-permute-start | bytes 442376 | tf_op jit(solution)/shard_map/ppermute | solution.py:383
  45.7 62.5 %collective-permute-start.21 = (bf16[96,768]{1,0:T(8,128)(2,1)}, bf16[96,768]{1,0:T(8,128)(2,1)}, u32[]{:S(2)}, u32[]{:S(2)}) collective-permute-start(bf16[96,768]{1,0:T(8,128)(2,1)} %bitcast.52), channel_id=1, source_target_pairs={{0,8},{1,9},{2,10},{3,11},{4,12},{5,13},{6,14},{7,15},{8,0},{9,1},... | collective-permute-start | bytes 442376 | tf_op jit(solution)/shard_map/ppermute | solution.py:383
  66.9 25.9 %collective-permute-start.3 = (bf16[4,112,768]{2,1,0:T(8,128)(2,1)}, bf16[4,112,768]{2,1,0:T(8,128)(2,1)}, u32[]{:S(2)}, u32[]{:S(2)}) collective-permute-start(bf16[4,112,768]{2,1,0:T(8,128)(2,1)} %bitcast_dynamic-update-slice_fusion.24), channel_id=1, source_target_pairs={{0,2},{1,3},{2,0},{3,1},{4,6},{5,7},{6,4},{7,5},{8,10},{9,11},{10,... | collective-permute-start | bytes 2064392 | tf_op jit(solution)/shard_map/ppermute | solution.py:383
  67.4 23.9 %collective-permute-start.4 = (bf16[4,112,768]{2,1,0:T(8,128)(2,1)}, bf16[4,112,768]{2,1,0:T(8,128)(2,1)}, u32[]{:S(2)}, u32[]{:S(2)}) collective-permute-start(bf16[4,112,768]{2,1,0:T(8,128)(2,1)} %bitcast_dynamic-update-slice_fusion.24), channel_id=1, source_target_pairs={{0,16},{1,17},{2,18},{3,19},{4,20},{5,21},{6,22},{7,23},{8,24},{9,... | collective-permute-start | bytes 2064392 | tf_op jit(solution)/shard_map/ppermute | solution.py:383
  75.8 33.9 %collective-permute-start.22 = (bf16[96,768]{1,0:T(8,128)(2,1)}, bf16[96,768]{1,0:T(8,128)(2,1)}, u32[]{:S(2)}, u32[]{:S(2)}) collective-permute-start(bf16[96,768]{1,0:T(8,128)(2,1)} %bitcast.52), channel_id=1, source_target_pairs={{0,12},{1,13},{2,14},{3,15},{4,0},{5,1},{6,2},{7,3},{8,4},{9,5},{1... | collective-permute-start | bytes 442376 | tf_op jit(solution)/shard_map/ppermute | solution.py:383
  91.2 170.0 %all-gather.9.cloned.1.call-start = ((), (), s32[]{:S(2)}) async-start(), calls=%async_computation.6 | async-start | bytes 3932160 | tf_op jit(solution)/shard_map/all_gather | solution.py:438
  107.3 37.8 %collective-permute-start.7 = (bf16[2,4,2,1,112,768]{5,4,3,2,1,0:T(8,128)(2,1)}, bf16[2,4,2,1,112,768]{5,4,3,2,1,0:T(8,128)(2,1)}, u32[]{:S(2)}, u32[]{:S(2)}) collective-permute-start(bf16[2,4,2,1,112,768]{5,4,3,2,1,0:T(8,128)(2,1)} %constant_dynamic-slice_fusion.21), channel_id=1, source_target_pairs={{0,1},{1,0},{2,3},{3,2},{4,5},{5,4},{6,7},{7,6},{8,9},{9,8},{10,11... | collective-permute-start | bytes 8257544 | tf_op jit(solution)/shard_map/ppermute | solution.py:383
  117.5 283.9 %reduce-scatter.11.cloned.1.call-start = ((), (), s32[]{:S(2)}) async-start(), calls=%async_computation.11 | async-start | bytes 1966080 | tf_op jit(solution)/shard_map/reduce_scatter | solution.py:443
  145.0 53.1 %collective-permute-start.27 = (bf16[2,4,2,1,96,768]{5,4,3,2,1,0:T(8,128)(2,1)}, bf16[2,4,2,1,96,768]{5,4,3,2,1,0:T(8,128)(2,1)}, u32[]{:S(2)}, u32[]{:S(2)}) collective-permute-start(bf16[2,4,2,1,96,768]{5,4,3,2,1,0:T(8,128)(2,1)} %constant_dynamic-slice_fusion.17), channel_id=1, source_target_pairs={{0,1},{1,0},{2,3},{3,2},{4,5},{5,4},{6,7},{7,6},{8,9},{9,8},{10,11... | collective-permute-start | bytes 7077896 | tf_op jit(solution)/shard_map/ppermute | solution.py:383
  247.2 25.2 %collective-permute-start.43 = (bf16[4,80,768]{2,1,0:T(8,128)(2,1)S(1)}, bf16[4,80,768]{2,1,0:T(8,128)(2,1)S(1)}, u32[]{:S(2)}, u32[]{:S(2)}) collective-permute-start(bf16[4,80,768]{2,1,0:T(8,128)(2,1)S(1)} %pad_maximum_fusion.9), channel_id=1, source_target_pairs={{0,1},{1,0},{2,3},{3,2},{4,5},{5,4},{6,7},{7,6},{8,9},{9,8},{10,11... | collective-permute-start | bytes 1474568 | tf_op jit(solution)/shard_map/ppermute | solution.py:383
  277.6 143.9 %reduce-scatter.9.cloned.1.call-start = ((), (), s32[]{:S(2)}) async-start(), calls=%async_computation.10 | async-start | bytes 1966080 | tf_op jit(solution)/shard_map/reduce_scatter | solution.py:443
  335.7 196.7 %reduce-scatter.7.cloned.1.call-start = ((), (), s32[]{:S(2)}) async-start(), calls=%async_computation.9 | async-start | bytes 3932160 | tf_op jit(solution)/shard_map/reduce_scatter | solution.py:443
  341.5 202.9 %reduce-scatter.5.cloned.1.call-start = ((), (), s32[]{:S(2)}) async-start(), calls=%async_computation.8 | async-start | bytes 3932160 | tf_op jit(solution)/shard_map/reduce_scatter | solution.py:443
  398.8 31.3 %collective-permute-start.65 = (bf16[2,4,2,112,768]{4,3,2,1,0:T(8,128)(2,1)}, bf16[2,4,2,112,768]{4,3,2,1,0:T(8,128)(2,1)}, u32[]{:S(2)}, u32[]{:S(2)}) collective-permute-start(bf16[2,4,2,112,768]{4,3,2,1,0:T(8,128)(2,1)} %pad_maximum_fusion.3), channel_id=1, source_target_pairs={{0,1},{1,0},{2,3},{3,2},{4,5},{5,4},{6,7},{7,6},{8,9},{9,8},{10,11... | collective-permute-start | bytes 8257544 | tf_op jit(solution)/shard_map/ppermute | solution.py:383
  400.9 34.5 %collective-permute-start.56 = (bf16[2,4,2,112,768]{4,3,2,1,0:T(8,128)(2,1)}, bf16[2,4,2,112,768]{4,3,2,1,0:T(8,128)(2,1)}, u32[]{:S(2)}, u32[]{:S(2)}) collective-permute-start(bf16[2,4,2,112,768]{4,3,2,1,0:T(8,128)(2,1)} %pad_maximum_fusion.2), channel_id=1, source_target_pairs={{0,1},{1,0},{2,3},{3,2},{4,5},{5,4},{6,7},{7,6},{8,9},{9,8},{10,11... | collective-permute-start | bytes 8257544 | tf_op jit(solution)/shard_map/ppermute | solution.py:383
  438.2 27.9 %collective-permute-start.57 = (bf16[2,2,1,112,768]{4,3,1,2,0:T(8,128)(2,1)S(1)}, bf16[2,2,1,112,768]{4,3,1,2,0:T(8,128)(2,1)S(1)}, u32[]{:S(2)}, u32[]{:S(2)}) collective-permute-start(bf16[2,2,1,112,768]{4,3,1,2,0:T(8,128)(2,1)S(1)} %dynamic-slice_bitcast_fusion.3), channel_id=1, source_target_pairs={{0,2},{1,3},{2,0},{3,1},{4,6},{5,7},{6,4},{7,5},{8,10},{9,11},{10,... | collective-permute-start | bytes 2064392 | tf_op jit(solution)/shard_map/ppermute | solution.py:383
  438.9 31.4 %collective-permute-start.59 = (bf16[2,2,112,768]{3,2,1,0:T(8,128)(2,1)S(1)}, bf16[2,2,112,768]{3,2,1,0:T(8,128)(2,1)S(1)}, u32[]{:S(2)}, u32[]{:S(2)}) collective-permute-start(bf16[2,2,112,768]{3,2,1,0:T(8,128)(2,1)S(1)} %dynamic-slice_bitcast_fusion.2), channel_id=1, source_target_pairs={{0,16},{1,17},{2,18},{3,19},{4,20},{5,21},{6,22},{7,23},{8,24},{9,... | collective-permute-start | bytes 2064392 | tf_op jit(solution)/shard_map/ppermute | solution.py:383
  451.6 26.1 %collective-permute-start.67 = (bf16[2,112,768]{2,1,0:T(8,128)(2,1)S(1)}, bf16[2,112,768]{2,1,0:T(8,128)(2,1)S(1)}, u32[]{:S(2)}, u32[]{:S(2)}) collective-permute-start(bf16[2,112,768]{2,1,0:T(8,128)(2,1)S(1)} %dynamic-slice_bitcast_fusion.4), channel_id=1, source_target_pairs={{0,16},{1,17},{2,18},{3,19},{4,20},{5,21},{6,22},{7,23},{8,24},{9,... | collective-permute-start | bytes 1032200 | tf_op jit(solution)/shard_map/ppermute | solution.py:383
  479.4 31.7 %collective-permute-start.71 = (bf16[112,768]{1,0:T(8,128)(2,1)S(1)}, bf16[112,768]{1,0:T(8,128)(2,1)S(1)}, u32[]{:S(2)}, u32[]{:S(2)}) collective-permute-start(bf16[112,768]{1,0:T(8,128)(2,1)S(1)} %get-tuple-element.196), channel_id=1, source_target_pairs={{0,8},{1,9},{2,10},{3,11},{4,12},{5,13},{6,14},{7,15},{8,0},{9,1},... | collective-permute-start | bytes 516104 | tf_op jit(solution)/shard_map/ppermute | solution.py:383
  479.4 31.6 %collective-permute-start.70 = (bf16[112,768]{1,0:T(8,128)(2,1)S(1)}, bf16[112,768]{1,0:T(8,128)(2,1)S(1)}, u32[]{:S(2)}, u32[]{:S(2)}) collective-permute-start(bf16[112,768]{1,0:T(8,128)(2,1)S(1)} %get-tuple-element.195), channel_id=1, source_target_pairs={{0,4},{1,5},{2,6},{3,7},{4,8},{5,9},{6,10},{7,11},{8,12},{9,13},{1... | collective-permute-start | bytes 516104 | tf_op jit(solution)/shard_map/ppermute | solution.py:383
  482.6 30.1 %collective-permute-start.63 = (bf16[112,768]{1,0:T(8,128)(2,1)S(1)}, bf16[112,768]{1,0:T(8,128)(2,1)S(1)}, u32[]{:S(2)}, u32[]{:S(2)}) collective-permute-start(bf16[112,768]{1,0:T(8,128)(2,1)S(1)} %get-tuple-element.194), channel_id=1, source_target_pairs={{0,12},{1,13},{2,14},{3,15},{4,0},{5,1},{6,2},{7,3},{8,4},{9,5},{1... | collective-permute-start | bytes 516104 | tf_op jit(solution)/shard_map/ppermute | solution.py:383
  483.9 38.5 %collective-permute-start.62 = (bf16[112,768]{1,0:T(8,128)(2,1)S(1)}, bf16[112,768]{1,0:T(8,128)(2,1)S(1)}, u32[]{:S(2)}, u32[]{:S(2)}) collective-permute-start(bf16[112,768]{1,0:T(8,128)(2,1)S(1)} %get-tuple-element.193), channel_id=1, source_target_pairs={{0,8},{1,9},{2,10},{3,11},{4,12},{5,13},{6,14},{7,15},{8,0},{9,1},... | collective-permute-start | bytes 516104 | tf_op jit(solution)/shard_map/ppermute | solution.py:383
  494.0 28.3 %collective-permute-start.61 = (bf16[112,768]{1,0:T(8,128)(2,1)S(1)}, bf16[112,768]{1,0:T(8,128)(2,1)S(1)}, u32[]{:S(2)}, u32[]{:S(2)}) collective-permute-start(bf16[112,768]{1,0:T(8,128)(2,1)S(1)} %get-tuple-element.192), channel_id=1, source_target_pairs={{0,4},{1,5},{2,6},{3,7},{4,8},{5,9},{6,10},{7,11},{8,12},{9,13},{1... | collective-permute-start | bytes 516104 | tf_op jit(solution)/shard_map/ppermute | solution.py:383
  559.3 25.3 %collective-permute-start.77 = (bf16[4,48,2048]{2,1,0:T(8,128)(2,1)S(1)}, bf16[4,48,2048]{2,1,0:T(8,128)(2,1)S(1)}, u32[]{:S(2)}, u32[]{:S(2)}) collective-permute-start(bf16[4,48,2048]{2,1,0:T(8,128)(2,1)S(1)} %constant_dynamic-update-slice_fusion.24), channel_id=1, source_target_pairs={{0,16},{1,17},{2,18},{3,19},{4,20},{5,21},{6,22},{7,23},{8,24},{9,... | collective-permute-start | bytes 2359304 | tf_op jit(solution)/shard_map/ppermute | solution.py:383
  (216 other events, 2484.5 us)
Sparse Core Ops, SparseCore 0:
  31.7 60.3 all-gather.6
  94.2 65.7 all-gather.4
  161.6 35.7 all-gather.10
  198.8 62.3 all-gather.8
  277.7 33.9 reduce-scatter.10
  335.8 33.0 reduce-scatter.8
  371.2 59.2 reduce-scatter.6
  433.3 74.2 reduce-scatter.4

commit v3 on v2

--- a/solution.py
+++ b/solution.py
@@ -365,6 +365,10 @@
     )(*args)
 
 
+def after(x, *others):
+    return lax.optimization_barrier((x,) + others)[0]
+
+
 class Layout:
     def __init__(self, mesh):
         self.reps, self.shards = mesh.shape["rep"], mesh.shape["shard"]
@@ -444,23 +448,13 @@
             x, "shard", scatter_dimension=0, tiled=True, axis_index_groups=self.line_groups()
         )
 
-    def dense_gather(self, x, rep, j):
-        z = lax.axis_index("shard") // EF
+    def dense_gather(self, x):
         reps, lines = self.reps, self.lines
-        line = lax.dynamic_update_slice_in_dim(
-            jnp.zeros((lines,) + x.shape, x.dtype), x[None], z, 0
-        )
+        line = [x[None]]
         for shift in range(1, lines):
-            block = self.send(x, lambda r, q, k: (r, (q + shift) % lines, k))
-            line = lax.dynamic_update_slice_in_dim(
-                line, block[None], (z + lines - shift) % lines, 0
-            )
+            line.append(self.send(x, lambda r, q, k: (r, (q + shift) % lines, k))[None])
+        line = jnp.concatenate(line)
         cut = lines // 2
-        high, core = j // 2, j % 2
-        full = jnp.zeros((reps, lines, 2, 2) + x.shape, x.dtype)
-
-        def put(full, block, r, at, hi, lo):
-            return lax.dynamic_update_slice(full, block[None, :, None, None], (r, at, hi, lo, 0, 0))
 
         def over_rep(block, shift):
             return self.send(block, lambda r, q, k: ((r + shift) % reps, q, k))
@@ -468,48 +462,85 @@
         def over_high(block):
             return self.send(block, lambda r, q, k: (r, q, k ^ 2))
 
-        sides = [(shift, over_rep(line, shift)) for shift in range(1, reps)]
+        sides = [over_rep(line, shift) for shift in range(1, reps)]
         flip = over_high(line)
-        full = put(full, line, rep, 0, high, core)
-        full = put(full, flip, rep, 0, 1 - high, core)
-        for shift, block in sides:
-            source = (rep + reps - shift) % reps
-            full = put(full, block, source, 0, high, core)
-            full = put(full, over_high(block[:cut]), source, 0, 1 - high, core)
-            full = put(full, over_rep(flip[cut:], shift), source, cut, 1 - high, core)
-        half = lax.dynamic_slice_in_dim(full, core, 1, 3)
-        half = self.send(half, lambda r, q, k: (r, q, k ^ 1))
-        return lax.dynamic_update_slice_in_dim(full, half, 1 - core, 3)
-
-    def dense_sum(self, parts, rep, j):
-        z = lax.axis_index("shard") // EF
+        pieces = [(line, 0, 0, 0), (flip, 0, 0, 1)]
+        for shift, block in enumerate(sides, 1):
+            pieces.append((block, 0, shift, 0))
+            pieces.append((over_high(block[:cut]), 0, shift, 1))
+            pieces.append((over_rep(flip[cut:], shift), cut, shift, 1))
+        pieces = [piece + (0,) for piece in pieces if piece[0].shape[0]]
+        others = [
+            (self.send(piece[0], lambda r, q, k: (r, q, k ^ 1)),) + piece[1:4] + (1,)
+            for piece in pieces
+        ]
+        return pieces + others
+
+    def assemble(self, pieces, where, count):
         reps, lines = self.reps, self.lines
-        high, core = j // 2, j % 2
-
-        def over_rep(block, shift):
-            return self.send(block, lambda r, q, k: ((r + shift) % reps, q, k))
-
-        def over_high(block):
-            return self.send(block, lambda r, q, k: (r, q, k ^ 2))
+        rows, features = pieces[0][0].shape[1:]
+        slim = features // self.shards
+        extra = rows - count * slim
+        notes = [piece[1:] for piece in pieces]
+
+        def kernel(where_ref, *refs):
+            out = refs[len(pieces)]
+            rep, z, high, core = [where_ref[k] for k in range(4)]
+            for ref, (start, back, flip, other) in zip(refs, notes):
+                r = lax.rem(rep + reps - back, reps)
+                hi = high if flip == 0 else 1 - high
+                lo = core if other == 0 else 1 - core
+                for step in range(ref.shape[0]):
+                    at = lax.rem(z + lines - start - step, lines)
+                    for k in range(count):
+                        out[r, k, at, hi, lo] = ref[step, k * slim : (k + 1) * slim]
+                    if extra and back == 0:
+                        refs[-1][at, hi, lo] = ref[step, count * slim :]
+
+        shapes = [jax.ShapeDtypeStruct((reps, count, lines, 2, 2, slim, features), BF16)]
+        if extra:
+            shapes.append(jax.ShapeDtypeStruct((lines, 2, 2, extra, features), BF16))
+        return pl.pallas_call(
+            kernel,
+            out_shape=shapes,
+            in_specs=[pl.BlockSpec(memory_space=pltpu.SMEM)]
+            + [pl.BlockSpec(memory_space=pltpu.VMEM)] * len(pieces),
+            out_specs=[pl.BlockSpec(memory_space=pltpu.VMEM)] * len(shapes),
+            compiler_params=pltpu.CompilerParams(vmem_limit_bytes=32 * 1024 * 1024),
+        )(where, *[piece[0] for piece in pieces])
+
+    def over_rep(self, block, shift):
+        return self.send(block, lambda r, q, k: ((r + shift) % self.reps, q, k))
+
+    def sum_core(self, parts, j):
+        core = j % 2
+        other = self.send(parts(1 - core), lambda r, q, k: (r, q, k ^ 1))
+        return (parts(core).astype(F32) + other.astype(F32)).astype(BF16)
+
+    def sum_cross(self, both, rep, j):
+        high = j // 2
 
         def rep_step(x):
             total = lax.dynamic_slice_in_dim(x, rep, 1, 0)[0].astype(F32)
-            for shift in range(1, reps):
-                block = lax.dynamic_slice_in_dim(x, (rep + shift) % reps, 1, 0)[0]
-                total = total + over_rep(block, shift).astype(F32)
+            for shift in range(1, self.reps):
+                block = lax.dynamic_slice_in_dim(x, (rep + shift) % self.reps, 1, 0)[0]
+                total = total + self.over_rep(block, shift).astype(F32)
             return total.astype(BF16)
 
         def high_step(x, axis):
             mine = lax.dynamic_slice_in_dim(x, high, 1, axis)
-            other = over_high(lax.dynamic_slice_in_dim(x, 1 - high, 1, axis))
+            other = lax.dynamic_slice_in_dim(x, 1 - high, 1, axis)
+            other = self.send(other, lambda r, q, k: (r, q, k ^ 2))
             return jnp.squeeze(mine.astype(F32) + other.astype(F32), axis).astype(BF16)
 
-        other = self.send(parts(1 - core), lambda r, q, k: (r, q, k ^ 1))
-        both = (parts(core).astype(F32) + other.astype(F32)).astype(BF16)
-        cut = lines // 2
+        cut = self.lines // 2
         first = rep_step(high_step(both[:, :cut], 2))
         second = high_step(rep_step(both[:, cut:]), 1)
-        line = jnp.concatenate([first, second])
+        return jnp.concatenate([first, second])
+
+    def sum_line(self, line, rep):
+        z = lax.axis_index("shard") // EF
+        lines = self.lines
         total = lax.dynamic_slice_in_dim(line, z, 1, 0)[0].astype(F32)
         for shift in range(1, lines):
             block = lax.dynamic_slice_in_dim(line, (z + shift) % lines, 1, 0)[0]
@@ -536,36 +567,88 @@
         )
 
 
-def split_columns(array, layout):
-    width = array.shape[-1] // (2 * layout.shards)
-    return array.reshape(array.shape[:-1] + (2, layout.shards // layout.reps, layout.reps, width))
-
-
-def expert_weights(layout, w_gate_up, w_down, rep, j):
-    features = w_gate_up.shape[1]
-    blocks = split_columns(w_gate_up, layout)
-    blocks = jnp.transpose(blocks, (0, 4, 1, 2, 3, 5)).reshape(EF * layout.reps, features, -1)
-    mine = lax.dynamic_slice_in_dim(blocks, rep * EF, EF, 0)
-    mine = layout.quad_exchange(mine, j).reshape(EF * features, -1)
-    gate_up = layout.line_gather(mine)
+def split_gate_up(layout, w_gate_up, layer, where):
+    _, experts, rows, columns = w_gate_up.shape
+    width = columns // (2 * layout.shards)
+    parts = layout.reps
+    per = layout.shards // parts
+
+    def kernel(where_ref, x, o):
+        for j in range(EF):
+            e = where_ref[0] * (EF // layout.reps) + j // parts
+            for b in range(2 * per):
+                at = (b * parts + j % parts) * width
+                o[j, :, b * width : (b + 1) * width] = x[0, e, :, at : at + width]
+
+    return pl.pallas_call(
+        kernel,
+        grid=(1,),
+        out_shape=jax.ShapeDtypeStruct((EF, rows, columns // parts), BF16),
+        in_specs=[
+            pl.BlockSpec(memory_space=pltpu.SMEM),
+            pl.BlockSpec((1, experts, rows, columns), lambda _: (layer, 0, 0, 0)),
+        ],
+        out_specs=pl.BlockSpec((EF, rows, columns // parts), lambda _: (0, 0, 0)),
+        compiler_params=pltpu.CompilerParams(vmem_limit_bytes=32 * 1024 * 1024),
+    )(where, w_gate_up)
+
+
+def expert_weights(layout, w_gate_up, w_down, layer, rep, j, where):
     count = EF // layout.reps
-    down = lax.dynamic_slice_in_dim(w_down, rep * count, count, 0)
-    down = layout.part_exchange(down, j).reshape(count * w_down.shape[1], -1)
-    return gate_up, layout.line_gather(down)
-
-
-def expert_grads(layout, grad_gate_up, grad_down, rep, j):
-    down = layout.line_sum(grad_down)
-    count = EF // layout.reps
-    down = layout.part_exchange(down.reshape(count, -1, down.shape[-1]), j)
-    down = layout.rep_gather(down, rep).reshape((EF,) + down.shape[1:]).astype(F32)
-    mine = layout.line_sum(grad_gate_up)
+    mine = layout.quad_exchange(split_gate_up(layout, w_gate_up, layer, where), j)
+    mine = mine.reshape(-1, mine.shape[-1])
+    down = lax.dynamic_slice_in_dim(after(w_down[layer], mine), rep * count, count, 0)
+    down = layout.part_exchange(down, j)
+    down = down.reshape(-1, down.shape[-1])
+    return layout.line_gather(mine), layout.line_gather(down), down
+
+
+def place_down(layout, down, rep, j):
+    down = layout.part_exchange(down.reshape(EF // layout.reps, -1, down.shape[-1]), j)
+    return layout.rep_gather(down, rep).reshape((1, EF) + down.shape[1:])
+
+
+def place_gate_up(layout, mine, rep, j):
     mine = layout.quad_exchange(mine.reshape(EF, -1, mine.shape[-1]), j)
-    full = layout.rep_gather(mine, rep)
-    features = mine.shape[1]
-    full = full.reshape(EF, layout.reps, features, 2, layout.shards // layout.reps, -1)
-    full = jnp.transpose(full, (0, 2, 3, 4, 1, 5)).reshape(EF, features, -1)
-    return full.astype(F32), down
+    return layout.rep_gather(mine, rep).reshape((EF, layout.reps) + mine.shape[1:])
+
+
+def store_layer(kernel, source, block, index, shape, layer, held):
+    spec = pl.BlockSpec((1, 1) + shape[2:], lambda e: (layer, e) + (0,) * (len(shape) - 2))
+    whole = [] if held is None else [held]
+    return pl.pallas_call(
+        (lambda x, o: kernel(x, o)) if held is None else (lambda x, h, o: kernel(x, o)),
+        grid=(shape[1],),
+        out_shape=jax.ShapeDtypeStruct(shape, F32),
+        in_specs=[pl.BlockSpec(block, index)] + [pl.BlockSpec(memory_space=pl.ANY)] * len(whole),
+        out_specs=spec,
+        input_output_aliases={} if held is None else {1: 0},
+        compiler_params=pltpu.CompilerParams(vmem_limit_bytes=32 * 1024 * 1024),
+    )(source, *whole)
+
+
+def store_gate_up(layout, source, shape, layer, held):
+    width = shape[3] // (2 * layout.shards)
+    per = layout.shards // layout.reps
+
+    def kernel(x, o):
+        for half in range(2):
+            for b in range(per):
+                for f in range(layout.reps):
+                    start = ((half * per + b) * layout.reps + f) * width
+                    at = (half * per + b) * width
+                    o[0, 0, :, start : start + width] = x[0, f, :, at : at + width].astype(F32)
+
+    block = (1,) + source.shape[1:]
+    return store_layer(kernel, source, block, lambda e: (e, 0, 0, 0), shape, layer, held)
+
+
+def store_down(source, shape, layer, held):
+    def kernel(x, o):
+        o[...] = x[...].astype(F32)
+
+    block = (1, 1) + source.shape[2:]
+    return store_layer(kernel, source, block, lambda e: (0, e, 0, 0), shape, layer, held)
 
 
 def place_pairs(routes, priority, expert):
@@ -651,30 +734,37 @@
     extra = ROWS * features
     small = jnp.pad(small, ((0, 0), (0, extra - small.shape[1]))).reshape(ROWS, features)
     count = EF // layout.reps
-    dense, moe = [], []
-    small_full = None
-    for l in range(layers):
+    shard = lax.axis_index("shard")
+    where = jnp.stack([rep, shard // EF, j // 2, j % 2]).astype(jnp.int32)
+
+    group = rep.reshape(1).astype(jnp.int32)
+
+    def share(l, *more):
         blocks = jnp.concatenate(
             [jnp.transpose(w_qkv[l].reshape(slim, 3, features), (1, 0, 2)), w_out[l][None]]
         )
-        mine = lax.dynamic_slice_in_dim(blocks, rep * count, count, 0).reshape(count * slim, features)
-        if l == 0:
-            mine = jnp.concatenate([mine, small])
-        full = layout.dense_gather(mine, rep, j)
-        if l == 0:
-            small_full = full[0, :, :, :, count * slim :].reshape(layout.shards, -1)
-        full = full[:, :, :, :, : count * slim].reshape(
-            layout.reps, layout.shards, count, slim, features
-        )
-        dense.append(jnp.transpose(full, (0, 2, 1, 3, 4)).reshape(4, features, features))
-        moe.append(expert_weights(layout, w_gate_up[l], w_down[l], rep, j))
+        mine = lax.dynamic_slice_in_dim(blocks, rep * count, count, 0)
+        return jnp.concatenate([mine.reshape(count * slim, features), *more])
+
+    def dense_weights(x):
+        full = layout.assemble(layout.dense_gather(x), where, count)
+        return full[0].reshape(4, features, features), *full[1:]
+
+    full, small_full = dense_weights(share(0, small))
+    small_full = small_full.reshape(layout.shards, -1)
+    dense, moe = [full], []
+    raw = w_gate_up
+    for l in range(layers):
+        *found, last = expert_weights(layout, raw, w_down, l, rep, j, group)
+        moe.append(found)
+        raw = after(raw, last)
     packs, vectors, mixing_t = [], [], []
     for l in range(layers):
         part = small_full[:, l * slim * SMALL : (l + 1) * slim * SMALL]
         part = part.reshape(features, SMALL)
         mixing = part[:, 2 : SMALL - NCONST]
         mixing = jnp.pad(mixing, ((0, 0), (0, LANES - mixing.shape[1])))
-        packs.append((part[:, :2].T.astype(F32), dense[l], mixing))
+        packs.append([part[:, :2].T.astype(F32), None, mixing])
         mixing_t.append(mixing.T)
         vectors.append(part[:, SMALL - NCONST :].T.astype(F32))
 
@@ -686,8 +776,11 @@
     kept = []
     for l in range(layers):
         gather, scatter = pairs[l]
+        packs[l][1] = dense[l]
         state = attention_forward(shared, packs[l], hidden, previous, routes[l], gather)
         normed, query, keys, values, log_total, attended, middle, low, logits, coefs, rows = state
+        if l + 1 < layers:
+            dense.append(dense_weights(after(share(l + 1), rows))[0])
         inputs = layout.dispatch(rows)
         gate_up, activated, own, others = expert_forward(layout, inputs, *moe[l])
         outputs = layout.collect(own, others)
@@ -701,7 +794,23 @@
 
     grad_hidden = grad_out
     grad_gate = jnp.zeros_like(previous)
-    dense_grads, moe_grads = [None] * layers, [None] * layers
+    dense_grads = [None] * layers
+    waiting = None
+    gate_up_out, down_out = None, None
+
+    def store(wide, down, l, gate_up_out, down_out):
+        down_out = store_down(
+            place_down(layout, down, rep, j), (layers, EF) + w_down.shape[2:], l, down_out
+        )
+        gate_up_out = store_gate_up(
+            layout,
+            place_gate_up(layout, wide, rep, j),
+            (layers, EF) + w_gate_up.shape[2:],
+            l,
+            gate_up_out,
+        )
+        return gate_up_out, down_out
+
     for l in reversed(range(layers)):
         gather, scatter = pairs[l]
         source, state, inputs, gate_up, activated, outputs = kept[l]
@@ -718,11 +827,21 @@
             (coefs, middle, packs[l][0], scatter, outputs, vectors[l], routes[l], low)
             + (mixing_t[l], grad_hidden, grad_gate),
         )
-        grad_down = dot(activated, d_expert, ((0,), (0,))).astype(BF16)
+        if waiting is not None:
+            d_expert, waiting = lax.optimization_barrier((d_expert, waiting))
+            waiting = layout.sum_cross(waiting, rep, j)
+        if l > 0:
+            grad_down = dot(activated, d_expert, ((0,), (0,))).astype(BF16)
         d_gate_up, own, others = expert_backward(layout, d_expert, *moe[l], gate_up)
         d_rows = layout.collect(own, others)
         grad_gate_up = dot(inputs, d_gate_up, ((0,), (0,))).astype(BF16)
-        moe_grads[l] = expert_grads(layout, grad_gate_up, grad_down, rep, j)
+        wide = layout.line_sum(grad_gate_up)
+        if l > 0:
+            down = layout.line_sum(grad_down)
+            gate_up_out, down_out = store(wide, down, l, gate_up_out, down_out)
+        if waiting is not None:
+            d_rows, waiting = lax.optimization_barrier((d_rows, waiting))
+            dense_grads[l + 1] = layout.sum_line(waiting, rep)
         grad_hidden, d_branch, d_projected, gain_grads = call(
             attention_backward_kernel,
             [((tokens, features), F32), ((tokens, features), BF16)]
@@ -731,6 +850,10 @@
             + (packs[l][0], packs[l][1], *shared, query, keys, values, log_total),
             [((tokens, tokens), F32), ((tokens, features), BF16), ((tokens, features), F32)],
         )
+        if l == 0:
+            activated = after(activated, d_branch)
+            grad_down = dot(activated, d_expert, ((0,), (0,))).astype(BF16)
+            down = layout.line_sum(grad_down)
         grad_dense = jnp.stack(
             [dot(normed, d_projected[b], ((0,), (0,))).astype(BF16) for b in range(3)]
             + [dot(attended, d_branch, ((0,), (0,))).astype(BF16)]
@@ -752,8 +875,12 @@
             extra = jnp.broadcast_to(extra[None], (layout.reps,) + extra.shape)
             return jnp.concatenate([chosen, extra], axis=3)
 
-        dense_grads[l] = layout.dense_sum(parts, rep, j)
-
+        waiting = layout.sum_core(parts, j)
+
+    waiting = layout.sum_cross(waiting, rep, j)
+    waiting, gate_up_out, down_out = lax.optimization_barrier((waiting, gate_up_out, down_out))
+    dense_grads[0] = layout.sum_line(waiting, rep)
+    gate_up_out, down_out = store(wide, down, 0, gate_up_out, down_out)
     dense_all = jnp.stack(dense_grads).astype(F32)
     small_all = dense_all[:, 0, count * slim :].reshape(layers, -1)[:, : slim * SMALL]
     small_all = small_all.reshape(layers, slim, SMALL)
@@ -770,8 +897,8 @@
         small_all[:, :, 2 : 2 + EXPERTS],
         small_all[:, :, 2 + EXPERTS : SMALL - NCONST],
         jnp.transpose(small_all[:, :, SMALL - NCONST :], (0, 2, 1)),
-        jnp.stack([g[0] for g in moe_grads]),
-        jnp.stack([g[1] for g in moe_grads]),
+        gate_up_out,
+        down_out,
     )
 
 

time: 619 us -> 604 us (0.976)
  local copies, waits for them, and re-layouts: 185 us -> 117 us
  waiting for transfers between devices: 179 us -> 239 us
  starting transfers between devices: 101 us -> 82.1 us
  Pallas kernels: 67.6 us -> 82.1 us
    ppermute x86 -> x94, waiting for transfers between devices: 165 us -> 219 us  [send(): return lax.ppermute(x, AXES, self.pairs(move))]
    dynamic_update_slice x21 -> x0, local copies, waits for them, and re-layouts: 27.8 us -> none  [the longest x10 13.7 us: put(): lax.dynamic_update_slice(full, block[None, :, None, None], (r, at, hi, lo...]
    ppermute x86 -> x94, starting transfers between devices: 101 us -> 81.2 us  [send(): return lax.ppermute(x, AXES, self.pairs(move))]
    transpose x4 -> x0, local copies, waits for them, and re-layouts: 13.1 us -> none  [the longest x2 10.1 us: local(): jnp.transpose(full, (0, 2, 1, 3, 4)).reshape(4, features, features)]
    convert_element_type x4 -> x0, local copies, waits for them, and re-layouts: 12.9 us -> none  [expert_grads(): return (full.astype(F32), down)]
    unnamed x348 -> x361, local copies, waits for them, and re-layouts: 48.7 us -> 61.3 us
    pallas_call x0 -> x8, Pallas kernels: none -> 12.2 us  [the longest x4 7.71 us: store_layer(): pl.pallas_call((lambda x, o: kernel(x, o)) if held is None else lambda x,...]
    slice x12 -> x9, local copies, waits for them, and re-layouts: 17.1 us -> 8.42 us  [the longest x2 2.46 us: dense_gather(): pieces.append((over_high(block[:cut]), 0, shift, 1))]
  transfers between devices with their start and end apart: 94 -> 102, of which waited for: 44 -> 50; matrix products, arithmetic and copies ran while one was open for 29% -> 20% of each run, Pallas kernels for 11% -> 13%
where the time goes in v3:
time: 604 us; the launch traced here: 594 us
  waiting for transfers between devices  239 us (40%)
  local copies, waits for them, and re-layouts  117 us (19%)
  starting transfers between devices  82.1 us (14%)
  Pallas kernels  82.1 us (14%)
  other arithmetic  32.9 us (5%)
  matrix products  22.8 us (4%)
  between operations  17.6 us (3%)
    ppermute x94, waiting for transfers between devices, send(): return lax.ppermute(x, AXES, self.pairs(move))  219 us
    ppermute x94, starting transfers between devices, send(): return lax.ppermute(x, AXES, self.pairs(move))  81.2 us
    pallas_call x14, Pallas kernels, call(): pl.pallas_call(kernel, out_shape=[jax.ShapeDtypeStruct(shape, dtype) for...  69.9 us
    unnamed x361, local copies, waits for them, and re-layouts  61.3 us
    dot_general x12, matrix products, dot(): return lax.dot_general(a, b, (dims, ((), ())), preferred_element_type=F32)  22.8 us
    all_gather x4, waiting for transfers between devices, line_gather(): lax.all_gather(x, 'shard', axis=0, tiled=True, axis_index_groups=self.lin...  19.9 us
  transfers between devices with their start and end apart: 102, of which 50 were waited for; matrix products, arithmetic and copies ran while one was open for 20% of the time, Pallas kernels for 13%

profile of v3, /device:TPU:0, one launch (start us, length us, event | category | flops | bytes accessed | tf_op | source)
XLA Modules:
  0.0 594.1 jit_solution(14318160729438872357)
XLA Ops:
  28.0 5.4 collective-permute-done.19
  42.3 5.2 collective-permute-done.41
  60.0 3.8 collective-permute-start.2
  65.6 8.4 %collective-permute-done.2 = bf16[112,768]{1,0:T(8,128)(2,1)S(1)} collective-permute-done((bf16[112,768]{1,0:T(8,128)(2,1)S(1)}, bf16[112,768]{1,0:T(8,128)(2,1)S(1)}, u32[]{:S(2)}, u32[]{:S(2)}) %collective-permute-start.2) | collective-permute-done | bytes 172064 | tf_op jit(solution)/shard_map/ppermute | solution.py:387
  74.0 13.2 %collective-permute-done.1 = bf16[112,768]{1,0:T(8,128)(2,1)S(1)} collective-permute-done((bf16[112,768]{1,0:T(8,128)(2,1)S(1)}, bf16[112,768]{1,0:T(8,128)(2,1)S(1)}, u32[]{:S(2)}, u32[]{:S(2)}) %collective-permute-start.1) | collective-permute-done | bytes 172064 | tf_op jit(solution)/shard_map/ppermute | solution.py:387
  92.0 13.7 %collective-permute-done.4.refs_2_ = bf16[4,112,768]{2,1,0:T(8,128)(2,1)S(1)} collective-permute-done((bf16[4,112,768]{2,1,0:T(8,128)(2,1)S(1)}, bf16[4,112,768]{2,1,0:T(8,128)(2,1)S(1)}, u32[]{:S(2)}, u32[]{:S(2)}) %collective-permute-start.4) | collective-permute-done | bytes 688160 | tf_op jit(solution)/shard_map/ppermute | solution.py:387
  127.7 8.9 %shard_map.239 = (bf16[256,768]{1,0:T(8,128)(2,1)S(1)}, bf16[256,768]{1,0:T(8,128)(2,1)S(1)}, bf16[256,768]{1,0:T(8,128)(2,1)S(1)}, bf16[256,768]{1,0:T(8,128)(2...) custom-call(bf16[256,768]{1,0:T(8,128)(2,1)S(1)} %copy-done.48, ...), custom_call_target="tpu_custom_call" | custom-call | tf_op jit(solution)/shard_map/pallas_call | solution.py:360
  147.5 12.6 %collective-permute-done.25 = bf16[96,768]{1,0:T(8,128)(2,1)S(1)} collective-permute-done((bf16[96,768]{1,0:T(8,128)(2,1)S(1)}, bf16[96,768]{1,0:T(8,128)(2,1)S(1)}, u32[]{:S(2)}, u32[]{:S(2)}) %collective-permute-start.25) | collective-permute-done | bytes 147488 | tf_op jit(solution)/shard_map/ppermute | solution.py:387
  169.0 5.3 shard_map.241
  184.6 5.7 collective-permute-done.29.refs_3_
  213.7 9.2 %shard_map.244 = (bf16[256,768]{1,0:T(8,128)(2,1)S(1)}, bf16[256,768]{1,0:T(8,128)(2,1)S(1)}, bf16[256,768]{1,0:T(8,128)(2,1)S(1)}, bf16[256,768]{1,0:T(8,128)(2...) custom-call(f32[256,768]{1,0:T(8,128)S(1)} %shard_map.242.hidden, ...), custom_call_target="tpu_custom_call" | custom-call | tf_op jit(solution)/shard_map/pallas_call | solution.py:360
  239.7 19.9 %all-gather.9.cloned.1.call-done.w_gate_up = bf16[768,2048]{1,0:T(8,128)(2,1)} async-done(((bf16[192,2048]{1,0:T(8,128)(2,1)}), bf16[768,2048]{1,0:T(8,128)(2,1)}) %all-gather.9.cloned.1.call-update) | async-done | bytes 3145744 | tf_op jit(solution)/shard_map/all_gather | solution.py:442
  262.9 4.5 shard_map.246
  271.5 3.9 convolution_convert_fusion.3
  285.4 7.2 %shard_map.250 = (bf16[640,2048]{1,0:T(8,128)(2,1)S(1)}, f32[320,768]{1,0:T(8,128)S(1)}, bf16[320,768]{1,0:T(8,128)(2,1)}) custom-call(bf16[640,768]{1,0:T(8,128)(2,1)} %bitcast.66.d_expert, bf16[768,2048]{1,0:T(8,128)(2,1)S(1)} %copy-done.8, bf16[1024,768]{1,0:T(8,128)(2,1)S(1)} %copy-done.23, f32[640,2048]{1,0:T(8,128)S(1)} %copy-done.26), custom_call_target="tpu_custom_call" | custom-call | tf_op jit(solution)/shard_map/pallas_call | solution.py:360
  293.6 4.0 convolution_convert_fusion.1
  315.0 9.5 %shard_map.251 = (f32[256,768]{1,0:T(8,128)S(1)}, bf16[256,768]{1,0:T(8,128)(2,1)S(1)}, bf16[3,256,768]{2,1,0:T(8,128)(2,1)S(1)}, f32[2,768]{1,0:T(2,128)S(1)}) custom-call(f32[256,768]{1,0:T(8,128)S(1)} %copy-done.10, f32[256,768]{1,0:T(8,128)S(1)} %get-tuple-element.93.d_mixed, bf16[320,768]{1,0:T(8,128)(2,1)S(1)} %pad_maximum_fusion.14.d_rows, ...), custom_call_target="tpu_custom_call" | custom-call | tf_op jit(solution)/shard_map/pallas_call | solution.py:360
  350.8 6.2 %shard_map.254 = (bf16[640,2048]{1,0:T(8,128)(2,1)S(1)}, f32[320,768]{1,0:T(8,128)S(1)}, bf16[320,768]{1,0:T(8,128)(2,1)}) custom-call(bf16[640,768]{1,0:T(8,128)(2,1)S(1)} %bitcast.329, bf16[768,2048]{1,0:T(8,128)(2,1)S(1)} %copy-done.6, bf16[1024,768]{1,0:T(8,128)(2,1)S(1)} %copy-done.21, f32[640,2048]{1,0:T(8,128)S(1)} %bitcast.318), custom_call_target="tpu_custom_call" | custom-call | tf_op jit(solution)/shard_map/pallas_call | solution.py:360
  374.7 5.7 collective-permute-done.67
  382.1 7.4 %collective-permute-done.65 = bf16[2,2,1,112,768]{4,3,1,2,0:T(8,128)(2,1)S(1)} collective-permute-done((bf16[2,2,1,112,768]{4,3,1,2,0:T(8,128)(2,1)S(1)}, bf16[2,2,1,112,768]{4,3,1,2,0:T(8,128)(2,1)S(1)}, u32[]{:S(2)}, u32[]{:S(2)}) %collective-permute-start.65) | collective-permute-done | bytes 688160 | tf_op jit(solution)/shard_map/ppermute | solution.py:387
  392.2 6.5 %collective-permute-done.68 = bf16[2,1,112,768]{3,2,1,0:T(8,128)(2,1)S(1)} collective-permute-done((bf16[2,1,112,768]{3,2,1,0:T(8,128)(2,1)S(1)}, bf16[2,1,112,768]{3,2,1,0:T(8,128)(2,1)S(1)}, u32[]{:S(2)}, u32[]{:S(2)}) %collective-permute-start.68) | collective-permute-done | bytes 344096 | tf_op jit(solution)/shard_map/ppermute | solution.py:387
  399.9 10.3 %shard_map.255 = (f32[256,768]{1,0:T(8,128)}, bf16[256,768]{1,0:T(8,128)(2,1)S(1)}, bf16[3,256,768]{2,1,0:T(8,128)(2,1)S(1)}, f32[2,768]{1,0:T(2,128)S(1)}) custom-call(f32[256,768]{1,0:T(8,128)S(1)} %get-tuple-element.101.d_result, f32[256,768]{1,0:T(8,128)S(1)} %get-tuple-element.104.d_mixed, bf16[320,768]{1,0:T(8,128)(2,1)S(1)} %pad_maximum_fusion.16.d_rows, ...), custom_call_target="tpu_custom_call" | custom-call | tf_op jit(solution)/shard_map/pallas_call | solution.py:360
  435.9 4.1 convolution_convert_fusion
  449.2 12.0 %collective-permute-done.85 = bf16[112,768]{1,0:T(8,128)(2,1)S(1)} collective-permute-done((bf16[112,768]{1,0:T(8,128)(2,1)S(1)}, bf16[112,768]{1,0:T(8,128)(2,1)S(1)}, u32[]{:S(2)}, u32[]{:S(2)}) %collective-permute-start.85) | collective-permute-done | bytes 172064 | tf_op jit(solution)/shard_map/ppermute | solution.py:387
  470.1 6.0 %collective-permute-done.75 = bf16[1,48,2048]{2,1,0:T(8,128)(2,1)S(1)} collective-permute-done((bf16[1,48,2048]{2,1,0:T(8,128)(2,1)S(1)}, bf16[1,48,2048]{2,1,0:T(8,128)(2,1)S(1)}, u32[]{:S(2)}, u32[]{:S(2)}) %collective-permute-start.75) | collective-permute-done | bytes 196640 | tf_op jit(solution)/shard_map/ppermute | solution.py:387
  485.3 12.6 %collective-permute-done.77 = bf16[4,48,2048]{2,1,0:T(8,128)(2,1)S(1)} collective-permute-done((bf16[4,48,2048]{2,1,0:T(8,128)(2,1)S(1)}, bf16[4,48,2048]{2,1,0:T(8,128)(2,1)S(1)}, u32[]{:S(2)}, u32[]{:S(2)}) %collective-permute-start.77) | collective-permute-done | bytes 786464 | tf_op jit(solution)/shard_map/ppermute | solution.py:387
  501.3 11.5 %collective-permute-done.72 = bf16[2,2,112,768]{3,2,1,0:T(8,128)(2,1)} collective-permute-done((bf16[2,2,112,768]{3,2,1,0:T(8,128)(2,1)}, bf16[2,2,112,768]{3,2,1,0:T(8,128)(2,1)}, u32[]{:S(2)}, u32[]{:S(2)}) %collective-permute-start.72) | collective-permute-done | bytes 688160 | tf_op jit(solution)/shard_map/ppermute | solution.py:387
  517.6 6.8 %collective-permute-done.73 = bf16[2,1,112,768]{3,2,1,0:T(8,128)(2,1)S(1)} collective-permute-done((bf16[2,1,112,768]{3,2,1,0:T(8,128)(2,1)S(1)}, bf16[2,1,112,768]{3,2,1,0:T(8,128)(2,1)S(1)}, u32[]{:S(2)}, u32[]{:S(2)}) %collective-permute-start.73) | collective-permute-done | bytes 344096 | tf_op jit(solution)/shard_map/ppermute | solution.py:387
  529.5 4.0 collective-permute-done.82
  533.5 9.4 %collective-permute-done.81 = bf16[112,768]{1,0:T(8,128)(2,1)S(1)} collective-permute-done((bf16[112,768]{1,0:T(8,128)(2,1)S(1)}, bf16[112,768]{1,0:T(8,128)(2,1)S(1)}, u32[]{:S(2)}, u32[]{:S(2)}) %collective-permute-start.81) | collective-permute-done | bytes 172064 | tf_op jit(solution)/shard_map/ppermute | solution.py:387
  555.6 5.8 collective-permute-done.89
  567.8 16.8 %collective-permute-done.91 = bf16[4,48,2048]{2,1,0:T(8,128)(2,1)S(1)} collective-permute-done((bf16[4,48,2048]{2,1,0:T(8,128)(2,1)S(1)}, bf16[4,48,2048]{2,1,0:T(8,128)(2,1)S(1)}, u32[]{:S(2)}, u32[]{:S(2)}) %collective-permute-start.91) | collective-permute-done | bytes 786464 | tf_op jit(solution)/shard_map/ppermute | solution.py:387
  (787 shorter events, 311.2 us)
Async XLA Ops:
  7.2 157.2 %all-gather.7.cloned.1.call-start = ((), (), s32[]{:S(2)}) async-start(), calls=%async_computation.5 | async-start | bytes 1966080 | tf_op jit(solution)/shard_map/all_gather | solution.py:442
  34.2 130.2 %all-gather.5.cloned.1.call-start = ((), (), s32[]{:S(2)}) async-start(), calls=%async_computation.4 | async-start | bytes 3932160 | tf_op jit(solution)/shard_map/all_gather | solution.py:442
  34.9 204.7 %all-gather.11.cloned.1.call-start = ((), (), s32[]{:S(2)}) async-start(), calls=%async_computation.7 | async-start | bytes 1966080 | tf_op jit(solution)/shard_map/all_gather | solution.py:442
  59.9 199.7 %all-gather.9.cloned.1.call-start = ((), (), s32[]{:S(2)}) async-start(), calls=%async_computation.6 | async-start | bytes 3932160 | tf_op jit(solution)/shard_map/all_gather | solution.py:442
  63.7 23.4 %collective-permute-start.1 = (bf16[112,768]{1,0:T(8,128)(2,1)S(1)}, bf16[112,768]{1,0:T(8,128)(2,1)S(1)}, u32[]{:S(2)}, u32[]{:S(2)}) collective-permute-start(bf16[112,768]{1,0:T(8,128)(2,1)S(1)} %get-tuple-element.275), channel_id=1, source_target_pairs={{0,8},{1,9},{2,10},{3,11},{4,12},{5,13},{6,14},{7,15},{8,0},{9,1},... | collective-permute-start | bytes 516104 | tf_op jit(solution)/shard_map/ppermute | solution.py:387
  63.7 23.4 %collective-permute-start = (bf16[112,768]{1,0:T(8,128)(2,1)S(1)}, bf16[112,768]{1,0:T(8,128)(2,1)S(1)}, u32[]{:S(2)}, u32[]{:S(2)}) collective-permute-start(bf16[112,768]{1,0:T(8,128)(2,1)S(1)} %get-tuple-element.275), channel_id=1, source_target_pairs={{0,4},{1,5},{2,6},{3,7},{4,8},{5,9},{6,10},{7,11},{8,12},{9,13},{1... | collective-permute-start | bytes 516104 | tf_op jit(solution)/shard_map/ppermute | solution.py:387
  87.3 19.8 %collective-permute-start.3 = (bf16[4,112,768]{2,1,0:T(8,128)(2,1)S(1)}, bf16[4,112,768]{2,1,0:T(8,128)(2,1)S(1)}, u32[]{:S(2)}, u32[]{:S(2)}) collective-permute-start(bf16[4,112,768]{2,1,0:T(8,128)(2,1)S(1)} %pad_maximum_fusion.4.refs_0_), channel_id=1, source_target_pairs={{0,2},{1,3},{2,0},{3,1},{4,6},{5,7},{6,4},{7,5},{8,10},{9,11},{10,... | collective-permute-start | bytes 2064392 | tf_op jit(solution)/shard_map/ppermute | solution.py:387
  92.0 26.1 %collective-permute-start.7 = (bf16[4,112,768]{2,1,0:T(8,128)(2,1)S(1)}, bf16[4,112,768]{2,1,0:T(8,128)(2,1)S(1)}, u32[]{:S(2)}, u32[]{:S(2)}) collective-permute-start(bf16[4,112,768]{2,1,0:T(8,128)(2,1)S(1)} %pad_maximum_fusion.4.refs_0_), channel_id=1, source_target_pairs={{0,1},{1,0},{2,3},{3,2},{4,5},{5,4},{6,7},{7,6},{8,9},{9,8},{10,11... | collective-permute-start | bytes 2064392 | tf_op jit(solution)/shard_map/ppermute | solution.py:387
  118.1 296.6 %reduce-scatter.7.cloned.1.call-start = ((), (), s32[]{:S(2)}) async-start(), calls=%async_computation.9 | async-start | bytes 1966080 | tf_op jit(solution)/shard_map/reduce_scatter | solution.py:447
  137.6 22.6 %collective-permute-start.25 = (bf16[96,768]{1,0:T(8,128)(2,1)S(1)}, bf16[96,768]{1,0:T(8,128)(2,1)S(1)}, u32[]{:S(2)}, u32[]{:S(2)}) collective-permute-start(bf16[96,768]{1,0:T(8,128)(2,1)S(1)} %bitcast.362), channel_id=1, source_target_pairs={{0,8},{1,9},{2,10},{3,11},{4,12},{5,13},{6,14},{7,15},{8,0},{9,1},... | collective-permute-start | bytes 442376 | tf_op jit(solution)/shard_map/ppermute | solution.py:387
  143.2 16.9 %collective-permute-start.24 = (bf16[96,768]{1,0:T(8,128)(2,1)S(1)}, bf16[96,768]{1,0:T(8,128)(2,1)S(1)}, u32[]{:S(2)}, u32[]{:S(2)}) collective-permute-start(bf16[96,768]{1,0:T(8,128)(2,1)S(1)} %bitcast.363), channel_id=1, source_target_pairs={{0,4},{1,5},{2,6},{3,7},{4,8},{5,9},{6,10},{7,11},{8,12},{9,13},{1... | collective-permute-start | bytes 442376 | tf_op jit(solution)/shard_map/ppermute | solution.py:387
  160.2 20.9 %collective-permute-start.27 = (bf16[4,96,768]{2,1,0:T(8,128)(2,1)S(1)}, bf16[4,96,768]{2,1,0:T(8,128)(2,1)S(1)}, u32[]{:S(2)}, u32[]{:S(2)}) collective-permute-start(bf16[4,96,768]{2,1,0:T(8,128)(2,1)S(1)} %pad_maximum_fusion.8.refs_0_), channel_id=1, source_target_pairs={{0,2},{1,3},{2,0},{3,1},{4,6},{5,7},{6,4},{7,5},{8,10},{9,11},{10,... | collective-permute-start | bytes 1769480 | tf_op jit(solution)/shard_map/ppermute | solution.py:387
  161.8 17.1 %collective-permute-start.28 = (bf16[4,96,768]{2,1,0:T(8,128)(2,1)S(1)}, bf16[4,96,768]{2,1,0:T(8,128)(2,1)}, u32[]{:S(2)}, u32[]{:S(2)}) collective-permute-start(bf16[4,96,768]{2,1,0:T(8,128)(2,1)S(1)} %pad_maximum_fusion.8.refs_0_), channel_id=1, source_target_pairs={{0,16},{1,17},{2,18},{3,19},{4,20},{5,21},{6,22},{7,23},{8,24},{9,... | collective-permute-start | bytes 1769480 | tf_op jit(solution)/shard_map/ppermute | solution.py:387
  184.1 21.8 %collective-permute-start.32 = (bf16[4,96,768]{2,1,0:T(8,128)(2,1)S(1)}, bf16[4,96,768]{2,1,0:T(8,128)(2,1)}, u32[]{:S(2)}, u32[]{:S(2)}) collective-permute-start(bf16[4,96,768]{2,1,0:T(8,128)(2,1)S(1)} %collective-permute-done.27.refs_1_), channel_id=1, source_target_pairs={{0,1},{1,0},{2,3},{3,2},{4,5},{5,4},{6,7},{7,6},{8,9},{9,8},{10,11... | collective-permute-start | bytes 1769480 | tf_op jit(solution)/shard_map/ppermute | solution.py:387
  275.4 188.4 %reduce-scatter.5.cloned.1.call-start = ((), (), s32[]{:S(2)}) async-start(), calls=%async_computation.8 | async-start | bytes 3932160 | tf_op jit(solution)/shard_map/reduce_scatter | solution.py:447
  297.6 202.5 %reduce-scatter.11.cloned.1.call-start = ((), (), s32[]{:S(2)}) async-start(), calls=%async_computation.11 | async-start | bytes 1966080 | tf_op jit(solution)/shard_map/reduce_scatter | solution.py:447
  362.0 18.3 %collective-permute-start.67 = (bf16[2,2,112,768]{3,2,1,0:T(8,128)(2,1)S(1)}, bf16[2,2,112,768]{3,2,1,0:T(8,128)(2,1)S(1)}, u32[]{:S(2)}, u32[]{:S(2)}) collective-permute-start(bf16[2,2,112,768]{3,2,1,0:T(8,128)(2,1)S(1)} %dynamic-slice_bitcast_fusion.2), channel_id=1, source_target_pairs={{0,16},{1,17},{2,18},{3,19},{4,20},{5,21},{6,22},{7,23},{8,24},{9,... | collective-permute-start | bytes 2064392 | tf_op jit(solution)/shard_map/ppermute | solution.py:387
  368.5 21.0 %collective-permute-start.65 = (bf16[2,2,1,112,768]{4,3,1,2,0:T(8,128)(2,1)S(1)}, bf16[2,2,1,112,768]{4,3,1,2,0:T(8,128)(2,1)S(1)}, u32[]{:S(2)}, u32[]{:S(2)}) collective-permute-start(bf16[2,2,1,112,768]{4,3,1,2,0:T(8,128)(2,1)S(1)} %constant_dynamic-slice_fusion.11), channel_id=1, source_target_pairs={{0,2},{1,3},{2,0},{3,1},{4,6},{5,7},{6,4},{7,5},{8,10},{9,11},{10,... | collective-permute-start | bytes 2064392 | tf_op jit(solution)/shard_map/ppermute | solution.py:387
  371.1 19.3 %collective-permute-start.64 = (bf16[80,768]{1,0:T(8,128)(2,1)S(1)}, bf16[80,768]{1,0:T(8,128)(2,1)S(1)}, u32[]{:S(2)}, u32[]{:S(2)}) collective-permute-start(bf16[80,768]{1,0:T(8,128)(2,1)S(1)} %get-tuple-element.227), channel_id=1, source_target_pairs={{0,18},{1,19},{2,16},{3,17},{4,22},{5,23},{6,20},{7,21},{8,26},{9,... | collective-permute-start | bytes 368648 | tf_op jit(solution)/shard_map/ppermute | solution.py:387
  372.4 18.1 %collective-permute-start.63 = (bf16[80,768]{1,0:T(8,128)(2,1)S(1)}, bf16[80,768]{1,0:T(8,128)(2,1)S(1)}, u32[]{:S(2)}, u32[]{:S(2)}) collective-permute-start(bf16[80,768]{1,0:T(8,128)(2,1)S(1)} %get-tuple-element.228), channel_id=1, source_target_pairs={{0,16},{1,17},{2,18},{3,19},{4,20},{5,21},{6,22},{7,23},{8,24},{9,... | collective-permute-start | bytes 368648 | tf_op jit(solution)/shard_map/ppermute | solution.py:387
  373.8 18.4 %collective-permute-start.62 = (bf16[80,768]{1,0:T(8,128)(2,1)S(1)}, bf16[80,768]{1,0:T(8,128)(2,1)S(1)}, u32[]{:S(2)}, u32[]{:S(2)}) collective-permute-start(bf16[80,768]{1,0:T(8,128)(2,1)S(1)} %get-tuple-element.229), channel_id=1, source_target_pairs={{0,2},{1,3},{2,0},{3,1},{4,6},{5,7},{6,4},{7,5},{8,10},{9,11},{10,... | collective-permute-start | bytes 368648 | tf_op jit(solution)/shard_map/ppermute | solution.py:387
  380.6 18.1 %collective-permute-start.68 = (bf16[2,1,112,768]{3,2,1,0:T(8,128)(2,1)S(1)}, bf16[2,1,112,768]{3,2,1,0:T(8,128)(2,1)S(1)}, u32[]{:S(2)}, u32[]{:S(2)}) collective-permute-start(bf16[2,1,112,768]{3,2,1,0:T(8,128)(2,1)S(1)} %constant_dynamic-slice_fusion.10), channel_id=1, source_target_pairs={{0,2},{1,3},{2,0},{3,1},{4,6},{5,7},{6,4},{7,5},{8,10},{9,11},{10,... | collective-permute-start | bytes 1032200 | tf_op jit(solution)/shard_map/ppermute | solution.py:387
  414.4 137.2 %reduce-scatter.9.cloned.1.call-start = ((), (), s32[]{:S(2)}) async-start(), calls=%async_computation.10 | async-start | bytes 3932160 | tf_op jit(solution)/shard_map/reduce_scatter | solution.py:447
  424.0 20.4 %collective-permute-start.79 = (bf16[2,128,768]{2,1,0:T(8,128)(2,1)}, bf16[2,128,768]{2,1,0:T(8,128)(2,1)}, u32[]{:S(2)}, u32[]{:S(2)}) collective-permute-start(bf16[2,128,768]{2,1,0:T(8,128)(2,1)} %constant_dynamic-update-slice_fusion.23), channel_id=1, source_target_pairs={{0,16},{1,17},{2,18},{3,19},{4,20},{5,21},{6,22},{7,23},{8,24},{9,... | collective-permute-start | bytes 1179656 | tf_op jit(solution)/shard_map/ppermute | solution.py:387
  434.7 44.7 %collective-permute-start.69 = (bf16[2,4,2,112,768]{4,3,2,1,0:T(8,128)(2,1)}, bf16[2,4,2,112,768]{4,3,2,1,0:T(8,128)(2,1)}, u32[]{:S(2)}, u32[]{:S(2)}) collective-permute-start(bf16[2,4,2,112,768]{4,3,2,1,0:T(8,128)(2,1)} %pad_maximum_fusion.3), channel_id=1, source_target_pairs={{0,1},{1,0},{2,3},{3,2},{4,5},{5,4},{6,7},{7,6},{8,9},{9,8},{10,11... | collective-permute-start | bytes 8257544 | tf_op jit(solution)/shard_map/ppermute | solution.py:387
  442.4 18.7 %collective-permute-start.85 = (bf16[112,768]{1,0:T(8,128)(2,1)S(1)}, bf16[112,768]{1,0:T(8,128)(2,1)S(1)}, u32[]{:S(2)}, u32[]{:S(2)}) collective-permute-start(bf16[112,768]{1,0:T(8,128)(2,1)S(1)} %get-tuple-element.225), channel_id=1, source_target_pairs={{0,8},{1,9},{2,10},{3,11},{4,12},{5,13},{6,14},{7,15},{8,0},{9,1},... | collective-permute-start | bytes 516104 | tf_op jit(solution)/shard_map/ppermute | solution.py:387
  442.4 18.7 %collective-permute-start.84 = (bf16[112,768]{1,0:T(8,128)(2,1)S(1)}, bf16[112,768]{1,0:T(8,128)(2,1)S(1)}, u32[]{:S(2)}, u32[]{:S(2)}) collective-permute-start(bf16[112,768]{1,0:T(8,128)(2,1)S(1)} %get-tuple-element.223), channel_id=1, source_target_pairs={{0,4},{1,5},{2,6},{3,7},{4,8},{5,9},{6,10},{7,11},{8,12},{9,13},{1... | collective-permute-start | bytes 516104 | tf_op jit(solution)/shard_map/ppermute | solution.py:387
  477.7 20.2 %collective-permute-start.77 = (bf16[4,48,2048]{2,1,0:T(8,128)(2,1)S(1)}, bf16[4,48,2048]{2,1,0:T(8,128)(2,1)S(1)}, u32[]{:S(2)}, u32[]{:S(2)}) collective-permute-start(bf16[4,48,2048]{2,1,0:T(8,128)(2,1)S(1)} %constant_dynamic-update-slice_fusion.24), channel_id=1, source_target_pairs={{0,16},{1,17},{2,18},{3,19},{4,20},{5,21},{6,22},{7,23},{8,24},{9,... | collective-permute-start | bytes 2359304 | tf_op jit(solution)/shard_map/ppermute | solution.py:387
  483.1 29.6 %collective-permute-start.72 = (bf16[2,2,112,768]{3,2,1,0:T(8,128)(2,1)}, bf16[2,2,112,768]{3,2,1,0:T(8,128)(2,1)}, u32[]{:S(2)}, u32[]{:S(2)}) collective-permute-start(bf16[2,2,112,768]{3,2,1,0:T(8,128)(2,1)} %dynamic-slice_bitcast_fusion), channel_id=1, source_target_pairs={{0,16},{1,17},{2,18},{3,19},{4,20},{5,21},{6,22},{7,23},{8,24},{9,... | collective-permute-start | bytes 2064392 | tf_op jit(solution)/shard_map/ppermute | solution.py:387
  484.6 29.5 %collective-permute-start.70 = (bf16[2,2,1,112,768]{4,3,1,2,0:T(8,128)(2,1)}, bf16[2,2,1,112,768]{4,3,1,2,0:T(8,128)(2,1)}, u32[]{:S(2)}, u32[]{:S(2)}) collective-permute-start(bf16[2,2,1,112,768]{4,3,1,2,0:T(8,128)(2,1)} %dynamic-slice_bitcast_fusion.1), channel_id=1, source_target_pairs={{0,2},{1,3},{2,0},{3,1},{4,6},{5,7},{6,4},{7,5},{8,10},{9,11},{10,... | collective-permute-start | bytes 2064392 | tf_op jit(solution)/shard_map/ppermute | solution.py:387
  516.9 27.4 %collective-permute-start.93 = (bf16[2,128,768]{2,1,0:T(8,128)(2,1)S(1)}, bf16[2,128,768]{2,1,0:T(8,128)(2,1)S(1)}, u32[]{:S(2)}, u32[]{:S(2)}) collective-permute-start(bf16[2,128,768]{2,1,0:T(8,128)(2,1)S(1)} %constant_dynamic-update-slice_fusion.31), channel_id=1, source_target_pairs={{0,16},{1,17},{2,18},{3,19},{4,20},{5,21},{6,22},{7,23},{8,24},{9,... | collective-permute-start | bytes 1179656 | tf_op jit(solution)/shard_map/ppermute | solution.py:387
  564.9 19.7 %collective-permute-start.91 = (bf16[4,48,2048]{2,1,0:T(8,128)(2,1)S(1)}, bf16[4,48,2048]{2,1,0:T(8,128)(2,1)S(1)}, u32[]{:S(2)}, u32[]{:S(2)}) collective-permute-start(bf16[4,48,2048]{2,1,0:T(8,128)(2,1)S(1)} %constant_dynamic-update-slice_fusion.20), channel_id=1, source_target_pairs={{0,16},{1,17},{2,18},{3,19},{4,20},{5,21},{6,22},{7,23},{8,24},{9,... | collective-permute-start | bytes 2359304 | tf_op jit(solution)/shard_map/ppermute | solution.py:387
  (232 other events, 2560.8 us)
Sparse Core Ops, SparseCore 0:
  34.3 50.2 all-gather.6
  86.8 71.7 all-gather.4
  160.1 34.9 all-gather.10
  197.2 62.3 all-gather.8
  275.5 33.9 reduce-scatter.6
  312.2 59.2 reduce-scatter.4
  414.5 35.1 reduce-scatter.10
  452.0 63.9 reduce-scatter.8

commit v4 on v3

--- a/solution.py
+++ b/solution.py
@@ -79,17 +79,34 @@
     return pl.ds(pl.multiple_of(step * width, width), width)
 
 
-def attention_forward_kernel(
-    hidden, gains, weights, cosine, sine, seg_col, seg_row, mixing, previous, routes, gather,
-    normed, query, keys, values, log_total, attended, middle, mixed_low, logits, coefs, rows,
-    bias,
-):
+def attention_forward_kernel(joined, last, *refs):
+    refs = iter(refs)
+
+    def take(number):
+        return [next(refs) for _ in range(number)]
+
+    parts = take(6 if joined else 1)
+    gains, weights, cosine, sine, seg_col, seg_row, mixing, previous, routes, gather = take(10)
+    d_result = take(1) if last else None
+    hidden = take(1)[0] if joined else parts[0]
+    normed, query, keys, values, log_total, attended, middle, mixed_low = take(8)
+    logits, coefs, rows, bias, held, arrived = take(6)
+    copies = [
+        pltpu.make_async_copy(weights.at[block], held.at[block], arrived.at[block])
+        for block in range(4)
+    ]
+    for copy in copies:
+        copy.start()
+    weights = held
+    if joined:
+        combine_kernel(*parts, hidden)
     tokens, features = hidden.shape
     h = hidden[...].astype(F32)
     normed[...] = (h * inverse_rms(h) * gains[0:1]).astype(BF16)
     bias[...] = attention_bias(seg_col, seg_row)
     wide = 2 * LANES
     for block, out in ((0, query), (1, keys)):
+        copies[block].wait()
 
         @pl.loop(0, features // wide)
         def _(step):
@@ -97,6 +114,8 @@
             for k in range(2):
                 turned = turn(part[:, k * LANES : (k + 1) * LANES], cosine[...], sine[...])
                 out[:, columns_of(2 * step + k, LANES)] = turned.astype(BF16)
+
+    copies[2].wait()
 
     @pl.loop(0, features // wide)
     def _(step):
@@ -123,6 +142,8 @@
             )
         attended[:, at] = total_out.astype(BF16)
 
+    copies[3].wait()
+
     @pl.loop(0, features // wide)
     def _(step):
         at = columns_of(step, wide)
@@ -131,7 +152,7 @@
     m = middle[...]
     low = (m * inverse_rms(m) * gains[1:2]).astype(BF16)
     mixed_low[...] = low
-    rows[...] = dot(gather[...], low).astype(BF16)
+    rows[:, :features] = dot(gather[0] + gather[1], low).astype(BF16)
     raw = dot(low, mixing[...])
     lane = lax.broadcasted_iota(jnp.int32, raw.shape, 1)
     now = jnp.where(lane < EXPERTS, raw + previous[...], 0.0)
@@ -166,6 +187,8 @@
     for index, column in enumerate(columns):
         packed = jnp.where(lane == index, column, packed)
     coefs[...] = packed
+    if last:
+        rows[:, features:] = value_rows(gates, gather, d_result[0])
 
 
 GATE, MIXED, VECTOR, SHARE, WEIGHT, DIRECT, CONST = 0, 2, 4, 8, 12, 14, 15
@@ -176,17 +199,15 @@
     m = middle[...]
     total = m + coef[:, DIRECT : DIRECT + 1] * (m * inverse_rms(m) * gains[1:2])
     for k in range(TOP):
-        total += coef[:, GATE + k : GATE + k + 1] * dot(scatter[k], outputs[...])
+        total += coef[:, GATE + k : GATE + k + 1] * dot(scatter[k], outputs[:, : m.shape[1]])
     for c in range(NCONST):
         total += coef[:, CONST + c : CONST + c + 1] * vectors[c : c + 1]
     result[...] = total
 
 
-def value_rows_kernel(coefs, gather, d_result, rows):
-    coef = coefs[...]
-    rows[...] = sum(
-        dot(gather[k], (coef[:, GATE + k : GATE + k + 1] * d_result[...]).astype(BF16))
-        for k in range(TOP)
+def value_rows(gates, gather, d_result):
+    return sum(
+        dot(gather[k], (gates[k] * d_result[...]).astype(BF16)) for k in range(TOP)
     ).astype(BF16)
 
 
@@ -213,7 +234,7 @@
     ]
     d_gates = []
     for k in range(TOP):
-        value = jnp.sum(dot(scatter[k], outputs[...]) * dh, axis=-1, keepdims=True)
+        value = jnp.sum(dot(scatter[k], outputs[:, : dh.shape[1]]) * dh, axis=-1, keepdims=True)
         value += column(MIXED + k) * along
         value += sum(column(VECTOR + k * NCONST + c) * with_vector[c] for c in range(NCONST))
         d_gates.append(value)
@@ -293,6 +314,40 @@
         others[:, at] = out[kept:].astype(BF16)
 
 
+def expert_both_kernel(
+    rows, w_gate_up, w_down, d_gate_up, activated, own, others, gate_up
+):
+    features, units = w_gate_up.shape[0], w_down.shape[0]
+    wide = min(2 * LANES, units)
+    kept = own.shape[0]
+
+    @pl.loop(0, units // wide)
+    def _(step):
+        at = columns_of(step, wide)
+        up_at = pl.ds(pl.multiple_of(units + step * wide, wide), wide)
+        gate_up[:, :wide] = dot(rows[:, :features], w_gate_up[:, at])
+        gate_up[:, wide:] = dot(rows[:, :features], w_gate_up[:, up_at])
+        d_active = dot(rows[:, features:], w_down[at, :], ((1,), (1,)))
+        gate, up = gate_up[:, :wide], gate_up[:, wide:]
+        sigmoid = 1.0 / (1.0 + jnp.exp(-gate))
+        activated[:, at] = (gate * sigmoid * up).astype(BF16)
+        d_gate_up[:, at] = (
+            d_active * up * sigmoid * (1.0 + gate * (1.0 - sigmoid))
+        ).astype(BF16)
+        d_gate_up[:, up_at] = (d_active * gate * sigmoid).astype(BF16)
+
+    @pl.loop(0, features // (2 * LANES))
+    def _(step):
+        at = columns_of(step, 2 * LANES)
+        out = dot(activated[...], w_down[:, at])
+        own[:, at] = out[:kept]
+        others[:, at] = out[kept:].astype(BF16)
+        out = dot(d_gate_up[...], w_gate_up[at, :], ((1,), (1,)))
+        to = pl.ds(pl.multiple_of(features + step * 2 * LANES, 2 * LANES), 2 * LANES)
+        own[:, to] = out[:kept]
+        others[:, to] = out[kept:].astype(BF16)
+
+
 def norm_backward(grad, source, gain):
     inverse = inverse_rms(source)
     scaled = grad * gain
@@ -301,21 +356,37 @@
     return inverse * scaled - source * (inverse * inverse * inverse * mean), gain_grad
 
 
-def attention_backward_kernel(
-    d_result, d_mixed, d_rows, scatter, middle, hidden, gains, weights, cosine, sine, seg_col,
-    seg_row, query, keys, values, log_total,
-    d_hidden, d_branch, d_projected, gain_grads,
-    bias, d_attended, d_normed,
-):
+def attention_backward_kernel(more, *refs):
+    refs = iter(refs)
+
+    def take(number):
+        return [next(refs) for _ in range(number)]
+
+    d_result, d_mixed, d_rows, scatter, middle, hidden, gains, weights = take(8)
+    cosine, sine, seg_col, seg_row, query, keys, values, log_total = take(8)
+    coefs, gather = take(2) if more else (None, None)
+    d_hidden, d_branch, d_projected, gain_grads = take(4)
+    rows = take(1)[0] if more else None
+    bias, d_attended, d_normed, held, arrived = take(5)
+    copies = [
+        pltpu.make_async_copy(weights.at[block], held.at[block], arrived.at[block])
+        for block in range(4)
+    ]
+    for copy in copies[::-1]:
+        copy.start()
+    weights = held
     tokens, features = hidden.shape
     wide = 2 * LANES
-    total = d_mixed[...] + dot(scatter[...], d_rows[...])
+    total = d_mixed[...] + dot(
+        scatter[0] + scatter[1], d_rows[:, d_rows.shape[1] - features :]
+    )
     d_middle, gain_grad = norm_backward(total, middle[...], gains[1:2])
     d_middle = d_middle + d_result[...]
     gain_grads[1:2] = gain_grad
     d_hidden[...] = d_middle
     d_branch[...] = d_middle.astype(BF16)
     bias[...] = attention_bias(seg_col, seg_row)
+    copies[3].wait()
 
     @pl.loop(0, features // wide)
     def _(step):
@@ -344,6 +415,9 @@
         d_projected[1, :, at] = turn(dk * SCALE, cosine[...], -sine[...]).astype(BF16)
         d_projected[2, :, at] = dv.astype(BF16)
 
+    for copy in copies[:3]:
+        copy.wait()
+
     @pl.loop(0, features // wide)
     def _(step):
         at = columns_of(step, wide)
@@ -354,14 +428,29 @@
     d_input, gain_grad = norm_backward(d_normed[...], hidden[...].astype(F32), gains[0:1])
     gain_grads[0:1] = gain_grad
     d_hidden[...] += d_input
-
-
-def call(kernel, outs, args, scratch=(), megabytes=32):
+    if more:
+        gates = [coefs[:, GATE + k : GATE + k + 1] for k in range(TOP)]
+        rows[...] = value_rows(gates, gather, d_hidden)
+
+
+def call(kernel, outs, args, scratch=(), apart=None):
+    specs = [
+        pl.BlockSpec(memory_space=pl.ANY) if k == apart else pl.BlockSpec()
+        for k in range(len(args))
+    ]
+    scratch = [pltpu.VMEM(shape, dtype) for shape, dtype in scratch]
+    if apart is not None:
+        scratch += [
+            pltpu.VMEM(args[apart].shape, args[apart].dtype),
+            pltpu.SemaphoreType.DMA((4,)),
+        ]
     return pl.pallas_call(
         kernel,
         out_shape=[jax.ShapeDtypeStruct(shape, dtype) for shape, dtype in outs],
-        scratch_shapes=[pltpu.VMEM(shape, dtype) for shape, dtype in scratch],
-        compiler_params=pltpu.CompilerParams(vmem_limit_bytes=megabytes * 1024 * 1024),
+        in_specs=specs,
+        scratch_shapes=scratch,
+        compiler_params=pltpu.CompilerParams(vmem_limit_bytes=60 * 1024 * 1024),
+        cost_estimate=pl.CostEstimate(flops=1, bytes_accessed=1, transcendentals=0),
     )(*args)
 
 
@@ -435,6 +524,25 @@
             )
         return got
 
+    def trade(self, blocks, chosen):
+        groups = [
+            [(n // EF) * self.shards + z * EF + n % EF for n in numbers]
+            for z in range(self.lines)
+            for numbers in chosen
+        ]
+        return lax.all_to_all(blocks, AXES, 0, 0, axis_index_groups=groups, tiled=True)
+
+    def return_gate_up(self, blocks):
+        return self.trade(
+            jnp.concatenate([blocks] * self.reps), [list(range(self.reps * EF))]
+        )
+
+    def return_down(self, blocks):
+        return self.trade(
+            jnp.concatenate([blocks] * self.reps),
+            [[e * self.reps + f for e in range(EF)] for f in range(self.reps)],
+        )
+
     def line_groups(self):
         return [[z * EF + j for z in range(self.lines)] for j in range(EF)]
 
@@ -448,12 +556,14 @@
             x, "shard", scatter_dimension=0, tiled=True, axis_index_groups=self.line_groups()
         )
 
-    def dense_gather(self, x):
+    def dense_line(self, x):
+        line = [x[None]]
+        for shift in range(1, self.lines):
+            line.append(self.send(x, lambda r, q, k: (r, (q + shift) % self.lines, k))[None])
+        return jnp.concatenate(line)
+
+    def dense_gather(self, line):
         reps, lines = self.reps, self.lines
-        line = [x[None]]
-        for shift in range(1, lines):
-            line.append(self.send(x, lambda r, q, k: (r, (q + shift) % lines, k))[None])
-        line = jnp.concatenate(line)
         cut = lines // 2
 
         def over_rep(block, shift):
@@ -506,39 +616,39 @@
             in_specs=[pl.BlockSpec(memory_space=pltpu.SMEM)]
             + [pl.BlockSpec(memory_space=pltpu.VMEM)] * len(pieces),
             out_specs=[pl.BlockSpec(memory_space=pltpu.VMEM)] * len(shapes),
-            compiler_params=pltpu.CompilerParams(vmem_limit_bytes=32 * 1024 * 1024),
+            compiler_params=pltpu.CompilerParams(vmem_limit_bytes=60 * 1024 * 1024),
         )(where, *[piece[0] for piece in pieces])
 
     def over_rep(self, block, shift):
         return self.send(block, lambda r, q, k: ((r + shift) % self.reps, q, k))
 
-    def sum_core(self, parts, j):
-        core = j % 2
-        other = self.send(parts(1 - core), lambda r, q, k: (r, q, k ^ 1))
-        return (parts(core).astype(F32) + other.astype(F32)).astype(BF16)
+    def sum_core(self, terms, core):
+        mine = lax.dynamic_slice_in_dim(terms, core, 1, 0)[0]
+        other = lax.dynamic_slice_in_dim(terms, 1 - core, 1, 0)[0]
+        other = self.send(other, lambda r, q, k: (r, q, k ^ 1))
+        return (mine.astype(F32) + other.astype(F32)).astype(BF16)
+
+    def rep_step(self, x, rep):
+        total = lax.dynamic_slice_in_dim(x, rep, 1, 0)[0].astype(F32)
+        for shift in range(1, self.reps):
+            block = lax.dynamic_slice_in_dim(x, (rep + shift) % self.reps, 1, 0)[0]
+            total = total + self.over_rep(block, shift).astype(F32)
+        return total.astype(BF16)
+
+    def high_step(self, x, high, axis):
+        mine = lax.dynamic_slice_in_dim(x, high, 1, axis)
+        other = lax.dynamic_slice_in_dim(x, 1 - high, 1, axis)
+        other = self.send(other, lambda r, q, k: (r, q, k ^ 2))
+        return jnp.squeeze(mine.astype(F32) + other.astype(F32), axis).astype(BF16)
 
     def sum_cross(self, both, rep, j):
-        high = j // 2
-
-        def rep_step(x):
-            total = lax.dynamic_slice_in_dim(x, rep, 1, 0)[0].astype(F32)
-            for shift in range(1, self.reps):
-                block = lax.dynamic_slice_in_dim(x, (rep + shift) % self.reps, 1, 0)[0]
-                total = total + self.over_rep(block, shift).astype(F32)
-            return total.astype(BF16)
-
-        def high_step(x, axis):
-            mine = lax.dynamic_slice_in_dim(x, high, 1, axis)
-            other = lax.dynamic_slice_in_dim(x, 1 - high, 1, axis)
-            other = self.send(other, lambda r, q, k: (r, q, k ^ 2))
-            return jnp.squeeze(mine.astype(F32) + other.astype(F32), axis).astype(BF16)
-
         cut = self.lines // 2
-        first = rep_step(high_step(both[:, :cut], 2))
-        second = high_step(rep_step(both[:, cut:]), 1)
-        return jnp.concatenate([first, second])
-
-    def sum_line(self, line, rep):
+        return self.high_step(both[:, :cut], j // 2, 2), self.rep_step(both[:, cut:], rep)
+
+    def sum_cross_end(self, first, second, rep, j):
+        return jnp.concatenate([self.rep_step(first, rep), self.high_step(second, j // 2, 1)])
+
+    def sum_line(self, line):
         z = lax.axis_index("shard") // EF
         lines = self.lines
         total = lax.dynamic_slice_in_dim(line, z, 1, 0)[0].astype(F32)
@@ -546,7 +656,7 @@
             block = lax.dynamic_slice_in_dim(line, (z + shift) % lines, 1, 0)[0]
             block = self.send(block, lambda r, q, k: (r, (q + shift) % lines, k))
             total = total + block.astype(F32)
-        return self.rep_gather(total.astype(BF16), rep)
+        return total.astype(BF16)
 
     def dispatch(self, rows):
         blocks = rows.reshape(EF, CAP, -1)
@@ -589,7 +699,7 @@
             pl.BlockSpec((1, experts, rows, columns), lambda _: (layer, 0, 0, 0)),
         ],
         out_specs=pl.BlockSpec((EF, rows, columns // parts), lambda _: (0, 0, 0)),
-        compiler_params=pltpu.CompilerParams(vmem_limit_bytes=32 * 1024 * 1024),
+        compiler_params=pltpu.CompilerParams(vmem_limit_bytes=60 * 1024 * 1024),
     )(where, w_gate_up)
 
 
@@ -603,14 +713,33 @@
     return layout.line_gather(mine), layout.line_gather(down), down
 
 
-def place_down(layout, down, rep, j):
-    down = layout.part_exchange(down.reshape(EF // layout.reps, -1, down.shape[-1]), j)
-    return layout.rep_gather(down, rep).reshape((1, EF) + down.shape[1:])
-
-
-def place_gate_up(layout, mine, rep, j):
-    mine = layout.quad_exchange(mine.reshape(EF, -1, mine.shape[-1]), j)
-    return layout.rep_gather(mine, rep).reshape((EF, layout.reps) + mine.shape[1:])
+def dense_gradients(layout, terms, small, count):
+    tokens, features = terms[0].shape
+    lines, slim = layout.lines, features // layout.shards
+    wide = 2 * LANES
+
+    def kernel(normed, attended, d_projected, d_branch, small_ref, out, turned):
+        turned[0] = normed[...].T
+        turned[1] = attended[...].T
+        for block in range(4):
+            r, k = block // count, block % count
+
+            @pl.loop(0, features // wide)
+            def _(step):
+                at = columns_of(step, wide)
+                grad = d_branch[:, at] if block == 3 else d_projected[block, :, at]
+                term = dot(turned[block // 3], grad).astype(BF16)
+                for s in range(layout.shards):
+                    out[s % 2, r, s // EF, s // 2 % 2, k * slim : (k + 1) * slim, at] = term[
+                        s * slim : (s + 1) * slim
+                    ]
+
+        for s in range(layout.shards):
+            for r in range(layout.reps):
+                out[s % 2, r, s // EF, s // 2 % 2, count * slim :] = small_ref[s]
+
+    shape = (2, layout.reps, lines, 2, count * slim + ROWS, features)
+    return call(kernel, [(shape, BF16)], (*terms, small), [((2, features, tokens), BF16)])[0]
 
 
 def store_layer(kernel, source, block, index, shape, layer, held):
@@ -623,7 +752,7 @@
         in_specs=[pl.BlockSpec(block, index)] + [pl.BlockSpec(memory_space=pl.ANY)] * len(whole),
         out_specs=spec,
         input_output_aliases={} if held is None else {1: 0},
-        compiler_params=pltpu.CompilerParams(vmem_limit_bytes=32 * 1024 * 1024),
+        compiler_params=pltpu.CompilerParams(vmem_limit_bytes=60 * 1024 * 1024),
     )(source, *whole)
 
 
@@ -663,19 +792,35 @@
     return gather, scatter
 
 
-def attention_forward(shared, dense, hidden, previous, routes, gather):
+def attention_forward(shared, dense, source, previous, routes, gather, d_result):
     gains, weights, mixing = dense
-    tokens, features = hidden.shape
-    cosine, sine, seg_col, seg_row = shared
+    tokens, features = source[1 if len(source) > 1 else 0].shape
+    joined, last = len(source) > 1, d_result is not None
     low = ((tokens, features), BF16)
+    full = ((tokens, features), F32)
     lanes = ((tokens, LANES), F32)
+    found = call(
+        functools.partial(attention_forward_kernel, joined, last),
+        [full] * joined
+        + [low, low, low, low, lanes, low, full, low, lanes, lanes]
+        + [((gather.shape[1], features * (2 if last else 1)), BF16)],
+        (*source, gains, weights, *shared, mixing, previous, routes, gather)
+        + ((d_result,) if last else ()),
+        [((tokens, tokens), F32)],
+        len(source) + 1,
+    )
+    return found if joined else [source[0], *found]
+
+
+def expert_both(rows, w_gate_up, w_down):
+    count, double = rows.shape
+    units = w_down.shape[0]
     return call(
-        attention_forward_kernel,
-        [low, low, low, low, lanes, low, ((tokens, features), F32), low, lanes, lanes]
-        + [((EF * CAP, features), BF16)],
-        (hidden, gains, weights, cosine, sine, seg_col, seg_row, mixing, previous, routes)
-        + (gather[0] + gather[1],),
-        [((tokens, tokens), F32)],
+        expert_both_kernel,
+        [((count, 2 * units), BF16), ((count, units), BF16)]
+        + [((EF * CAP, double), F32), ((count - EF * CAP, double), BF16)],
+        (rows, w_gate_up, w_down),
+        [((count, 2 * min(2 * LANES, units)), F32)],
     )
 
 
@@ -750,11 +895,14 @@
         full = layout.assemble(layout.dense_gather(x), where, count)
         return full[0].reshape(4, features, features), *full[1:]
 
-    full, small_full = dense_weights(share(0, small))
+    line = layout.dense_line(share(0, small))
+    *found, last = expert_weights(layout, w_gate_up, w_down, 0, rep, j, group)
+    moe = [found]
+    full, small_full = dense_weights(after(line, last))
     small_full = small_full.reshape(layout.shards, -1)
-    dense, moe = [full], []
-    raw = w_gate_up
-    for l in range(layers):
+    dense = [full]
+    raw = after(w_gate_up, full)
+    for l in range(1, layers):
         *found, last = expert_weights(layout, raw, w_down, l, rep, j, group)
         moe.append(found)
         raw = after(raw, last)
@@ -771,123 +919,128 @@
     shared = (*rope_tables(tokens), segments.reshape(-1, 1), segments)
     pairs = [place_pairs(routes[l], priority[l, 0], expert) for l in range(layers)]
 
-    hidden = hidden_in
+    source = (hidden_in,)
     previous = jnp.pad(gate_in, ((0, 0), (0, LANES - EXPERTS)))
     kept = []
     for l in range(layers):
         gather, scatter = pairs[l]
         packs[l][1] = dense[l]
-        state = attention_forward(shared, packs[l], hidden, previous, routes[l], gather)
-        normed, query, keys, values, log_total, attended, middle, low, logits, coefs, rows = state
-        if l + 1 < layers:
-            dense.append(dense_weights(after(share(l + 1), rows))[0])
-        inputs = layout.dispatch(rows)
-        gate_up, activated, own, others = expert_forward(layout, inputs, *moe[l])
+        last = l + 1 == layers
+        state = attention_forward(
+            shared, packs[l], source, previous, routes[l], gather, grad_out if last else None
+        )
+        middle, logits, coefs, rows = state[7], state[9], state[10], state[11]
+        if last:
+            inputs = layout.dispatch(rows)
+            d_gate_up, activated, own, others = expert_both(inputs, *moe[l])
+            wide = dot(inputs[:, :features], d_gate_up, ((0,), (0,))).astype(BF16)
+            down = dot(activated, inputs[:, features:], ((0,), (0,))).astype(BF16)
+        else:
+            dense.append(dense_weights(layout.dense_line(after(share(l + 1), rows)))[0])
+            inputs = layout.dispatch(rows)
+            gate_up, activated, own, others = expert_forward(layout, inputs, *moe[l])
         outputs = layout.collect(own, others)
-        (result,) = call(
-            combine_kernel,
-            [((tokens, features), F32)],
-            (coefs, middle, packs[l][0], scatter, outputs, vectors[l]),
-        )
-        kept.append((hidden, state, inputs, gate_up, activated, outputs))
-        hidden, previous = result, logits
+        if last:
+            outputs, wide, down = lax.optimization_barrier((outputs, wide, down))
+        source = (coefs, middle, packs[l][0], scatter, outputs, vectors[l])
+        previous = logits
+        kept.append((state, inputs, gate_up, activated, outputs))
+    (result,) = call(combine_kernel, [((tokens, features), F32)], source)
 
     grad_hidden = grad_out
     grad_gate = jnp.zeros_like(previous)
-    dense_grads = [None] * layers
-    waiting = None
+    join = lax.optimization_barrier
+
+    def back_down(x):
+        return layout.return_down(x.reshape(count, -1, features))
+
+    def back_gate_up(x):
+        return layout.return_gate_up(x.reshape(EF, -1, x.shape[-1]))
+
+    def put_down(x, l, held):
+        return store_down(x[None], (layers, EF) + w_down.shape[2:], l, held)
+
+    def put_gate_up(x, l, held):
+        x = x.reshape((EF, layout.reps) + x.shape[1:])
+        return store_gate_up(layout, x, (layers, EF) + w_gate_up.shape[2:], l, held)
+
+    boths, wides, downs = [None] * layers, [None] * layers, [None] * layers
     gate_up_out, down_out = None, None
-
-    def store(wide, down, l, gate_up_out, down_out):
-        down_out = store_down(
-            place_down(layout, down, rep, j), (layers, EF) + w_down.shape[2:], l, down_out
-        )
-        gate_up_out = store_gate_up(
-            layout,
-            place_gate_up(layout, wide, rep, j),
-            (layers, EF) + w_gate_up.shape[2:],
-            l,
-            gate_up_out,
-        )
-        return gate_up_out, down_out
-
     for l in reversed(range(layers)):
         gather, scatter = pairs[l]
-        source, state, inputs, gate_up, activated, outputs = kept[l]
-        normed, query, keys, values, log_total, attended, middle, low, logits, coefs, _ = state
-        (rows,) = call(
-            value_rows_kernel,
-            [((EF * CAP, features), BF16)],
-            (coefs, gather, grad_hidden),
-        )
-        d_expert = layout.dispatch(rows)
+        state, inputs, gate_up, activated, outputs = kept[l]
+        hidden, normed, query, keys, values, log_total, attended, middle, low = state[:9]
+        coefs = state[10]
+        last = l + 1 == layers
+        if not last:
+            d_expert = layout.dispatch(rows)
         grad_gate, d_mixed, mix_grads = call(
             gate_backward_kernel,
             [((tokens, LANES), F32), ((tokens, features), F32), ((SMALL - 2, features), F32)],
             (coefs, middle, packs[l][0], scatter, outputs, vectors[l], routes[l], low)
             + (mixing_t[l], grad_hidden, grad_gate),
         )
-        if waiting is not None:
-            d_expert, waiting = lax.optimization_barrier((d_expert, waiting))
-            waiting = layout.sum_cross(waiting, rep, j)
-        if l > 0:
+        if last:
+            d_rows = outputs
+            wides[l], downs[l] = layout.line_sum(wide), layout.line_sum(down)
+        else:
+            d_expert, d_mixed = join((d_expert, d_mixed))
+            down = back_down(after(downs[l + 1], d_expert))
+            d_gate_up, own, others = expert_backward(layout, d_expert, *moe[l], gate_up)
+            own, down = join((own, down))
+            down_out = put_down(down, l + 1, down_out)
+            grad_gate_up = dot(inputs, d_gate_up, ((0,), (0,))).astype(BF16)
+            d_rows = layout.collect(own, others)
+            boths[l + 1] = layout.sum_core(
+                dense_gradients(layout, *after(ready, d_expert), count), j % 2
+            )
             grad_down = dot(activated, d_expert, ((0,), (0,))).astype(BF16)
-        d_gate_up, own, others = expert_backward(layout, d_expert, *moe[l], gate_up)
-        d_rows = layout.collect(own, others)
-        grad_gate_up = dot(inputs, d_gate_up, ((0,), (0,))).astype(BF16)
-        wide = layout.line_sum(grad_gate_up)
-        if l > 0:
-            down = layout.line_sum(grad_down)
-            gate_up_out, down_out = store(wide, down, l, gate_up_out, down_out)
-        if waiting is not None:
-            d_rows, waiting = lax.optimization_barrier((d_rows, waiting))
-            dense_grads[l + 1] = layout.sum_line(waiting, rep)
-        grad_hidden, d_branch, d_projected, gain_grads = call(
-            attention_backward_kernel,
+            d_rows, grad_gate_up, grad_down, boths[l + 1], down_out = join(
+                (d_rows, grad_gate_up, grad_down, boths[l + 1], down_out)
+            )
+            wides[l], downs[l] = layout.line_sum(grad_gate_up), layout.line_sum(grad_down)
+            d_rows, wides[l + 1] = join((d_rows, wides[l + 1]))
+            wide = back_gate_up(wides[l + 1])
+        more = () if l == 0 else (kept[l - 1][0][10], pairs[l - 1][0])
+        grad_hidden, d_branch, d_projected, gain_grads, *rows = call(
+            functools.partial(attention_backward_kernel, l > 0),
             [((tokens, features), F32), ((tokens, features), BF16)]
-            + [((3, tokens, features), BF16), ((2, features), F32)],
-            (grad_hidden, d_mixed, d_rows, scatter[0] + scatter[1], middle, source)
-            + (packs[l][0], packs[l][1], *shared, query, keys, values, log_total),
+            + [((3, tokens, features), BF16), ((2, features), F32)]
+            + [((gather.shape[1], features), BF16)] * (l > 0),
+            (grad_hidden, d_mixed, d_rows, scatter, middle, hidden, packs[l][0], packs[l][1])
+            + (*shared, query, keys, values, log_total, *more),
             [((tokens, tokens), F32), ((tokens, features), BF16), ((tokens, features), F32)],
-        )
-        if l == 0:
-            activated = after(activated, d_branch)
-            grad_down = dot(activated, d_expert, ((0,), (0,))).astype(BF16)
-            down = layout.line_sum(grad_down)
-        grad_dense = jnp.stack(
-            [dot(normed, d_projected[b], ((0,), (0,))).astype(BF16) for b in range(3)]
-            + [dot(attended, d_branch, ((0,), (0,))).astype(BF16)]
-        )
+            7,
+        )
+        rows = rows[0] if rows else None
+        if not last:
+            d_branch, wide = join((d_branch, wide))
+            gate_up_out = put_gate_up(wide, l + 1, gate_up_out)
         small_grads = jnp.concatenate([gain_grads, mix_grads]).T.astype(BF16)
-        lines = layout.lines
-        blocks = grad_dense.reshape(layout.reps, count, lines, 2, 2, slim, features)
-        small_grads = small_grads.reshape(lines, 2, 2, slim * SMALL)
-        small_grads = jnp.pad(
-            small_grads, ((0, 0),) * 3 + ((0, ROWS * features - slim * SMALL),)
-        ).reshape(lines, 2, 2, ROWS, features)
-
-        def parts(c):
-            chosen = lax.dynamic_slice_in_dim(blocks, c, 1, 4)[:, :, :, :, 0]
-            chosen = jnp.transpose(chosen, (0, 2, 3, 1, 4, 5)).reshape(
-                layout.reps, lines, 2, count * slim, features
-            )
-            extra = lax.dynamic_slice_in_dim(small_grads, c, 1, 2)[:, :, 0]
-            extra = jnp.broadcast_to(extra[None], (layout.reps,) + extra.shape)
-            return jnp.concatenate([chosen, extra], axis=3)
-
-        waiting = layout.sum_core(parts, j)
-
-    waiting = layout.sum_cross(waiting, rep, j)
-    waiting, gate_up_out, down_out = lax.optimization_barrier((waiting, gate_up_out, down_out))
-    dense_grads[0] = layout.sum_line(waiting, rep)
-    gate_up_out, down_out = store(wide, down, 0, gate_up_out, down_out)
-    dense_all = jnp.stack(dense_grads).astype(F32)
+        small_grads = small_grads.reshape(layout.shards, slim * SMALL)
+        small_grads = jnp.pad(small_grads, ((0, 0), (0, ROWS * features - slim * SMALL)))
+        ready = (
+            (normed, attended, d_projected, d_branch),
+            small_grads.reshape(layout.shards, ROWS, features),
+        )
+
+    boths[0] = layout.sum_core(dense_gradients(layout, *ready, count), j % 2)
+    both, gate_up_out = join((jnp.concatenate(boths, axis=3), gate_up_out))
+    cross, down = join((layout.sum_cross(both, rep, j), back_down(after(downs[0], both))))
+    down_out = put_down(down, 0, down_out)
+    line = layout.sum_cross_end(*cross, rep, j)
+    line, wides[0] = join((line, wides[0]))
+    line, wide = join((layout.sum_line(line), back_gate_up(wides[0])))
+    gate_up_out = put_gate_up(wide, 0, gate_up_out)
+    dense_all = layout.rep_gather(line, rep).reshape(layout.reps, layers, -1, features)
+    dense_grads = jnp.swapaxes(dense_all, 0, 1)
+    dense_all = dense_grads.astype(F32)
     small_all = dense_all[:, 0, count * slim :].reshape(layers, -1)[:, : slim * SMALL]
     small_all = small_all.reshape(layers, slim, SMALL)
     dense_all = dense_all[:, :, : count * slim].reshape(layers, 4, slim, features)
     qkv_all = jnp.transpose(dense_all[:, :3], (0, 2, 1, 3)).reshape(layers, slim, 3 * features)
     return (
-        hidden.astype(BF16),
+        result.astype(BF16),
         grad_hidden,
         grad_gate[:, :EXPERTS],
         small_all[:, :, 0],

time: 604 us -> 577 us (0.955)
  the two profiles are of different devices: /device:TPU:0 before, /device:TPU:8 now
where the time goes in v4:
time: 577 us; the launch traced here: 567 us
  waiting for transfers between devices  212 us (37%)
  Pallas kernels  146 us (25%)
  starting transfers between devices  72 us (12%)
  local copies, waits for them, and re-layouts  60.2 us (10%)
  other arithmetic  40.8 us (7%)
  matrix products  19.7 us (3%)
  between operations  16.1 us (3%)
    ppermute x66, waiting for transfers between devices, send(): return lax.ppermute(x, AXES, self.pairs(move))  195 us
    pallas_call x12, Pallas kernels, call(): pl.pallas_call(kernel, out_shape=[jax.ShapeDtypeStruct(shape, dtype) for...  117 us
    ppermute x66, starting transfers between devices, send(): return lax.ppermute(x, AXES, self.pairs(move))  56.4 us
    unnamed x133, local copies, waits for them, and re-layouts  21.2 us
    dot_general x4, matrix products, dot(): return lax.dot_general(a, b, (dims, ((), ())), preferred_element_type=F32)  19.7 us
    all_to_all x4, starting transfers between devices, trade(): lax.all_to_all(blocks, AXES, 0, 0, axis_index_groups=groups, tiled=True)  15.2 us
    pallas_call x4, Pallas kernels, store_layer(): pl.pallas_call((lambda x, o: kernel(x, o)) if held is None else lambda x,...  14.6 us
  transfers between devices with their start and end apart: 78, of which 42 were waited for; matrix products, arithmetic and copies ran while one was open for 18% of the time, Pallas kernels for 23%

profile of v4, /device:TPU:8, one launch (start us, length us, event | category | flops | bytes accessed | tf_op | source)
XLA Modules:
  0.0 567.3 jit_solution(15003661269142606430)
XLA Ops:
  23.9 5.6 collective-permute-done.6
  38.8 12.5 %collective-permute-done = bf16[112,768]{1,0:T(8,128)(2,1)S(1)} collective-permute-done((bf16[112,768]{1,0:T(8,128)(2,1)S(1)}, bf16[112,768]{1,0:T(8,128)(2,1)S(1)}, u32[]{:S(2)}, u32[]{:S(2)}) %collective-permute-start) | collective-permute-done | bytes 172064 | tf_op jit(solution)/shard_map/ppermute | solution.py:476
  51.3 13.4 %collective-permute-done.1 = bf16[112,768]{1,0:T(8,128)(2,1)S(1)} collective-permute-done((bf16[112,768]{1,0:T(8,128)(2,1)S(1)}, bf16[112,768]{1,0:T(8,128)(2,1)S(1)}, u32[]{:S(2)}, u32[]{:S(2)}) %collective-permute-start.1) | collective-permute-done | bytes 172064 | tf_op jit(solution)/shard_map/ppermute | solution.py:476
  71.8 14.2 %collective-permute-done.8.refs_2_ = bf16[4,112,768]{2,1,0:T(8,128)(2,1)S(1)} collective-permute-done((bf16[4,112,768]{2,1,0:T(8,128)(2,1)S(1)}, bf16[4,112,768]{2,1,0:T(8,128)(2,1)S(1)}, u32[]{:S(2)}, u32[]{:S(2)}) %collective-permute-start.8) | collective-permute-done | bytes 688160 | tf_op jit(solution)/shard_map/ppermute | solution.py:476
  89.7 5.4 collective-permute-done.9.refs_3_
  98.5 5.2 shard_map.239
  109.5 5.9 %collective-permute-done.41 = bf16[1,48,2048]{2,1,0:T(8,128)(2,1)S(1)} collective-permute-done((bf16[1,48,2048]{2,1,0:T(8,128)(2,1)S(1)}, bf16[1,48,2048]{2,1,0:T(8,128)(2,1)S(1)}, u32[]{:S(2)}, u32[]{:S(2)}) %collective-permute-start.41) | collective-permute-done | bytes 196640 | tf_op jit(solution)/shard_map/ppermute | solution.py:476
  121.0 5.4 collective-permute-done.43
  134.0 12.3 %shard_map.240 = (bf16[256,768]{1,0:T(8,128)(2,1)}, bf16[256,768]{1,0:T(8,128)(2,1)}, bf16[256,768]{1,0:T(8,128)(2,1)}, bf16[256,768]{1,0:T(8,128)(2,1)}, f32[25...) custom-call(bf16[256,768]{1,0:T(8,128)(2,1)} %refs_5_.1, ...), custom_call_target="tpu_custom_call" | custom-call | flops 1 | bytes 1 | tf_op jit(solution)/shard_map/pallas_call | solution.py:447
  157.4 8.6 %collective-permute-done.25 = bf16[96,768]{1,0:T(8,128)(2,1)S(1)} collective-permute-done((bf16[96,768]{1,0:T(8,128)(2,1)S(1)}, bf16[96,768]{1,0:T(8,128)(2,1)S(1)}, u32[]{:S(2)}, u32[]{:S(2)}) %collective-permute-start.25) | collective-permute-done | bytes 147488 | tf_op jit(solution)/shard_map/ppermute | solution.py:476
  174.4 9.9 %shard_map.241 = (f32[640,2048]{1,0:T(8,128)}, bf16[640,1024]{1,0:T(8,128)(2,1)}, f32[320,768]{1,0:T(8,128)}, bf16[320,768]{1,0:T(8,128)(2,1)}) custom-call(bf16[640,768]{1,0:T(8,128)(2,1)} %bitcast.211, bf16[768,2048]{1,0:T(8,128)(2,1)} %all-gather.5.cloned.1.call-done.w_gate_up, bf16[1024,768]{1,0:T(8,128)(2,1)} %all-gather.7.cloned.1.call-done.w_down), custom_call_target="tpu_custom_call" | custom-call | flops 1 | bytes 1 | tf_op jit(solution)/shard_map/pallas_call | solution.py:447
  206.6 4.9 shard_map.242
  213.4 13.0 %shard_map.243 = (f32[256,768]{1,0:T(8,128)}, bf16[256,768]{1,0:T(8,128)(2,1)}, bf16[256,768]{1,0:T(8,128)(2,1)}, bf16[256,768]{1,0:T(8,128)(2,1)}, bf16[256,768...) custom-call(f32[256,128]{1,0:T(8,128)} %get-tuple-element.103.refs_0, ...), custom_call_target="tpu_custom_call" | custom-call | flops 1 | bytes 1 | tf_op jit(solution)/shard_map/pallas_call | solution.py:447
  244.2 4.7 all-gather.9.cloned.1.call-done.w_gate_up
  248.9 12.3 %shard_map.245 = (bf16[640,2048]{1,0:T(8,128)(2,1)}, bf16[640,1024]{1,0:T(8,128)(2,1)}, f32[320,1536]{1,0:T(8,128)}, bf16[320,1536]{1,0:T(8,128)(2,1)}) custom-call(bf16[640,1536]{1,0:T(8,128)(2,1)} %bitcast.202, bf16[768,2048]{1,0:T(8,128)(2,1)} %all-gather.9.cloned.1.call-done.w_gate_up, bf16[1024,768]{1,0:T(8,128)(2,1)} %all-gather.11.cloned.1.call-done.w_down), custom_call_target="tpu_custom_call" | custom-call | flops 1 | bytes 1 | tf_op jit(solution)/shard_map/pallas_call | solution.py:447
  261.3 6.5 %convolution_convert_fusion.1 = bf16[768,2048]{1,0:T(8,128)(2,1)} fusion(bf16[640,2048]{1,0:T(8,128)(2,1)} %get-tuple-element.117, bf16[640,1536]{1,0:T(8,128)(2,1)} %bitcast.203), kind=kOutput, calls=%fused_computation.6 | convolution fusion | flops 2014838784 | bytes 6750208 | tf_op jit(solution)/shard_map/dot_general | solution.py:30
  278.5 4.5 collective-permute-done.47
  288.4 5.9 %shard_map.247 = (f32[256,128]{1,0:T(8,128)}, f32[256,768]{1,0:T(8,128)}, f32[14,768]{1,0:T(8,128)}) custom-call(f32[256,128]{1,0:T(8,128)} %get-tuple-element.110.coefs, f32[256,768]{1,0:T(8,128)} %get-tuple-element.111.middle.refs_4_, f32[2,768]{1,0:T(2,128)} %bitcast.242, bf16[2,256,320]{2,1,0:T(8,128)(2,1)} %fusion.8.scatter.refs_3_, ...), custom_call_target="tpu_custom_call" | custom-call | flops 1 | bytes 1 | tf_op jit(solution)/shard_map/pallas_call | solution.py:447
  294.3 14.4 %shard_map.248 = (f32[256,768]{1,0:T(8,128)}, bf16[256,768]{1,0:T(8,128)(2,1)}, bf16[3,256,768]{2,1,0:T(8,128)(2,1)}, f32[2,768]{1,0:T(2,128)}, bf16[320,768]{1,0:T(8,128)(2,1)}) custom-call(f32[256,768]{1,0:T(8,128)} %refs_0_.3, f32[256,768]{1,0:T(8,128)} %get-tuple-element.121.refs_1_, bf16[320,1536]{1,0:T(8,128)(2,1)} %pad_maximum_fusion.5.outputs.refs_2_, ...), custom_call_target="tpu_custom_call" | custom-call | flops 1 | bytes 1 | tf_op jit(solution)/shard_map/pallas_call | solution.py:447
  308.7 5.8 %shard_map.249 = (f32[256,128]{1,0:T(8,128)}, f32[256,768]{1,0:T(8,128)}, f32[14,768]{1,0:T(8,128)}) custom-call(f32[256,128]{1,0:T(8,128)} %get-tuple-element.103.refs_0_.refs_16_.coefs, f32[256,768]{1,0:T(8,128)} %get-tuple-element.104.refs_1_.middle.refs_4_, f32[2,768]{1,0:T(2,128)} %bitcast.247, bf16[2,256,320]{2,1,0:T(8,128)(2,1)} %fusion.7.refs_3_.scatter, ...), custom_call_target="tpu_custom_call" | custom-call | flops 1 | bytes 1 | tf_op jit(solution)/shard_map/pallas_call | solution.py:447
  327.9 7.9 %shard_map.251 = bf16[2,2,4,2,112,768]{5,4,3,2,1,0:T(8,128)(2,1)} custom-call(bf16[256,768]{1,0:T(8,128)(2,1)} %get-tuple-element.148.normed, bf16[256,768]{1,0:T(8,128)(2,1)} %get-tuple-element.149.attended, bf16[3,256,768]{2,1,0:T(8,128)(2,1)} %get-tuple-element.150.d_projected, bf16[256,768]{1,0:T(8,128)(2,1)} %get-tuple-element.151.d_branch, ...), custom_call_target="tpu_custom_call" | custom-call | flops 1 | bytes 1 | tf_op jit(solution)/shard_map/pallas_call | solution.py:447
  348.1 10.7 %shard_map.250 = (bf16[640,2048]{1,0:T(8,128)(2,1)}, f32[320,768]{1,0:T(8,128)}, bf16[320,768]{1,0:T(8,128)(2,1)}) custom-call(bf16[640,768]{1,0:T(8,128)(2,1)} %bitcast.64.d_expert, bf16[768,2048]{1,0:T(8,128)(2,1)} %all-gather.5.cloned.1.call-done.w_gate_up, bf16[1024,768]{1,0:T(8,128)(2,1)} %all-gather.7.cloned.1.call-done.w_down, ...), custom_call_target="tpu_custom_call" | custom-call | flops 1 | bytes 1 | tf_op jit(solution)/shard_map/pallas_call | solution.py:447
  358.9 6.4 %convolution_convert_fusion = bf16[768,2048]{1,0:T(8,128)(2,1)} fusion(bf16[640,768]{1,0:T(8,128)(2,1)} %bitcast.212, bf16[640,2048]{1,0:T(8,128)(2,1)} %get-tuple-element.140), kind=kOutput, calls=%fused_computation.5 | convolution fusion | flops 2014838784 | bytes 6750208 | tf_op jit(solution)/shard_map/dot_general | solution.py:30
  384.1 4.4 all-to-all-start.1
  388.6 13.7 %shard_map.253 = (f32[256,768]{1,0:T(8,128)}, bf16[256,768]{1,0:T(8,128)(2,1)}, bf16[3,256,768]{2,1,0:T(8,128)(2,1)}, f32[2,768]{1,0:T(2,128)}) custom-call(f32[256,768]{1,0:T(8,128)} %get-tuple-element.127.d_result.refs_0_, f32[256,768]{1,0:T(8,128)} %get-tuple-element.132.refs_1_, bf16[320,768]{1,0:T(8,128)(2,1)} %pad_maximum_fusion.13.refs_2_, ...), custom_call_target="tpu_custom_call" | custom-call | flops 1 | bytes 1 | tf_op jit(solution)/shard_map/pallas_call | solution.py:447
  404.3 4.4 all-to-all-done.1
  408.6 7.6 %shard_map.254 = bf16[2,2,4,2,112,768]{5,4,3,2,1,0:T(8,128)(2,1)} custom-call(bf16[256,768]{1,0:T(8,128)(2,1)} %get-tuple-element.163.normed, bf16[256,768]{1,0:T(8,128)(2,1)} %get-tuple-element.164.attended, bf16[3,256,768]{2,1,0:T(8,128)(2,1)} %get-tuple-element.165.d_projected, bf16[256,768]{1,0:T(8,128)(2,1)} %get-tuple-element.168.d_branch, ...), custom_call_target="tpu_custom_call" | custom-call | flops 1 | bytes 1 | tf_op jit(solution)/shard_map/pallas_call | solution.py:447
  445.3 21.2 %collective-permute-done.58 = bf16[2,2,1,224,768]{4,3,1,0,2:T(8,128)(2,1)} collective-permute-done((bf16[2,2,1,224,768]{4,3,1,0,2:T(8,128)(2,1)}, bf16[2,2,1,224,768]{4,3,1,0,2:T(8,128)(2,1)}, u32[]{:S(2)}, u32[]{:S(2)}) %collective-permute-start.58) | collective-permute-done | bytes 1376288 | tf_op jit(solution)/shard_map/ppermute | solution.py:476
  474.5 5.4 all-to-all-done.2
  482.2 14.2 %collective-permute-done.60 = bf16[2,224,768]{2,1,0:T(8,128)(2,1)S(1)} collective-permute-done((bf16[2,224,768]{2,1,0:T(8,128)(2,1)S(1)}, bf16[2,224,768]{2,1,0:T(8,128)(2,1)S(1)}, u32[]{:S(2)}, u32[]{:S(2)}) %collective-permute-start.60) | collective-permute-done | bytes 688160 | tf_op jit(solution)/shard_map/ppermute | solution.py:476
  508.0 21.9 %collective-permute-done.62 = bf16[224,768]{1,0:T(8,128)(2,1)S(1)} collective-permute-done((bf16[224,768]{1,0:T(8,128)(2,1)}, bf16[224,768]{1,0:T(8,128)(2,1)S(1)}, u32[]{:S(2)}, u32[]{:S(2)}) %collective-permute-start.62) | collective-permute-done | bytes 344096 | tf_op jit(solution)/shard_map/ppermute | solution.py:476
  529.9 6.8 %collective-permute-done.63 = bf16[224,768]{1,0:T(8,128)(2,1)} collective-permute-done((bf16[224,768]{1,0:T(8,128)(2,1)}, bf16[224,768]{1,0:T(8,128)(2,1)}, u32[]{:S(2)}, u32[]{:S(2)}) %collective-permute-start.63) | collective-permute-done | bytes 344096 | tf_op jit(solution)/shard_map/ppermute | solution.py:476
  (438 shorter events, 256.2 us)
Async XLA Ops:
  7.2 167.2 %all-gather.7.cloned.1.call-start = ((), (), s32[]{:S(2)}) async-start(), calls=%async_computation.9 | async-start | bytes 1966080 | tf_op jit(solution)/shard_map/all_gather | solution.py:550
  30.3 144.0 %all-gather.5.cloned.1.call-start = ((), (), s32[]{:S(2)}) async-start(), calls=%async_computation.8 | async-start | bytes 3932160 | tf_op jit(solution)/shard_map/all_gather | solution.py:550
  31.7 212.5 %all-gather.11.cloned.1.call-start = ((), (), s32[]{:S(2)}) async-start(), calls=%async_computation.11 | async-start | bytes 1966080 | tf_op jit(solution)/shard_map/all_gather | solution.py:550
  34.1 17.2 %collective-permute-start = (bf16[112,768]{1,0:T(8,128)(2,1)S(1)}, bf16[112,768]{1,0:T(8,128)(2,1)S(1)}, u32[]{:S(2)}, u32[]{:S(2)}) collective-permute-start(bf16[112,768]{1,0:T(8,128)(2,1)S(1)} %get-tuple-element.286), channel_id=1, source_target_pairs={{0,4},{1,5},{2,6},{3,7},{4,8},{5,9},{6,10},{7,11},{8,12},{9,13},{1... | collective-permute-start | bytes 516104 | tf_op jit(solution)/shard_map/ppermute | solution.py:476
  35.7 28.9 %collective-permute-start.1 = (bf16[112,768]{1,0:T(8,128)(2,1)S(1)}, bf16[112,768]{1,0:T(8,128)(2,1)S(1)}, u32[]{:S(2)}, u32[]{:S(2)}) collective-permute-start(bf16[112,768]{1,0:T(8,128)(2,1)S(1)} %get-tuple-element.286), channel_id=1, source_target_pairs={{0,8},{1,9},{2,10},{3,11},{4,12},{5,13},{6,14},{7,15},{8,0},{9,1},... | collective-permute-start | bytes 516104 | tf_op jit(solution)/shard_map/ppermute | solution.py:476
  36.8 31.8 %collective-permute-start.2 = (bf16[112,768]{1,0:T(8,128)(2,1)S(1)}, bf16[112,768]{1,0:T(8,128)(2,1)S(1)}, u32[]{:S(2)}, u32[]{:S(2)}) collective-permute-start(bf16[112,768]{1,0:T(8,128)(2,1)S(1)} %get-tuple-element.286), channel_id=1, source_target_pairs={{0,12},{1,13},{2,14},{3,15},{4,0},{5,1},{6,2},{7,3},{8,4},{9,5},{1... | collective-permute-start | bytes 516104 | tf_op jit(solution)/shard_map/ppermute | solution.py:476
  68.7 17.2 %collective-permute-start.8 = (bf16[4,112,768]{2,1,0:T(8,128)(2,1)S(1)}, bf16[4,112,768]{2,1,0:T(8,128)(2,1)S(1)}, u32[]{:S(2)}, u32[]{:S(2)}) collective-permute-start(bf16[4,112,768]{2,1,0:T(8,128)(2,1)S(1)} %pad_maximum_fusion.8.refs_0_), channel_id=1, source_target_pairs={{0,16},{1,17},{2,18},{3,19},{4,20},{5,21},{6,22},{7,23},{8,24},{9,... | collective-permute-start | bytes 2064392 | tf_op jit(solution)/shard_map/ppermute | solution.py:476
  70.3 17.3 %collective-permute-start.7 = (bf16[4,112,768]{2,1,0:T(8,128)(2,1)S(1)}, bf16[4,112,768]{2,1,0:T(8,128)(2,1)S(1)}, u32[]{:S(2)}, u32[]{:S(2)}) collective-permute-start(bf16[4,112,768]{2,1,0:T(8,128)(2,1)S(1)} %pad_maximum_fusion.8.refs_0_), channel_id=1, source_target_pairs={{0,2},{1,3},{2,0},{3,1},{4,6},{5,7},{6,4},{7,5},{8,10},{9,11},{10,... | collective-permute-start | bytes 2064392 | tf_op jit(solution)/shard_map/ppermute | solution.py:476
  71.8 25.6 %collective-permute-start.11 = (bf16[4,112,768]{2,1,0:T(8,128)(2,1)S(1)}, bf16[4,112,768]{2,1,0:T(8,128)(2,1)}, u32[]{:S(2)}, u32[]{:S(2)}) collective-permute-start(bf16[4,112,768]{2,1,0:T(8,128)(2,1)S(1)} %pad_maximum_fusion.8.refs_0_), channel_id=1, source_target_pairs={{0,1},{1,0},{2,3},{3,2},{4,5},{5,4},{6,7},{7,6},{8,9},{9,8},{10,11... | collective-permute-start | bytes 2064392 | tf_op jit(solution)/shard_map/ppermute | solution.py:476
  127.2 121.8 %all-gather.9.cloned.1.call-start = ((), (), s32[]{:S(2)}) async-start(), calls=%async_computation.10 | async-start | bytes 3932160 | tf_op jit(solution)/shard_map/all_gather | solution.py:550
  146.3 19.7 %collective-permute-start.25 = (bf16[96,768]{1,0:T(8,128)(2,1)S(1)}, bf16[96,768]{1,0:T(8,128)(2,1)S(1)}, u32[]{:S(2)}, u32[]{:S(2)}) collective-permute-start(bf16[96,768]{1,0:T(8,128)(2,1)S(1)} %bitcast.222), channel_id=1, source_target_pairs={{0,8},{1,9},{2,10},{3,11},{4,12},{5,13},{6,14},{7,15},{8,0},{9,1},... | collective-permute-start | bytes 442376 | tf_op jit(solution)/shard_map/ppermute | solution.py:476
  152.9 16.5 %collective-permute-start.26 = (bf16[96,768]{1,0:T(8,128)(2,1)S(1)}, bf16[96,768]{1,0:T(8,128)(2,1)S(1)}, u32[]{:S(2)}, u32[]{:S(2)}) collective-permute-start(bf16[96,768]{1,0:T(8,128)(2,1)S(1)} %bitcast.223), channel_id=1, source_target_pairs={{0,12},{1,13},{2,14},{3,15},{4,0},{5,1},{6,2},{7,3},{8,4},{9,5},{1... | collective-permute-start | bytes 442376 | tf_op jit(solution)/shard_map/ppermute | solution.py:476
  156.7 15.8 %collective-permute-start.19 = (bf16[4,80,768]{2,1,0:T(8,128)(2,1)S(1)}, bf16[4,80,768]{2,1,0:T(8,128)(2,1)}, u32[]{:S(2)}, u32[]{:S(2)}) collective-permute-start(bf16[4,80,768]{2,1,0:T(8,128)(2,1)S(1)} %pad_maximum_fusion.10), channel_id=1, source_target_pairs={{0,1},{1,0},{2,3},{3,2},{4,5},{5,4},{6,7},{7,6},{8,9},{9,8},{10,11... | collective-permute-start | bytes 1474568 | tf_op jit(solution)/shard_map/ppermute | solution.py:476
  169.5 15.0 %collective-permute-start.28 = (bf16[4,96,768]{2,1,0:T(8,128)(2,1)S(1)}, bf16[4,96,768]{2,1,0:T(8,128)(2,1)S(1)}, u32[]{:S(2)}, u32[]{:S(2)}) collective-permute-start(bf16[4,96,768]{2,1,0:T(8,128)(2,1)S(1)} %pad_maximum_fusion.9.refs_0_), channel_id=1, source_target_pairs={{0,16},{1,17},{2,18},{3,19},{4,20},{5,21},{6,22},{7,23},{8,24},{9,... | collective-permute-start | bytes 1769480 | tf_op jit(solution)/shard_map/ppermute | solution.py:476
  171.1 16.1 %collective-permute-start.27 = (bf16[4,96,768]{2,1,0:T(8,128)(2,1)S(1)}, bf16[4,96,768]{2,1,0:T(8,128)(2,1)S(1)}, u32[]{:S(2)}, u32[]{:S(2)}) collective-permute-start(bf16[4,96,768]{2,1,0:T(8,128)(2,1)S(1)} %pad_maximum_fusion.9.refs_0_), channel_id=1, source_target_pairs={{0,2},{1,3},{2,0},{3,1},{4,6},{5,7},{6,4},{7,5},{8,10},{9,11},{10,... | collective-permute-start | bytes 1769480 | tf_op jit(solution)/shard_map/ppermute | solution.py:476
  171.1 167.1 %reduce-scatter.5.cloned.1.call-start = ((), (), s32[]{:S(2)}) async-start(), calls=%async_computation.12 | async-start | bytes 1966080 | tf_op jit(solution)/shard_map/reduce_scatter | solution.py:555
  190.5 16.0 %collective-permute-start.32 = (bf16[4,96,768]{2,1,0:T(8,128)(2,1)S(1)}, bf16[4,96,768]{2,1,0:T(8,128)(2,1)}, u32[]{:S(2)}, u32[]{:S(2)}) collective-permute-start(bf16[4,96,768]{2,1,0:T(8,128)(2,1)S(1)} %collective-permute-done.27.refs_1_), channel_id=1, source_target_pairs={{0,1},{1,0},{2,3},{3,2},{4,5},{5,4},{6,7},{7,6},{8,9},{9,8},{10,11... | collective-permute-start | bytes 1769480 | tf_op jit(solution)/shard_map/ppermute | solution.py:476
  284.1 97.3 %reduce-scatter.7.cloned.1.call-start = ((), (), s32[]{:S(2)}) async-start(), calls=%async_computation.13 | async-start | bytes 3932160 | tf_op jit(solution)/shard_map/reduce_scatter | solution.py:555
  337.7 33.4 %collective-permute-start.56 = (bf16[2,4,2,112,768]{4,3,2,1,0:T(8,128)(2,1)S(1)}, bf16[2,4,2,112,768]{4,3,2,1,0:T(8,128)(2,1)}, u32[]{:S(2)}, u32[]{:S(2)}) collective-permute-start(bf16[2,4,2,112,768]{4,3,2,1,0:T(8,128)(2,1)S(1)} %dynamic-slice_bitcast_fusion.1), channel_id=1, source_target_pairs={{0,1},{1,0},{2,3},{3,2},{4,5},{5,4},{6,7},{7,6},{8,9},{9,8},{10,11... | collective-permute-start | bytes 8257544 | tf_op jit(solution)/shard_map/ppermute | solution.py:476
  340.2 25.0 %all-to-all-start = ((bf16[4,128,768]{2,1,0:T(8,128)(2,1)}), bf16[4,128,768]{2,1,0:T(8,128)(2,1)S(1)}, u32[]{:S(2)}, u32[]{:S(2)}) async-start(bf16[4,128,768]{2,1,0:T(8,128)(2,1)} %pad_maximum_fusion.6), calls=%async_computation.1 | async-start | bytes 1572864 | tf_op jit(solution)/shard_map/all_to_all | solution.py:533
  343.7 95.8 %reduce-scatter.9.cloned.1.call-start = ((), (), s32[]{:S(2)}) async-start(), calls=%async_computation.14 | async-start | bytes 1966080 | tf_op jit(solution)/shard_map/reduce_scatter | solution.py:555
  384.1 24.5 %all-to-all-start.1 = ((bf16[8,48,2048]{2,1,0:T(8,128)(2,1)}), bf16[8,48,2048]{2,1,0:T(8,128)(2,1)}, u32[]{:S(2)}, u32[]{:S(2)}) async-start(bf16[8,48,2048]{2,1,0:T(8,128)(2,1)} %pad_maximum_fusion.1), calls=%async_computation.3 | async-start | bytes 3145728 | tf_op jit(solution)/shard_map/all_to_all | solution.py:533
  388.6 108.6 %reduce-scatter.11.cloned.1.call-start = ((), (), s32[]{:S(2)}) async-start(), calls=%async_computation.15 | async-start | bytes 3932160 | tf_op jit(solution)/shard_map/reduce_scatter | solution.py:555
  433.2 33.3 %collective-permute-start.58 = (bf16[2,2,1,224,768]{4,3,1,0,2:T(8,128)(2,1)}, bf16[2,2,1,224,768]{4,3,1,0,2:T(8,128)(2,1)}, u32[]{:S(2)}, u32[]{:S(2)}) collective-permute-start(bf16[2,2,1,224,768]{4,3,1,0,2:T(8,128)(2,1)} %constant_dynamic-slice_fusion.1), channel_id=1, source_target_pairs={{0,2},{1,3},{2,0},{3,1},{4,6},{5,7},{6,4},{7,5},{8,10},{9,11},{10,... | collective-permute-start | bytes 4128776 | tf_op jit(solution)/shard_map/ppermute | solution.py:476
  439.4 33.4 %collective-permute-start.59 = (bf16[2,2,224,768]{3,2,1,0:T(8,128)(2,1)}, bf16[2,2,224,768]{3,2,1,0:T(8,128)(2,1)}, u32[]{:S(2)}, u32[]{:S(2)}) collective-permute-start(bf16[2,2,224,768]{3,2,1,0:T(8,128)(2,1)} %dynamic-slice_bitcast_fusion.2), channel_id=1, source_target_pairs={{0,16},{1,17},{2,18},{3,19},{4,20},{5,21},{6,22},{7,23},{8,24},{9,... | collective-permute-start | bytes 4128776 | tf_op jit(solution)/shard_map/ppermute | solution.py:476
  441.6 38.3 %all-to-all-start.2 = ((bf16[4,128,768]{2,1,0:T(8,128)(2,1)}), bf16[4,128,768]{2,1,0:T(8,128)(2,1)S(1)}, u32[]{:S(2)}, u32[]{:S(2)}) async-start(bf16[4,128,768]{2,1,0:T(8,128)(2,1)} %pad_maximum_fusion.7), calls=%async_computation.5 | async-start | bytes 1572864 | tf_op jit(solution)/shard_map/all_to_all | solution.py:533
  480.0 16.4 %collective-permute-start.60 = (bf16[2,224,768]{2,1,0:T(8,128)(2,1)S(1)}, bf16[2,224,768]{2,1,0:T(8,128)(2,1)S(1)}, u32[]{:S(2)}, u32[]{:S(2)}) collective-permute-start(bf16[2,224,768]{2,1,0:T(8,128)(2,1)S(1)} %dynamic-slice_bitcast_fusion.3), channel_id=1, source_target_pairs={{0,16},{1,17},{2,18},{3,19},{4,20},{5,21},{6,22},{7,23},{8,24},{9,... | collective-permute-start | bytes 2064392 | tf_op jit(solution)/shard_map/ppermute | solution.py:476
  480.4 16.4 %collective-permute-start.61 = (bf16[2,1,224,768]{3,2,1,0:T(8,128)(2,1)S(1)}, bf16[2,1,224,768]{3,2,1,0:T(8,128)(2,1)S(1)}, u32[]{:S(2)}, u32[]{:S(2)}) collective-permute-start(bf16[2,1,224,768]{3,2,1,0:T(8,128)(2,1)S(1)} %constant_dynamic-slice_fusion), channel_id=1, source_target_pairs={{0,2},{1,3},{2,0},{3,1},{4,6},{5,7},{6,4},{7,5},{8,10},{9,11},{10,... | collective-permute-start | bytes 2064392 | tf_op jit(solution)/shard_map/ppermute | solution.py:476
  499.8 40.0 %all-to-all-start.3 = ((bf16[8,48,2048]{2,1,0:T(8,128)(2,1)}), bf16[8,48,2048]{2,1,0:T(8,128)(2,1)S(1)}, u32[]{:S(2)}, u32[]{:S(2)}) async-start(bf16[8,48,2048]{2,1,0:T(8,128)(2,1)} %pad_maximum_fusion.2), calls=%async_computation.7 | async-start | bytes 3145728 | tf_op jit(solution)/shard_map/all_to_all | solution.py:533
  504.5 25.4 %collective-permute-start.62 = (bf16[224,768]{1,0:T(8,128)(2,1)}, bf16[224,768]{1,0:T(8,128)(2,1)S(1)}, u32[]{:S(2)}, u32[]{:S(2)}) collective-permute-start(bf16[224,768]{1,0:T(8,128)(2,1)} %get-tuple-element.238), channel_id=1, source_target_pairs={{0,4},{1,5},{2,6},{3,7},{4,8},{5,9},{6,10},{7,11},{8,12},{9,13},{1... | collective-permute-start | bytes 1032200 | tf_op jit(solution)/shard_map/ppermute | solution.py:476
  506.5 30.3 %collective-permute-start.63 = (bf16[224,768]{1,0:T(8,128)(2,1)}, bf16[224,768]{1,0:T(8,128)(2,1)}, u32[]{:S(2)}, u32[]{:S(2)}) collective-permute-start(bf16[224,768]{1,0:T(8,128)(2,1)} %get-tuple-element.240), channel_id=1, source_target_pairs={{0,8},{1,9},{2,10},{3,11},{4,12},{5,13},{6,14},{7,15},{8,0},{9,1},... | collective-permute-start | bytes 1032200 | tf_op jit(solution)/shard_map/ppermute | solution.py:476
  508.0 30.5 %collective-permute-start.64 = (bf16[224,768]{1,0:T(8,128)(2,1)}, bf16[224,768]{1,0:T(8,128)(2,1)}, u32[]{:S(2)}, u32[]{:S(2)}) collective-permute-start(bf16[224,768]{1,0:T(8,128)(2,1)} %get-tuple-element.239), channel_id=1, source_target_pairs={{0,12},{1,13},{2,14},{3,15},{4,0},{5,1},{6,2},{7,3},{8,4},{9,5},{1... | collective-permute-start | bytes 1032200 | tf_op jit(solution)/shard_map/ppermute | solution.py:476
  (95 other events, 807.3 us)
Sparse Core Ops, SparseCore 0:
  30.4 46.1 all-gather.6
  78.8 62.2 all-gather.4
  142.7 42.2 all-gather.10
  186.4 62.4 all-gather.8
  284.2 35.1 reduce-scatter.4
  321.6 59.8 reduce-scatter.6
  383.8 34.6 reduce-scatter.8
  420.8 59.8 reduce-scatter.10

commit v5 on v4

--- a/solution.py
+++ b/solution.py
@@ -433,7 +433,11 @@
         rows[...] = value_rows(gates, gather, d_hidden)
 
 
-def call(kernel, outs, args, scratch=(), apart=None):
+def cost(micros):
+    return pl.CostEstimate(flops=0, bytes_accessed=int(micros * 3.6e6), transcendentals=0)
+
+
+def call(kernel, outs, args, scratch=(), apart=None, micros=5):
     specs = [
         pl.BlockSpec(memory_space=pl.ANY) if k == apart else pl.BlockSpec()
         for k in range(len(args))
@@ -450,7 +454,7 @@
         in_specs=specs,
         scratch_shapes=scratch,
         compiler_params=pltpu.CompilerParams(vmem_limit_bytes=60 * 1024 * 1024),
-        cost_estimate=pl.CostEstimate(flops=1, bytes_accessed=1, transcendentals=0),
+        cost_estimate=cost(micros),
     )(*args)
 
 
@@ -617,6 +621,7 @@
             + [pl.BlockSpec(memory_space=pltpu.VMEM)] * len(pieces),
             out_specs=[pl.BlockSpec(memory_space=pltpu.VMEM)] * len(shapes),
             compiler_params=pltpu.CompilerParams(vmem_limit_bytes=60 * 1024 * 1024),
+            cost_estimate=cost(4),
         )(where, *[piece[0] for piece in pieces])
 
     def over_rep(self, block, shift):
@@ -700,6 +705,7 @@
         ],
         out_specs=pl.BlockSpec((EF, rows, columns // parts), lambda _: (0, 0, 0)),
         compiler_params=pltpu.CompilerParams(vmem_limit_bytes=60 * 1024 * 1024),
+        cost_estimate=cost(4),
     )(where, w_gate_up)
 
 
@@ -707,7 +713,7 @@
     count = EF // layout.reps
     mine = layout.quad_exchange(split_gate_up(layout, w_gate_up, layer, where), j)
     mine = mine.reshape(-1, mine.shape[-1])
-    down = lax.dynamic_slice_in_dim(after(w_down[layer], mine), rep * count, count, 0)
+    down = lax.dynamic_slice_in_dim(w_down[layer], rep * count, count, 0)
     down = layout.part_exchange(down, j)
     down = down.reshape(-1, down.shape[-1])
     return layout.line_gather(mine), layout.line_gather(down), down
@@ -739,7 +745,7 @@
                 out[s % 2, r, s // EF, s // 2 % 2, count * slim :] = small_ref[s]
 
     shape = (2, layout.reps, lines, 2, count * slim + ROWS, features)
-    return call(kernel, [(shape, BF16)], (*terms, small), [((2, features, tokens), BF16)])[0]
+    return call(kernel, [(shape, BF16)], (*terms, small), [((2, features, tokens), BF16)], micros=8)[0]
 
 
 def store_layer(kernel, source, block, index, shape, layer, held):
@@ -753,6 +759,7 @@
         out_specs=spec,
         input_output_aliases={} if held is None else {1: 0},
         compiler_params=pltpu.CompilerParams(vmem_limit_bytes=60 * 1024 * 1024),
+        cost_estimate=cost(4),
     )(source, *whole)
 
 
@@ -808,6 +815,7 @@
         + ((d_result,) if last else ()),
         [((tokens, tokens), F32)],
         len(source) + 1,
+        12,
     )
     return found if joined else [source[0], *found]
 
@@ -821,6 +829,7 @@
         + [((EF * CAP, double), F32), ((count - EF * CAP, double), BF16)],
         (rows, w_gate_up, w_down),
         [((count, 2 * min(2 * LANES, units)), F32)],
+        micros=12,
     )
 
 
@@ -832,6 +841,7 @@
         [((count, 2 * units), F32), ((count, units), BF16)]
         + [((EF * CAP, features), F32), ((count - EF * CAP, features), BF16)],
         (inputs, w_gate_up, w_down),
+        micros=10,
     )
 
 
@@ -843,6 +853,7 @@
         [((count, 2 * units), BF16)]
         + [((EF * CAP, features), F32), ((count - EF * CAP, features), BF16)],
         (d_expert, w_gate_up, w_down, gate_up),
+        micros=10,
     )
 
 
@@ -896,16 +907,11 @@
         return full[0].reshape(4, features, features), *full[1:]
 
     line = layout.dense_line(share(0, small))
-    *found, last = expert_weights(layout, w_gate_up, w_down, 0, rep, j, group)
+    *found, last = expert_weights(layout, after(w_gate_up, line), w_down, 0, rep, j, group)
     moe = [found]
     full, small_full = dense_weights(after(line, last))
     small_full = small_full.reshape(layout.shards, -1)
     dense = [full]
-    raw = after(w_gate_up, full)
-    for l in range(1, layers):
-        *found, last = expert_weights(layout, raw, w_down, l, rep, j, group)
-        moe.append(found)
-        raw = after(raw, last)
     packs, vectors, mixing_t = [], [], []
     for l in range(layers):
         part = small_full[:, l * slim * SMALL : (l + 1) * slim * SMALL]
@@ -930,14 +936,15 @@
             shared, packs[l], source, previous, routes[l], gather, grad_out if last else None
         )
         middle, logits, coefs, rows = state[7], state[9], state[10], state[11]
+        inputs = layout.dispatch(rows)
         if last:
-            inputs = layout.dispatch(rows)
             d_gate_up, activated, own, others = expert_both(inputs, *moe[l])
             wide = dot(inputs[:, :features], d_gate_up, ((0,), (0,))).astype(BF16)
             down = dot(activated, inputs[:, features:], ((0,), (0,))).astype(BF16)
         else:
             dense.append(dense_weights(layout.dense_line(after(share(l + 1), rows)))[0])
-            inputs = layout.dispatch(rows)
+            raw = after((w_gate_up, w_down), rows)
+            moe.append(expert_weights(layout, *raw, l + 1, rep, j, group)[:2])
             gate_up, activated, own, others = expert_forward(layout, inputs, *moe[l])
         outputs = layout.collect(own, others)
         if last:
@@ -979,6 +986,7 @@
             [((tokens, LANES), F32), ((tokens, features), F32), ((SMALL - 2, features), F32)],
             (coefs, middle, packs[l][0], scatter, outputs, vectors[l], routes[l], low)
             + (mixing_t[l], grad_hidden, grad_gate),
+            micros=6,
         )
         if last:
             d_rows = outputs
@@ -992,15 +1000,13 @@
             grad_gate_up = dot(inputs, d_gate_up, ((0,), (0,))).astype(BF16)
             d_rows = layout.collect(own, others)
             boths[l + 1] = layout.sum_core(
-                dense_gradients(layout, *after(ready, d_expert), count), j % 2
+                dense_gradients(layout, *after(ready, own), count), j % 2
             )
             grad_down = dot(activated, d_expert, ((0,), (0,))).astype(BF16)
             d_rows, grad_gate_up, grad_down, boths[l + 1], down_out = join(
                 (d_rows, grad_gate_up, grad_down, boths[l + 1], down_out)
             )
             wides[l], downs[l] = layout.line_sum(grad_gate_up), layout.line_sum(grad_down)
-            d_rows, wides[l + 1] = join((d_rows, wides[l + 1]))
-            wide = back_gate_up(wides[l + 1])
         more = () if l == 0 else (kept[l - 1][0][10], pairs[l - 1][0])
         grad_hidden, d_branch, d_projected, gain_grads, *rows = call(
             functools.partial(attention_backward_kernel, l > 0),
@@ -1011,11 +1017,11 @@
             + (*shared, query, keys, values, log_total, *more),
             [((tokens, tokens), F32), ((tokens, features), BF16), ((tokens, features), F32)],
             7,
+            14,
         )
         rows = rows[0] if rows else None
         if not last:
-            d_branch, wide = join((d_branch, wide))
-            gate_up_out = put_gate_up(wide, l + 1, gate_up_out)
+            wide = back_gate_up(after(wides[l + 1], d_branch))
         small_grads = jnp.concatenate([gain_grads, mix_grads]).T.astype(BF16)
         small_grads = small_grads.reshape(layout.shards, slim * SMALL)
         small_grads = jnp.pad(small_grads, ((0, 0), (0, ROWS * features - slim * SMALL)))
@@ -1025,12 +1031,18 @@
         )
 
     boths[0] = layout.sum_core(dense_gradients(layout, *ready, count), j % 2)
-    both, gate_up_out = join((jnp.concatenate(boths, axis=3), gate_up_out))
-    cross, down = join((layout.sum_cross(both, rep, j), back_down(after(downs[0], both))))
-    down_out = put_down(down, 0, down_out)
+    boths[0], wide = join((boths[0], wide))
+    gate_up_out = put_gate_up(wide, 1, gate_up_out)
+    both = jnp.concatenate(boths, axis=3)
+    cross, gate_up_out, down = join(
+        (layout.sum_cross(both, rep, j), gate_up_out, back_down(after(downs[0], both)))
+    )
     line = layout.sum_cross_end(*cross, rep, j)
     line, wides[0] = join((line, wides[0]))
-    line, wide = join((layout.sum_line(line), back_gate_up(wides[0])))
+    down_out = put_down(down, 0, down_out)
+    line, wide, gate_up_out, down_out, result = join(
+        (layout.sum_line(line), back_gate_up(wides[0]), gate_up_out, down_out, result)
+    )
     gate_up_out = put_gate_up(wide, 0, gate_up_out)
     dense_all = layout.rep_gather(line, rep).reshape(layout.reps, layers, -1, features)
     dense_grads = jnp.swapaxes(dense_all, 0, 1)

time: 577 us -> 551 us (0.955)
  waiting for transfers between devices: 212 us -> 182 us
  starting transfers between devices: 72 us -> 78.1 us
    ppermute x66, waiting for transfers between devices: 195 us -> 160 us  [send(): return lax.ppermute(x, AXES, self.pairs(move))]
    all_to_all x4, waiting for transfers between devices: 9.79 us -> 19.3 us  [trade(): lax.all_to_all(blocks, AXES, 0, 0, axis_index_groups=groups, tiled=True)]
    ppermute x66, starting transfers between devices: 56.4 us -> 62.4 us  [send(): return lax.ppermute(x, AXES, self.pairs(move))]
    unnamed x133 -> x151, local copies, waits for them, and re-layouts: 21.2 us -> 23.7 us
  transfers between devices with their start and end apart: 78 -> 78, of which waited for: 42 -> 34; matrix products, arithmetic and copies ran while one was open for 18% -> 19% of each run, Pallas kernels for 23% -> 25%
where the time goes in v5:
time: 551 us; the launch traced here: 542 us
  waiting for transfers between devices  182 us (33%)
  Pallas kernels  146 us (26%)
  starting transfers between devices  78.1 us (14%)
  local copies, waits for them, and re-layouts  58.1 us (11%)
  other arithmetic  43.3 us (8%)
  matrix products  18.1 us (3%)
  between operations  16 us (3%)
    ppermute x66, waiting for transfers between devices, send(): return lax.ppermute(x, AXES, self.pairs(move))  160 us
    pallas_call x12, Pallas kernels, call(): pl.pallas_call(kernel, out_shape=[jax.ShapeDtypeStruct(shape, dtype) for...  116 us
    ppermute x66, starting transfers between devices, send(): return lax.ppermute(x, AXES, self.pairs(move))  62.4 us
    unnamed x151, local copies, waits for them, and re-layouts  23.7 us
    all_to_all x4, waiting for transfers between devices, trade(): lax.all_to_all(blocks, AXES, 0, 0, axis_index_groups=groups, tiled=True)  19.3 us
    dot_general x4, matrix products, dot(): return lax.dot_general(a, b, (dims, ((), ())), preferred_element_type=F32)  18.1 us
    all_to_all x4, starting transfers between devices, trade(): lax.all_to_all(blocks, AXES, 0, 0, axis_index_groups=groups, tiled=True)  15.4 us
    pallas_call x4, Pallas kernels, store_layer(): pl.pallas_call((lambda x, o: kernel(x, o)) if held is None else lambda x,...  14.7 us
  transfers between devices with their start and end apart: 78, of which 34 were waited for; matrix products, arithmetic and copies ran while one was open for 19% of the time, Pallas kernels for 25%

profile of v5, /device:TPU:8, one launch (start us, length us, event | category | flops | bytes accessed | tf_op | source)
XLA Modules:
  0.0 541.7 jit_solution(17358630367455696879)
XLA Ops:
  21.7 13.7 %collective-permute-done = bf16[112,768]{1,0:T(8,128)(2,1)S(1)} collective-permute-done((bf16[112,768]{1,0:T(8,128)(2,1)S(1)}, bf16[112,768]{1,0:T(8,128)(2,1)S(1)}, u32[]{:S(2)}, u32[]{:S(2)}) %collective-permute-start) | collective-permute-done | bytes 172064 | tf_op jit(solution)/shard_map/ppermute | solution.py:480
  35.5 11.1 %collective-permute-done.1 = bf16[112,768]{1,0:T(8,128)(2,1)S(1)} collective-permute-done((bf16[112,768]{1,0:T(8,128)(2,1)S(1)}, bf16[112,768]{1,0:T(8,128)(2,1)S(1)}, u32[]{:S(2)}, u32[]{:S(2)}) %collective-permute-start.1) | collective-permute-done | bytes 172064 | tf_op jit(solution)/shard_map/ppermute | solution.py:480
  54.8 5.9 %collective-permute-done.18 = bf16[1,48,2048]{2,1,0:T(8,128)(2,1)S(1)} collective-permute-done((bf16[1,48,2048]{2,1,0:T(8,128)(2,1)S(1)}, bf16[1,48,2048]{2,1,0:T(8,128)(2,1)S(1)}, u32[]{:S(2)}, u32[]{:S(2)}) %collective-permute-start.18) | collective-permute-done | bytes 196640 | tf_op jit(solution)/shard_map/ppermute | solution.py:480
  70.1 12.6 %collective-permute-done.5.refs_2_ = bf16[4,112,768]{2,1,0:T(8,128)(2,1)S(1)} collective-permute-done((bf16[4,112,768]{2,1,0:T(8,128)(2,1)S(1)}, bf16[4,112,768]{2,1,0:T(8,128)(2,1)S(1)}, u32[]{:S(2)}, u32[]{:S(2)}) %collective-permute-start.5) | collective-permute-done | bytes 688160 | tf_op jit(solution)/shard_map/ppermute | solution.py:480
  96.2 5.2 shard_map.238
  105.3 12.4 %shard_map.239 = (bf16[256,768]{1,0:T(8,128)(2,1)}, bf16[256,768]{1,0:T(8,128)(2,1)}, bf16[256,768]{1,0:T(8,128)(2,1)}, bf16[256,768]{1,0:T(8,128)(2,1)}, f32[25...) custom-call(bf16[256,768]{1,0:T(8,128)(2,1)} %refs_5_.1, ...), custom_call_target="tpu_custom_call" | custom-call | bytes 43200000 | tf_op jit(solution)/shard_map/pallas_call | solution.py:451
  119.2 5.8 %collective-permute-done.43 = bf16[1,128,768]{2,1,0:T(8,128)(2,1)S(1)} collective-permute-done((bf16[1,128,768]{2,1,0:T(8,128)(2,1)S(1)}, bf16[1,128,768]{2,1,0:T(8,128)(2,1)S(1)}, u32[]{:S(2)}, u32[]{:S(2)}) %collective-permute-start.43) | collective-permute-done | bytes 196640 | tf_op jit(solution)/shard_map/ppermute | solution.py:480
  157.3 10.0 %shard_map.241 = (f32[640,2048]{1,0:T(8,128)}, bf16[640,1024]{1,0:T(8,128)(2,1)}, f32[320,768]{1,0:T(8,128)}, bf16[320,768]{1,0:T(8,128)(2,1)}) custom-call(bf16[640,768]{1,0:T(8,128)(2,1)} %bitcast.37.inputs, bf16[768,2048]{1,0:T(8,128)(2,1)} %all-gather.5.cloned.1.call-done.w_gate_up, bf16[1024,768]{1,0:T(8,128)(2,1)} %all-gather.7.cloned.1.call-done.w_down), custom_call_target="tpu_custom_call" | custom-call | bytes 36000000 | tf_op jit(solution)/shard_map/pallas_call | solution.py:451
  175.0 3.9 collective-permute-done.29.refs_3_
  190.0 4.9 shard_map.242
  195.7 13.0 %shard_map.243 = (f32[256,768]{1,0:T(8,128)}, bf16[256,768]{1,0:T(8,128)(2,1)}, bf16[256,768]{1,0:T(8,128)(2,1)}, bf16[256,768]{1,0:T(8,128)(2,1)}, bf16[256,768...) custom-call(f32[256,128]{1,0:T(8,128)} %get-tuple-element.105.refs_0, ...), custom_call_target="tpu_custom_call" | custom-call | bytes 43200000 | tf_op jit(solution)/shard_map/pallas_call | solution.py:451
  220.2 4.0 collective-permute-done.38
  229.1 12.3 %shard_map.245 = (bf16[640,2048]{1,0:T(8,128)(2,1)}, bf16[640,1024]{1,0:T(8,128)(2,1)}, f32[320,1536]{1,0:T(8,128)}, bf16[320,1536]{1,0:T(8,128)(2,1)}) custom-call(bf16[640,1536]{1,0:T(8,128)(2,1)} %bitcast.210, bf16[768,2048]{1,0:T(8,128)(2,1)} %all-gather.9.cloned.1.call-done.w_gate_up, bf16[1024,768]{1,0:T(8,128)(2,1)} %all-gather.11.cloned.1.call-done.w_down), custom_call_target="tpu_custom_call" | custom-call | bytes 43200000 | tf_op jit(solution)/shard_map/pallas_call | solution.py:451
  241.5 6.5 %convolution_convert_fusion.1 = bf16[768,2048]{1,0:T(8,128)(2,1)} fusion(bf16[640,2048]{1,0:T(8,128)(2,1)} %get-tuple-element.120, bf16[640,1536]{1,0:T(8,128)(2,1)} %bitcast.211), kind=kOutput, calls=%fused_computation.5 | convolution fusion | flops 2014838784 | bytes 6750208 | tf_op jit(solution)/shard_map/dot_general | solution.py:30
  258.7 4.5 collective-permute-done.47
  268.5 5.9 %shard_map.246 = (f32[256,128]{1,0:T(8,128)}, f32[256,768]{1,0:T(8,128)}, f32[14,768]{1,0:T(8,128)}) custom-call(f32[256,128]{1,0:T(8,128)} %get-tuple-element.113.coefs, f32[256,768]{1,0:T(8,128)} %get-tuple-element.114.middle.refs_4_, f32[2,768]{1,0:T(2,128)} %bitcast.250, bf16[2,256,320]{2,1,0:T(8,128)(2,1)} %fusion.8.scatter.refs_3_, ...), custom_call_target="tpu_custom_call" | custom-call | bytes 21600000 | tf_op jit(solution)/shard_map/pallas_call | solution.py:451
  274.4 14.2 %shard_map.247 = (f32[256,768]{1,0:T(8,128)}, bf16[256,768]{1,0:T(8,128)(2,1)}, bf16[3,256,768]{2,1,0:T(8,128)(2,1)}, f32[2,768]{1,0:T(2,128)}, bf16[320,768]{1,0:T(8,128)(2,1)}) custom-call(f32[256,768]{1,0:T(8,128)} %refs_0_.3, f32[256,768]{1,0:T(8,128)} %get-tuple-element.124.refs_1_, bf16[320,1536]{1,0:T(8,128)(2,1)} %pad_maximum_fusion.4.outputs.refs_2_, ...), custom_call_target="tpu_custom_call" | custom-call | bytes 50400000 | tf_op jit(solution)/shard_map/pallas_call | solution.py:451
  293.3 5.7 %shard_map.248 = (f32[256,128]{1,0:T(8,128)}, f32[256,768]{1,0:T(8,128)}, f32[14,768]{1,0:T(8,128)}) custom-call(f32[256,128]{1,0:T(8,128)} %get-tuple-element.105.refs_0_.refs_16_.coefs, f32[256,768]{1,0:T(8,128)} %get-tuple-element.106.refs_1_.middle.refs_4_, f32[2,768]{1,0:T(2,128)} %bitcast.255, bf16[2,256,320]{2,1,0:T(8,128)(2,1)} %fusion.7.refs_3_.scatter, ...), custom_call_target="tpu_custom_call" | custom-call | bytes 21600000 | tf_op jit(solution)/shard_map/pallas_call | solution.py:451
  309.5 10.6 %shard_map.249 = (bf16[640,2048]{1,0:T(8,128)(2,1)}, f32[320,768]{1,0:T(8,128)}, bf16[320,768]{1,0:T(8,128)(2,1)}) custom-call(bf16[640,768]{1,0:T(8,128)(2,1)} %bitcast.219, bf16[768,2048]{1,0:T(8,128)(2,1)} %all-gather.5.cloned.1.call-done.w_gate_up, bf16[1024,768]{1,0:T(8,128)(2,1)} %all-gather.7.cloned.1.call-done.w_down, ...), custom_call_target="tpu_custom_call" | custom-call | bytes 36000000 | tf_op jit(solution)/shard_map/pallas_call | solution.py:451
  320.1 8.0 %shard_map.250 = bf16[2,2,4,2,112,768]{5,4,3,2,1,0:T(8,128)(2,1)} custom-call(bf16[256,768]{1,0:T(8,128)(2,1)} %get-tuple-element.151.normed, bf16[256,768]{1,0:T(8,128)(2,1)} %get-tuple-element.152.attended, bf16[3,256,768]{2,1,0:T(8,128)(2,1)} %get-tuple-element.153.d_projected, bf16[256,768]{1,0:T(8,128)(2,1)} %get-tuple-element.154.d_branch, ...), custom_call_target="tpu_custom_call" | custom-call | bytes 28800000 | tf_op jit(solution)/shard_map/pallas_call | solution.py:451
  330.6 6.4 %convolution_convert_fusion = bf16[768,2048]{1,0:T(8,128)(2,1)} fusion(bf16[640,768]{1,0:T(8,128)(2,1)} %bitcast.37.inputs, bf16[640,2048]{1,0:T(8,128)(2,1)} %get-tuple-element.143), kind=kOutput, calls=%fused_computation.4 | convolution fusion | flops 2014838784 | bytes 6750208 | tf_op jit(solution)/shard_map/dot_general | solution.py:30
  353.3 13.4 %shard_map.252 = (f32[256,768]{1,0:T(8,128)}, bf16[256,768]{1,0:T(8,128)(2,1)}, bf16[3,256,768]{2,1,0:T(8,128)(2,1)}, f32[2,768]{1,0:T(2,128)}) custom-call(f32[256,768]{1,0:T(8,128)} %get-tuple-element.130.d_result.refs_0_, f32[256,768]{1,0:T(8,128)} %get-tuple-element.135.refs_1_, bf16[320,768]{1,0:T(8,128)(2,1)} %pad_maximum_fusion.12.refs_2_, ...), custom_call_target="tpu_custom_call" | custom-call | bytes 50400000 | tf_op jit(solution)/shard_map/pallas_call | solution.py:451
  368.7 7.7 %shard_map.253 = bf16[2,2,4,2,112,768]{5,4,3,2,1,0:T(8,128)(2,1)} custom-call(bf16[256,768]{1,0:T(8,128)(2,1)} %get-tuple-element.103.normed, bf16[256,768]{1,0:T(8,128)(2,1)} %get-tuple-element.104.attended, bf16[3,256,768]{2,1,0:T(8,128)(2,1)} %get-tuple-element.162.d_projected, bf16[256,768]{1,0:T(8,128)(2,1)} %get-tuple-element.163.d_branch, ...), custom_call_target="tpu_custom_call" | custom-call | bytes 28800000 | tf_op jit(solution)/shard_map/pallas_call | solution.py:451
  382.7 4.6 all-to-all-start.1
  387.3 4.9 fusion
  392.2 15.5 %all-to-all-done.1 = bf16[8,48,2048]{2,1,0:T(8,128)(2,1)} async-done(((bf16[8,48,2048]{2,1,0:T(8,128)(2,1)}), bf16[8,48,2048]{2,1,0:T(8,128)(2,1)}, u32[]{:S(2)}, u32[]{:S(2)}) %all-to-all-start.1) | async-done | bytes 1572896 | tf_op jit(solution)/shard_map/all_to_all | solution.py:537
  422.5 3.9 shard_map.254.h
  426.4 20.3 %collective-permute-done.58 = bf16[2,2,1,224,768]{4,3,1,0,2:T(8,128)(2,1)} collective-permute-done((bf16[2,2,1,224,768]{4,3,1,0,2:T(8,128)(2,1)}, bf16[2,2,1,224,768]{4,3,1,0,2:T(8,128)(2,1)}, u32[]{:S(2)}, u32[]{:S(2)}) %collective-permute-start.58) | collective-permute-done | bytes 1376288 | tf_op jit(solution)/shard_map/ppermute | solution.py:480
  452.6 3.7 all-to-all-done.2
  460.3 13.7 %collective-permute-done.60 = bf16[2,224,768]{2,1,0:T(8,128)(2,1)S(1)} collective-permute-done((bf16[2,224,768]{2,1,0:T(8,128)(2,1)S(1)}, bf16[2,224,768]{2,1,0:T(8,128)(2,1)S(1)}, u32[]{:S(2)}, u32[]{:S(2)}) %collective-permute-start.60) | collective-permute-done | bytes 688160 | tf_op jit(solution)/shard_map/ppermute | solution.py:480
  495.3 20.6 %collective-permute-done.63 = bf16[224,768]{1,0:T(8,128)(2,1)} collective-permute-done((bf16[224,768]{1,0:T(8,128)(2,1)}, bf16[224,768]{1,0:T(8,128)(2,1)}, u32[]{:S(2)}, u32[]{:S(2)}) %collective-permute-start.63) | collective-permute-done | bytes 344096 | tf_op jit(solution)/shard_map/ppermute | solution.py:480
  524.2 3.9 shard_map.257
  (456 shorter events, 237.0 us)
Async XLA Ops:
  7.2 150.1 %all-gather.7.cloned.1.call-start = ((), (), s32[]{:S(2)}) async-start(), calls=%async_computation.9 | async-start | bytes 1966080 | tf_op jit(solution)/shard_map/all_gather | solution.py:554
  16.1 141.2 %all-gather.5.cloned.1.call-start = ((), (), s32[]{:S(2)}) async-start(), calls=%async_computation.8 | async-start | bytes 3932160 | tf_op jit(solution)/shard_map/all_gather | solution.py:554
  17.1 18.4 %collective-permute-start = (bf16[112,768]{1,0:T(8,128)(2,1)S(1)}, bf16[112,768]{1,0:T(8,128)(2,1)S(1)}, u32[]{:S(2)}, u32[]{:S(2)}) collective-permute-start(bf16[112,768]{1,0:T(8,128)(2,1)S(1)} %get-tuple-element.284), channel_id=1, source_target_pairs={{0,4},{1,5},{2,6},{3,7},{4,8},{5,9},{6,10},{7,11},{8,12},{9,13},{1... | collective-permute-start | bytes 516104 | tf_op jit(solution)/shard_map/ppermute | solution.py:480
  18.7 27.8 %collective-permute-start.1 = (bf16[112,768]{1,0:T(8,128)(2,1)S(1)}, bf16[112,768]{1,0:T(8,128)(2,1)S(1)}, u32[]{:S(2)}, u32[]{:S(2)}) collective-permute-start(bf16[112,768]{1,0:T(8,128)(2,1)S(1)} %get-tuple-element.284), channel_id=1, source_target_pairs={{0,8},{1,9},{2,10},{3,11},{4,12},{5,13},{6,14},{7,15},{8,0},{9,1},... | collective-permute-start | bytes 516104 | tf_op jit(solution)/shard_map/ppermute | solution.py:480
  19.8 28.9 %collective-permute-start.2 = (bf16[112,768]{1,0:T(8,128)(2,1)S(1)}, bf16[112,768]{1,0:T(8,128)(2,1)S(1)}, u32[]{:S(2)}, u32[]{:S(2)}) collective-permute-start(bf16[112,768]{1,0:T(8,128)(2,1)S(1)} %get-tuple-element.284), channel_id=1, source_target_pairs={{0,12},{1,13},{2,14},{3,15},{4,0},{5,1},{6,2},{7,3},{8,4},{9,5},{1... | collective-permute-start | bytes 516104 | tf_op jit(solution)/shard_map/ppermute | solution.py:480
  65.0 162.1 %all-gather.11.cloned.1.call-start = ((), (), s32[]{:S(2)}) async-start(), calls=%async_computation.11 | async-start | bytes 1966080 | tf_op jit(solution)/shard_map/all_gather | solution.py:554
  65.0 17.7 %collective-permute-start.5 = (bf16[4,112,768]{2,1,0:T(8,128)(2,1)S(1)}, bf16[4,112,768]{2,1,0:T(8,128)(2,1)S(1)}, u32[]{:S(2)}, u32[]{:S(2)}) collective-permute-start(bf16[4,112,768]{2,1,0:T(8,128)(2,1)S(1)} %pad_maximum_fusion.7.refs_0_), channel_id=1, source_target_pairs={{0,16},{1,17},{2,18},{3,19},{4,20},{5,21},{6,22},{7,23},{8,24},{9,... | collective-permute-start | bytes 2064392 | tf_op jit(solution)/shard_map/ppermute | solution.py:480
  66.4 17.8 %collective-permute-start.4 = (bf16[4,112,768]{2,1,0:T(8,128)(2,1)S(1)}, bf16[4,112,768]{2,1,0:T(8,128)(2,1)S(1)}, u32[]{:S(2)}, u32[]{:S(2)}) collective-permute-start(bf16[4,112,768]{2,1,0:T(8,128)(2,1)S(1)} %pad_maximum_fusion.7.refs_0_), channel_id=1, source_target_pairs={{0,2},{1,3},{2,0},{3,1},{4,6},{5,7},{6,4},{7,5},{8,10},{9,11},{10,... | collective-permute-start | bytes 2064392 | tf_op jit(solution)/shard_map/ppermute | solution.py:480
  70.1 24.8 %collective-permute-start.8 = (bf16[4,112,768]{2,1,0:T(8,128)(2,1)S(1)}, bf16[4,112,768]{2,1,0:T(8,128)(2,1)}, u32[]{:S(2)}, u32[]{:S(2)}) collective-permute-start(bf16[4,112,768]{2,1,0:T(8,128)(2,1)S(1)} %pad_maximum_fusion.7.refs_0_), channel_id=1, source_target_pairs={{0,1},{1,0},{2,3},{3,2},{4,5},{5,4},{6,7},{7,6},{8,9},{9,8},{10,11... | collective-permute-start | bytes 2064392 | tf_op jit(solution)/shard_map/ppermute | solution.py:480
  125.7 103.4 %all-gather.9.cloned.1.call-start = ((), (), s32[]{:S(2)}) async-start(), calls=%async_computation.10 | async-start | bytes 3932160 | tf_op jit(solution)/shard_map/all_gather | solution.py:554
  125.8 20.0 %collective-permute-start.24 = (bf16[96,768]{1,0:T(8,128)(2,1)S(1)}, bf16[96,768]{1,0:T(8,128)(2,1)S(1)}, u32[]{:S(2)}, u32[]{:S(2)}) collective-permute-start(bf16[96,768]{1,0:T(8,128)(2,1)S(1)} %bitcast.229), channel_id=1, source_target_pairs={{0,4},{1,5},{2,6},{3,7},{4,8},{5,9},{6,10},{7,11},{8,12},{9,13},{1... | collective-permute-start | bytes 442376 | tf_op jit(solution)/shard_map/ppermute | solution.py:480
  125.9 19.9 %collective-permute-start.25 = (bf16[96,768]{1,0:T(8,128)(2,1)S(1)}, bf16[96,768]{1,0:T(8,128)(2,1)S(1)}, u32[]{:S(2)}, u32[]{:S(2)}) collective-permute-start(bf16[96,768]{1,0:T(8,128)(2,1)S(1)} %bitcast.230), channel_id=1, source_target_pairs={{0,8},{1,9},{2,10},{3,11},{4,12},{5,13},{6,14},{7,15},{8,0},{9,1},... | collective-permute-start | bytes 442376 | tf_op jit(solution)/shard_map/ppermute | solution.py:480
  128.5 18.3 %collective-permute-start.26 = (bf16[96,768]{1,0:T(8,128)(2,1)S(1)}, bf16[96,768]{1,0:T(8,128)(2,1)S(1)}, u32[]{:S(2)}, u32[]{:S(2)}) collective-permute-start(bf16[96,768]{1,0:T(8,128)(2,1)S(1)} %bitcast.231), channel_id=1, source_target_pairs={{0,12},{1,13},{2,14},{3,15},{4,0},{5,1},{6,2},{7,3},{8,4},{9,5},{1... | collective-permute-start | bytes 442376 | tf_op jit(solution)/shard_map/ppermute | solution.py:480
  147.0 21.9 %collective-permute-start.28 = (bf16[4,96,768]{2,1,0:T(8,128)(2,1)S(1)}, bf16[4,96,768]{2,1,0:T(8,128)(2,1)S(1)}, u32[]{:S(2)}, u32[]{:S(2)}) collective-permute-start(bf16[4,96,768]{2,1,0:T(8,128)(2,1)S(1)} %pad_maximum_fusion.8.refs_0_), channel_id=1, source_target_pairs={{0,16},{1,17},{2,18},{3,19},{4,20},{5,21},{6,22},{7,23},{8,24},{9,... | collective-permute-start | bytes 1769480 | tf_op jit(solution)/shard_map/ppermute | solution.py:480
  148.5 22.2 %collective-permute-start.27 = (bf16[4,96,768]{2,1,0:T(8,128)(2,1)S(1)}, bf16[4,96,768]{2,1,0:T(8,128)(2,1)S(1)}, u32[]{:S(2)}, u32[]{:S(2)}) collective-permute-start(bf16[4,96,768]{2,1,0:T(8,128)(2,1)S(1)} %pad_maximum_fusion.8.refs_0_), channel_id=1, source_target_pairs={{0,2},{1,3},{2,0},{3,1},{4,6},{5,7},{6,4},{7,5},{8,10},{9,11},{10,... | collective-permute-start | bytes 1769480 | tf_op jit(solution)/shard_map/ppermute | solution.py:480
  154.1 148.0 %reduce-scatter.5.cloned.1.call-start = ((), (), s32[]{:S(2)}) async-start(), calls=%async_computation.12 | async-start | bytes 1966080 | tf_op jit(solution)/shard_map/reduce_scatter | solution.py:559
  167.3 13.2 %collective-permute-start.20 = (bf16[320,768]{1,0:T(8,128)(2,1)}, bf16[320,768]{1,0:T(8,128)(2,1)S(1)}, u32[]{:S(2)}, u32[]{:S(2)}) collective-permute-start(bf16[320,768]{1,0:T(8,128)(2,1)} %get-tuple-element.110), channel_id=1, source_target_pairs={{0,1},{1,0},{2,3},{3,2},{4,5},{5,4},{6,7},{7,6},{8,9},{9,8},{10,11... | collective-permute-start | bytes 1474568 | tf_op jit(solution)/shard_map/ppermute | solution.py:480
  174.4 15.5 %collective-permute-start.32 = (bf16[4,96,768]{2,1,0:T(8,128)(2,1)S(1)}, bf16[4,96,768]{2,1,0:T(8,128)(2,1)}, u32[]{:S(2)}, u32[]{:S(2)}) collective-permute-start(bf16[4,96,768]{2,1,0:T(8,128)(2,1)S(1)} %collective-permute-done.27.refs_1_), channel_id=1, source_target_pairs={{0,1},{1,0},{2,3},{3,2},{4,5},{5,4},{6,7},{7,6},{8,9},{9,8},{10,11... | collective-permute-start | bytes 1769480 | tf_op jit(solution)/shard_map/ppermute | solution.py:480
  264.2 115.7 %reduce-scatter.7.cloned.1.call-start = ((), (), s32[]{:S(2)}) async-start(), calls=%async_computation.13 | async-start | bytes 3932160 | tf_op jit(solution)/shard_map/reduce_scatter | solution.py:559
  304.5 15.6 %all-to-all-start = ((bf16[4,128,768]{2,1,0:T(8,128)(2,1)}), bf16[4,128,768]{2,1,0:T(8,128)(2,1)S(1)}, u32[]{:S(2)}, u32[]{:S(2)}) async-start(bf16[4,128,768]{2,1,0:T(8,128)(2,1)} %pad_maximum_fusion.5), calls=%async_computation.1 | async-start | bytes 1572864 | tf_op jit(solution)/shard_map/all_to_all | solution.py:537
  308.2 108.7 %reduce-scatter.9.cloned.1.call-start = ((), (), s32[]{:S(2)}) async-start(), calls=%async_computation.14 | async-start | bytes 1966080 | tf_op jit(solution)/shard_map/reduce_scatter | solution.py:559
  330.0 19.9 %collective-permute-start.56 = (bf16[2,4,2,112,768]{4,3,2,1,0:T(8,128)(2,1)S(1)}, bf16[2,4,2,112,768]{4,3,2,1,0:T(8,128)(2,1)}, u32[]{:S(2)}, u32[]{:S(2)}) collective-permute-start(bf16[2,4,2,112,768]{4,3,2,1,0:T(8,128)(2,1)S(1)} %dynamic-slice_bitcast_fusion.1), channel_id=1, source_target_pairs={{0,1},{1,0},{2,3},{3,2},{4,5},{5,4},{6,7},{7,6},{8,9},{9,8},{10,11... | collective-permute-start | bytes 8257544 | tf_op jit(solution)/shard_map/ppermute | solution.py:480
  353.2 123.1 %reduce-scatter.11.cloned.1.call-start = ((), (), s32[]{:S(2)}) async-start(), calls=%async_computation.15 | async-start | bytes 3932160 | tf_op jit(solution)/shard_map/reduce_scatter | solution.py:559
  382.7 25.1 %all-to-all-start.1 = ((bf16[8,48,2048]{2,1,0:T(8,128)(2,1)}), bf16[8,48,2048]{2,1,0:T(8,128)(2,1)}, u32[]{:S(2)}, u32[]{:S(2)}) async-start(bf16[8,48,2048]{2,1,0:T(8,128)(2,1)} %pad_maximum_fusion), calls=%async_computation.3 | async-start | bytes 3145728 | tf_op jit(solution)/shard_map/all_to_all | solution.py:537
  413.3 33.4 %collective-permute-start.58 = (bf16[2,2,1,224,768]{4,3,1,0,2:T(8,128)(2,1)}, bf16[2,2,1,224,768]{4,3,1,0,2:T(8,128)(2,1)}, u32[]{:S(2)}, u32[]{:S(2)}) collective-permute-start(bf16[2,2,1,224,768]{4,3,1,0,2:T(8,128)(2,1)} %dynamic-slice_bitcast_fusion.3), channel_id=1, source_target_pairs={{0,2},{1,3},{2,0},{3,1},{4,6},{5,7},{6,4},{7,5},{8,10},{9,11},{10,... | collective-permute-start | bytes 4128776 | tf_op jit(solution)/shard_map/ppermute | solution.py:480
  415.9 33.9 %collective-permute-start.59 = (bf16[2,2,224,768]{3,2,1,0:T(8,128)(2,1)}, bf16[2,2,224,768]{3,2,1,0:T(8,128)(2,1)}, u32[]{:S(2)}, u32[]{:S(2)}) collective-permute-start(bf16[2,2,224,768]{3,2,1,0:T(8,128)(2,1)} %dynamic-slice_bitcast_fusion.2), channel_id=1, source_target_pairs={{0,16},{1,17},{2,18},{3,19},{4,20},{5,21},{6,22},{7,23},{8,24},{9,... | collective-permute-start | bytes 4128776 | tf_op jit(solution)/shard_map/ppermute | solution.py:480
  419.0 37.4 %all-to-all-start.2 = ((bf16[4,128,768]{2,1,0:T(8,128)(2,1)}), bf16[4,128,768]{2,1,0:T(8,128)(2,1)S(1)}, u32[]{:S(2)}, u32[]{:S(2)}) async-start(bf16[4,128,768]{2,1,0:T(8,128)(2,1)} %pad_maximum_fusion.6), calls=%async_computation.5 | async-start | bytes 1572864 | tf_op jit(solution)/shard_map/all_to_all | solution.py:537
  457.8 16.3 %collective-permute-start.60 = (bf16[2,224,768]{2,1,0:T(8,128)(2,1)S(1)}, bf16[2,224,768]{2,1,0:T(8,128)(2,1)S(1)}, u32[]{:S(2)}, u32[]{:S(2)}) collective-permute-start(bf16[2,224,768]{2,1,0:T(8,128)(2,1)S(1)} %dynamic-slice_bitcast_fusion.4), channel_id=1, source_target_pairs={{0,16},{1,17},{2,18},{3,19},{4,20},{5,21},{6,22},{7,23},{8,24},{9,... | collective-permute-start | bytes 2064392 | tf_op jit(solution)/shard_map/ppermute | solution.py:480
  460.0 16.0 %collective-permute-start.61 = (bf16[2,1,224,768]{3,2,1,0:T(8,128)(2,1)S(1)}, bf16[2,1,224,768]{3,2,1,0:T(8,128)(2,1)S(1)}, u32[]{:S(2)}, u32[]{:S(2)}) collective-permute-start(bf16[2,1,224,768]{3,2,1,0:T(8,128)(2,1)S(1)} %constant_dynamic-slice_fusion), channel_id=1, source_target_pairs={{0,2},{1,3},{2,0},{3,1},{4,6},{5,7},{6,4},{7,5},{8,10},{9,11},{10,... | collective-permute-start | bytes 2064392 | tf_op jit(solution)/shard_map/ppermute | solution.py:480
  479.1 40.7 %all-to-all-start.3 = ((bf16[8,48,2048]{2,1,0:T(8,128)(2,1)}), bf16[8,48,2048]{2,1,0:T(8,128)(2,1)S(1)}, u32[]{:S(2)}, u32[]{:S(2)}) async-start(bf16[8,48,2048]{2,1,0:T(8,128)(2,1)} %pad_maximum_fusion.1), calls=%async_computation.7 | async-start | bytes 3145728 | tf_op jit(solution)/shard_map/all_to_all | solution.py:537
  485.6 30.3 %collective-permute-start.63 = (bf16[224,768]{1,0:T(8,128)(2,1)}, bf16[224,768]{1,0:T(8,128)(2,1)}, u32[]{:S(2)}, u32[]{:S(2)}) collective-permute-start(bf16[224,768]{1,0:T(8,128)(2,1)} %get-tuple-element.242), channel_id=1, source_target_pairs={{0,8},{1,9},{2,10},{3,11},{4,12},{5,13},{6,14},{7,15},{8,0},{9,1},... | collective-permute-start | bytes 1032200 | tf_op jit(solution)/shard_map/ppermute | solution.py:480
  488.6 29.9 %collective-permute-start.64 = (bf16[224,768]{1,0:T(8,128)(2,1)}, bf16[224,768]{1,0:T(8,128)(2,1)}, u32[]{:S(2)}, u32[]{:S(2)}) collective-permute-start(bf16[224,768]{1,0:T(8,128)(2,1)} %get-tuple-element.241), channel_id=1, source_target_pairs={{0,12},{1,13},{2,14},{3,15},{4,0},{5,1},{6,2},{7,3},{8,4},{9,5},{1... | collective-permute-start | bytes 1032200 | tf_op jit(solution)/shard_map/ppermute | solution.py:480
  (103 other events, 848.8 us)
Sparse Core Ops, SparseCore 0:
  16.2 42.8 all-gather.6
  65.1 62.1 all-gather.4
  128.8 37.7 all-gather.10
  168.0 61.0 all-gather.8
  264.3 35.1 reduce-scatter.4
  301.7 59.8 reduce-scatter.6
  363.9 34.6 reduce-scatter.8
  400.9 59.8 reduce-scatter.10

commit v6 on v5

--- a/solution.py
+++ b/solution.py
@@ -723,8 +723,10 @@
     tokens, features = terms[0].shape
     lines, slim = layout.lines, features // layout.shards
     wide = 2 * LANES
-
-    def kernel(normed, attended, d_projected, d_branch, small_ref, out, turned):
+    extra = () if small is None else (small,)
+
+    def kernel(normed, attended, d_projected, d_branch, *refs):
+        out, turned = refs[-2:]
         turned[0] = normed[...].T
         turned[1] = attended[...].T
         for block in range(4):
@@ -740,12 +742,12 @@
                         s * slim : (s + 1) * slim
                     ]
 
-        for s in range(layout.shards):
+        for s in range(layout.shards if extra else 0):
             for r in range(layout.reps):
-                out[s % 2, r, s // EF, s // 2 % 2, count * slim :] = small_ref[s]
-
-    shape = (2, layout.reps, lines, 2, count * slim + ROWS, features)
-    return call(kernel, [(shape, BF16)], (*terms, small), [((2, features, tokens), BF16)], micros=8)[0]
+                out[s % 2, r, s // EF, s // 2 % 2, count * slim :] = refs[0][s]
+
+    shape = (2, layout.reps, lines, 2, count * slim + ROWS * len(extra), features)
+    return call(kernel, [(shape, BF16)], (*terms, *extra), [((2, features, tokens), BF16)], micros=8)[0]
 
 
 def store_layer(kernel, source, block, index, shape, layer, held):
@@ -973,6 +975,7 @@
 
     boths, wides, downs = [None] * layers, [None] * layers, [None] * layers
     gate_up_out, down_out = None, None
+    smalls = [None] * layers
     for l in reversed(range(layers)):
         gather, scatter = pairs[l]
         state, inputs, gate_up, activated, outputs = kept[l]
@@ -1023,13 +1026,12 @@
         if not last:
             wide = back_gate_up(after(wides[l + 1], d_branch))
         small_grads = jnp.concatenate([gain_grads, mix_grads]).T.astype(BF16)
-        small_grads = small_grads.reshape(layout.shards, slim * SMALL)
-        small_grads = jnp.pad(small_grads, ((0, 0), (0, ROWS * features - slim * SMALL)))
-        ready = (
-            (normed, attended, d_projected, d_branch),
-            small_grads.reshape(layout.shards, ROWS, features),
-        )
-
+        smalls[l] = small_grads.reshape(layout.shards, slim * SMALL)
+        ready = ((normed, attended, d_projected, d_branch), None)
+
+    smalls = jnp.concatenate(smalls, axis=1)
+    smalls = jnp.pad(smalls, ((0, 0), (0, ROWS * features - smalls.shape[1])))
+    ready = (ready[0], smalls.reshape(layout.shards, ROWS, features))
     boths[0] = layout.sum_core(dense_gradients(layout, *ready, count), j % 2)
     boths[0], wide = join((boths[0], wide))
     gate_up_out = put_gate_up(wide, 1, gate_up_out)
@@ -1044,12 +1046,12 @@
         (layout.sum_line(line), back_gate_up(wides[0]), gate_up_out, down_out, result)
     )
     gate_up_out = put_gate_up(wide, 0, gate_up_out)
-    dense_all = layout.rep_gather(line, rep).reshape(layout.reps, layers, -1, features)
-    dense_grads = jnp.swapaxes(dense_all, 0, 1)
-    dense_all = dense_grads.astype(F32)
-    small_all = dense_all[:, 0, count * slim :].reshape(layers, -1)[:, : slim * SMALL]
-    small_all = small_all.reshape(layers, slim, SMALL)
-    dense_all = dense_all[:, :, : count * slim].reshape(layers, 4, slim, features)
+    dense_all = layout.rep_gather(line, rep)
+    small_all = dense_all[0, count * slim : count * slim + ROWS].reshape(-1)
+    small_all = small_all[: layers * slim * SMALL].astype(F32).reshape(layers, slim, SMALL)
+    starts = [0] + [l * count * slim + ROWS for l in range(1, layers)]
+    dense_all = jnp.stack([dense_all[:, at : at + count * slim] for at in starts])
+    dense_all = dense_all.astype(F32).reshape(layers, 4, slim, features)
     qkv_all = jnp.transpose(dense_all[:, :3], (0, 2, 1, 3)).reshape(layers, slim, 3 * features)
     return (
         result.astype(BF16),

time: 551 us -> 544 us (0.987)
  waiting for transfers between devices: 182 us -> 176 us
    ppermute x66, waiting for transfers between devices: 160 us -> 152 us  [send(): return lax.ppermute(x, AXES, self.pairs(move))]
    unnamed x151 -> x148, local copies, waits for them, and re-layouts: 23.7 us -> 23.8 us
  transfers between devices with their start and end apart: 78 -> 78, of which waited for: 34 -> 35; matrix products, arithmetic and copies ran while one was open for 19% -> 19% of each run, Pallas kernels for 25% -> 25%
where the time goes in v6:
time: 544 us; the launch traced here: 534 us
  waiting for transfers between devices  176 us (32%)
  Pallas kernels  146 us (27%)
  starting transfers between devices  78.1 us (14%)
  local copies, waits for them, and re-layouts  57.4 us (11%)
  other arithmetic  43 us (8%)
  matrix products  18.1 us (3%)
  between operations  15.9 us (3%)
    ppermute x66, waiting for transfers between devices, send(): return lax.ppermute(x, AXES, self.pairs(move))  152 us
    pallas_call x12, Pallas kernels, call(): pl.pallas_call(kernel, out_shape=[jax.ShapeDtypeStruct(shape, dtype) for...  116 us
    ppermute x66, starting transfers between devices, send(): return lax.ppermute(x, AXES, self.pairs(move))  62.5 us
    unnamed x148, local copies, waits for them, and re-layouts  23.8 us
    all_to_all x4, waiting for transfers between devices, trade(): lax.all_to_all(blocks, AXES, 0, 0, axis_index_groups=groups, tiled=True)  20.8 us
    dot_general x4, matrix products, dot(): return lax.dot_general(a, b, (dims, ((), ())), preferred_element_type=F32)  18.1 us
    all_to_all x4, starting transfers between devices, trade(): lax.all_to_all(blocks, AXES, 0, 0, axis_index_groups=groups, tiled=True)  15.3 us
    pallas_call x4, Pallas kernels, store_layer(): pl.pallas_call((lambda x, o: kernel(x, o)) if held is None else lambda x,...  14.6 us
  transfers between devices with their start and end apart: 78, of which 35 were waited for; matrix products, arithmetic and copies ran while one was open for 19% of the time, Pallas kernels for 25%

profile of v6, /device:TPU:8, one launch (start us, length us, event | category | flops | bytes accessed | tf_op | source)
XLA Modules:
  0.0 534.3 jit_solution(2056872365383277359)
XLA Ops:
  21.7 13.7 %collective-permute-done = bf16[112,768]{1,0:T(8,128)(2,1)S(1)} collective-permute-done((bf16[112,768]{1,0:T(8,128)(2,1)S(1)}, bf16[112,768]{1,0:T(8,128)(2,1)S(1)}, u32[]{:S(2)}, u32[]{:S(2)}) %collective-permute-start) | collective-permute-done | bytes 172064 | tf_op jit(solution)/shard_map/ppermute | solution.py:480
  35.5 11.1 %collective-permute-done.1 = bf16[112,768]{1,0:T(8,128)(2,1)S(1)} collective-permute-done((bf16[112,768]{1,0:T(8,128)(2,1)S(1)}, bf16[112,768]{1,0:T(8,128)(2,1)S(1)}, u32[]{:S(2)}, u32[]{:S(2)}) %collective-permute-start.1) | collective-permute-done | bytes 172064 | tf_op jit(solution)/shard_map/ppermute | solution.py:480
  54.8 5.9 %collective-permute-done.18 = bf16[1,48,2048]{2,1,0:T(8,128)(2,1)S(1)} collective-permute-done((bf16[1,48,2048]{2,1,0:T(8,128)(2,1)S(1)}, bf16[1,48,2048]{2,1,0:T(8,128)(2,1)S(1)}, u32[]{:S(2)}, u32[]{:S(2)}) %collective-permute-start.18) | collective-permute-done | bytes 196640 | tf_op jit(solution)/shard_map/ppermute | solution.py:480
  70.1 12.6 %collective-permute-done.5.refs_2_ = bf16[4,112,768]{2,1,0:T(8,128)(2,1)S(1)} collective-permute-done((bf16[4,112,768]{2,1,0:T(8,128)(2,1)S(1)}, bf16[4,112,768]{2,1,0:T(8,128)(2,1)S(1)}, u32[]{:S(2)}, u32[]{:S(2)}) %collective-permute-start.5) | collective-permute-done | bytes 688160 | tf_op jit(solution)/shard_map/ppermute | solution.py:480
  96.2 5.2 shard_map.238
  105.3 12.4 %shard_map.239 = (bf16[256,768]{1,0:T(8,128)(2,1)}, bf16[256,768]{1,0:T(8,128)(2,1)}, bf16[256,768]{1,0:T(8,128)(2,1)}, bf16[256,768]{1,0:T(8,128)(2,1)}, f32[25...) custom-call(bf16[256,768]{1,0:T(8,128)(2,1)} %refs_5_.1, ...), custom_call_target="tpu_custom_call" | custom-call | bytes 43200000 | tf_op jit(solution)/shard_map/pallas_call | solution.py:451
  119.1 5.8 %collective-permute-done.43 = bf16[1,128,768]{2,1,0:T(8,128)(2,1)S(1)} collective-permute-done((bf16[1,128,768]{2,1,0:T(8,128)(2,1)S(1)}, bf16[1,128,768]{2,1,0:T(8,128)(2,1)S(1)}, u32[]{:S(2)}, u32[]{:S(2)}) %collective-permute-start.43) | collective-permute-done | bytes 196640 | tf_op jit(solution)/shard_map/ppermute | solution.py:480
  157.3 10.0 %shard_map.241 = (f32[640,2048]{1,0:T(8,128)}, bf16[640,1024]{1,0:T(8,128)(2,1)}, f32[320,768]{1,0:T(8,128)}, bf16[320,768]{1,0:T(8,128)(2,1)}) custom-call(bf16[640,768]{1,0:T(8,128)(2,1)} %bitcast.37.inputs, bf16[768,2048]{1,0:T(8,128)(2,1)} %all-gather.5.cloned.1.call-done.w_gate_up, bf16[1024,768]{1,0:T(8,128)(2,1)} %all-gather.7.cloned.1.call-done.w_down), custom_call_target="tpu_custom_call" | custom-call | bytes 36000000 | tf_op jit(solution)/shard_map/pallas_call | solution.py:451
  175.1 3.8 collective-permute-done.29.refs_3_
  189.9 4.9 shard_map.242
  195.6 13.0 %shard_map.243 = (f32[256,768]{1,0:T(8,128)}, bf16[256,768]{1,0:T(8,128)(2,1)}, bf16[256,768]{1,0:T(8,128)(2,1)}, bf16[256,768]{1,0:T(8,128)(2,1)}, bf16[256,768...) custom-call(f32[256,128]{1,0:T(8,128)} %get-tuple-element.104.refs_0, ...), custom_call_target="tpu_custom_call" | custom-call | bytes 43200000 | tf_op jit(solution)/shard_map/pallas_call | solution.py:451
  220.3 4.0 collective-permute-done.38
  229.2 12.3 %shard_map.245 = (bf16[640,2048]{1,0:T(8,128)(2,1)}, bf16[640,1024]{1,0:T(8,128)(2,1)}, f32[320,1536]{1,0:T(8,128)}, bf16[320,1536]{1,0:T(8,128)(2,1)}) custom-call(bf16[640,1536]{1,0:T(8,128)(2,1)} %bitcast.201, bf16[768,2048]{1,0:T(8,128)(2,1)} %all-gather.9.cloned.1.call-done.w_gate_up, bf16[1024,768]{1,0:T(8,128)(2,1)} %all-gather.11.cloned.1.call-done.w_down), custom_call_target="tpu_custom_call" | custom-call | bytes 43200000 | tf_op jit(solution)/shard_map/pallas_call | solution.py:451
  241.5 6.5 %convolution_convert_fusion.1 = bf16[768,2048]{1,0:T(8,128)(2,1)} fusion(bf16[640,2048]{1,0:T(8,128)(2,1)} %get-tuple-element.119, bf16[640,1536]{1,0:T(8,128)(2,1)} %bitcast.202), kind=kOutput, calls=%fused_computation.5 | convolution fusion | flops 2014838784 | bytes 6750208 | tf_op jit(solution)/shard_map/dot_general | solution.py:30
  258.7 4.5 collective-permute-done.47
  268.5 5.9 %shard_map.246 = (f32[256,128]{1,0:T(8,128)}, f32[256,768]{1,0:T(8,128)}, f32[14,768]{1,0:T(8,128)}) custom-call(f32[256,128]{1,0:T(8,128)} %get-tuple-element.112.coefs, f32[256,768]{1,0:T(8,128)} %get-tuple-element.113.middle.refs_4_, f32[2,768]{1,0:T(2,128)} %bitcast.239, bf16[2,256,320]{2,1,0:T(8,128)(2,1)} %fusion.10.scatter.refs_3_, ...), custom_call_target="tpu_custom_call" | custom-call | bytes 21600000 | tf_op jit(solution)/shard_map/pallas_call | solution.py:451
  274.4 14.2 %shard_map.247 = (f32[256,768]{1,0:T(8,128)}, bf16[256,768]{1,0:T(8,128)(2,1)}, bf16[3,256,768]{2,1,0:T(8,128)(2,1)}, f32[2,768]{1,0:T(2,128)}, bf16[320,768]{1,0:T(8,128)(2,1)}) custom-call(f32[256,768]{1,0:T(8,128)} %refs_0_.3, f32[256,768]{1,0:T(8,128)} %get-tuple-element.123.refs_1_, bf16[320,1536]{1,0:T(8,128)(2,1)} %pad_maximum_fusion.4.outputs.refs_2_, ...), custom_call_target="tpu_custom_call" | custom-call | bytes 50400000 | tf_op jit(solution)/shard_map/pallas_call | solution.py:451
  293.3 5.7 %shard_map.248 = (f32[256,128]{1,0:T(8,128)}, f32[256,768]{1,0:T(8,128)}, f32[14,768]{1,0:T(8,128)}) custom-call(f32[256,128]{1,0:T(8,128)} %get-tuple-element.104.refs_0_.refs_16_.coefs, f32[256,768]{1,0:T(8,128)} %get-tuple-element.105.refs_1_.middle.refs_4_, f32[2,768]{1,0:T(2,128)} %bitcast.244, bf16[2,256,320]{2,1,0:T(8,128)(2,1)} %fusion.9.refs_3_.scatter, ...), custom_call_target="tpu_custom_call" | custom-call | bytes 21600000 | tf_op jit(solution)/shard_map/pallas_call | solution.py:451
  308.2 10.7 %shard_map.249 = (bf16[640,2048]{1,0:T(8,128)(2,1)}, f32[320,768]{1,0:T(8,128)}, bf16[320,768]{1,0:T(8,128)(2,1)}) custom-call(bf16[640,768]{1,0:T(8,128)(2,1)} %bitcast.208, bf16[768,2048]{1,0:T(8,128)(2,1)} %all-gather.5.cloned.1.call-done.w_gate_up, bf16[1024,768]{1,0:T(8,128)(2,1)} %all-gather.7.cloned.1.call-done.w_down, ...), custom_call_target="tpu_custom_call" | custom-call | bytes 36000000 | tf_op jit(solution)/shard_map/pallas_call | solution.py:451
  319.4 7.5 %shard_map.250 = bf16[2,2,4,2,96,768]{5,4,3,2,1,0:T(8,128)(2,1)} custom-call(bf16[256,768]{1,0:T(8,128)(2,1)} %get-tuple-element.148.normed, bf16[256,768]{1,0:T(8,128)(2,1)} %get-tuple-element.149.attended, bf16[3,256,768]{2,1,0:T(8,128)(2,1)} %get-tuple-element.150.d_projected, bf16[256,768]{1,0:T(8,128)(2,1)} %get-tuple-element.151.d_branch), custom_call_target="tpu_custom_call" | custom-call | bytes 28800000 | tf_op jit(solution)/shard_map/pallas_call | solution.py:451
  330.7 6.4 %convolution_convert_fusion = bf16[768,2048]{1,0:T(8,128)(2,1)} fusion(bf16[640,768]{1,0:T(8,128)(2,1)} %bitcast.37.inputs, bf16[640,2048]{1,0:T(8,128)(2,1)} %get-tuple-element.142), kind=kOutput, calls=%fused_computation.4 | convolution fusion | flops 2014838784 | bytes 6750208 | tf_op jit(solution)/shard_map/dot_general | solution.py:30
  350.8 3.8 fusion.1
  355.2 13.4 %shard_map.252 = (f32[256,768]{1,0:T(8,128)}, bf16[256,768]{1,0:T(8,128)(2,1)}, bf16[3,256,768]{2,1,0:T(8,128)(2,1)}, f32[2,768]{1,0:T(2,128)}) custom-call(f32[256,768]{1,0:T(8,128)} %get-tuple-element.129.d_result.refs_0_, f32[256,768]{1,0:T(8,128)} %get-tuple-element.134.refs_1_, bf16[320,768]{1,0:T(8,128)(2,1)} %pad_maximum_fusion.12.refs_2_, ...), custom_call_target="tpu_custom_call" | custom-call | bytes 50400000 | tf_op jit(solution)/shard_map/pallas_call | solution.py:451
  370.6 7.7 %shard_map.253 = bf16[2,2,4,2,112,768]{5,4,3,2,1,0:T(8,128)(2,1)} custom-call(bf16[256,768]{1,0:T(8,128)(2,1)} %get-tuple-element.102.normed, bf16[256,768]{1,0:T(8,128)(2,1)} %get-tuple-element.103.attended, bf16[3,256,768]{2,1,0:T(8,128)(2,1)} %get-tuple-element.158.d_projected, bf16[256,768]{1,0:T(8,128)(2,1)} %get-tuple-element.159.d_branch, ...), custom_call_target="tpu_custom_call" | custom-call | bytes 28800000 | tf_op jit(solution)/shard_map/pallas_call | solution.py:451
  383.1 4.5 all-to-all-start.1
  391.0 16.7 %all-to-all-done.1 = bf16[8,48,2048]{2,1,0:T(8,128)(2,1)} async-done(((bf16[8,48,2048]{2,1,0:T(8,128)(2,1)}), bf16[8,48,2048]{2,1,0:T(8,128)(2,1)}, u32[]{:S(2)}, u32[]{:S(2)}) %all-to-all-start.1) | async-done | bytes 1572896 | tf_op jit(solution)/shard_map/all_to_all | solution.py:537
  421.7 3.9 shard_map.254.h
  425.6 18.5 %collective-permute-done.58 = bf16[2,2,1,208,768]{4,3,1,0,2:T(8,128)(2,1)} collective-permute-done((bf16[2,2,1,208,768]{4,3,1,0,2:T(8,128)(2,1)}, bf16[2,2,1,208,768]{4,3,1,0,2:T(8,128)(2,1)}, u32[]{:S(2)}, u32[]{:S(2)}) %collective-permute-start.58) | collective-permute-done | bytes 1277984 | tf_op jit(solution)/shard_map/ppermute | solution.py:480
  457.5 12.4 %collective-permute-done.60 = bf16[2,208,768]{2,1,0:T(8,128)(2,1)S(1)} collective-permute-done((bf16[2,208,768]{2,1,0:T(8,128)(2,1)S(1)}, bf16[2,208,768]{2,1,0:T(8,128)(2,1)S(1)}, u32[]{:S(2)}, u32[]{:S(2)}) %collective-permute-start.60) | collective-permute-done | bytes 639008 | tf_op jit(solution)/shard_map/ppermute | solution.py:480
  490.5 12.6 %collective-permute-done.62 = bf16[208,768]{1,0:T(8,128)(2,1)S(1)} collective-permute-done((bf16[208,768]{1,0:T(8,128)(2,1)}, bf16[208,768]{1,0:T(8,128)(2,1)S(1)}, u32[]{:S(2)}, u32[]{:S(2)}) %collective-permute-start.62) | collective-permute-done | bytes 319520 | tf_op jit(solution)/shard_map/ppermute | solution.py:480
  503.1 6.4 %collective-permute-done.63 = bf16[208,768]{1,0:T(8,128)(2,1)S(1)} collective-permute-done((bf16[208,768]{1,0:T(8,128)(2,1)}, bf16[208,768]{1,0:T(8,128)(2,1)S(1)}, u32[]{:S(2)}, u32[]{:S(2)}) %collective-permute-start.63) | collective-permute-done | bytes 319520 | tf_op jit(solution)/shard_map/ppermute | solution.py:480
  518.2 3.9 shard_map.257
  (451 shorter events, 238.2 us)
Async XLA Ops:
  7.2 150.1 %all-gather.7.cloned.1.call-start = ((), (), s32[]{:S(2)}) async-start(), calls=%async_computation.9 | async-start | bytes 1966080 | tf_op jit(solution)/shard_map/all_gather | solution.py:554
  16.1 141.1 %all-gather.5.cloned.1.call-start = ((), (), s32[]{:S(2)}) async-start(), calls=%async_computation.8 | async-start | bytes 3932160 | tf_op jit(solution)/shard_map/all_gather | solution.py:554
  17.1 18.4 %collective-permute-start = (bf16[112,768]{1,0:T(8,128)(2,1)S(1)}, bf16[112,768]{1,0:T(8,128)(2,1)S(1)}, u32[]{:S(2)}, u32[]{:S(2)}) collective-permute-start(bf16[112,768]{1,0:T(8,128)(2,1)S(1)} %get-tuple-element.284), channel_id=1, source_target_pairs={{0,4},{1,5},{2,6},{3,7},{4,8},{5,9},{6,10},{7,11},{8,12},{9,13},{1... | collective-permute-start | bytes 516104 | tf_op jit(solution)/shard_map/ppermute | solution.py:480
  18.7 27.8 %collective-permute-start.1 = (bf16[112,768]{1,0:T(8,128)(2,1)S(1)}, bf16[112,768]{1,0:T(8,128)(2,1)S(1)}, u32[]{:S(2)}, u32[]{:S(2)}) collective-permute-start(bf16[112,768]{1,0:T(8,128)(2,1)S(1)} %get-tuple-element.284), channel_id=1, source_target_pairs={{0,8},{1,9},{2,10},{3,11},{4,12},{5,13},{6,14},{7,15},{8,0},{9,1},... | collective-permute-start | bytes 516104 | tf_op jit(solution)/shard_map/ppermute | solution.py:480
  19.8 28.9 %collective-permute-start.2 = (bf16[112,768]{1,0:T(8,128)(2,1)S(1)}, bf16[112,768]{1,0:T(8,128)(2,1)S(1)}, u32[]{:S(2)}, u32[]{:S(2)}) collective-permute-start(bf16[112,768]{1,0:T(8,128)(2,1)S(1)} %get-tuple-element.284), channel_id=1, source_target_pairs={{0,12},{1,13},{2,14},{3,15},{4,0},{5,1},{6,2},{7,3},{8,4},{9,5},{1... | collective-permute-start | bytes 516104 | tf_op jit(solution)/shard_map/ppermute | solution.py:480
  64.9 162.2 %all-gather.11.cloned.1.call-start = ((), (), s32[]{:S(2)}) async-start(), calls=%async_computation.11 | async-start | bytes 1966080 | tf_op jit(solution)/shard_map/all_gather | solution.py:554
  65.0 17.7 %collective-permute-start.5 = (bf16[4,112,768]{2,1,0:T(8,128)(2,1)S(1)}, bf16[4,112,768]{2,1,0:T(8,128)(2,1)S(1)}, u32[]{:S(2)}, u32[]{:S(2)}) collective-permute-start(bf16[4,112,768]{2,1,0:T(8,128)(2,1)S(1)} %pad_maximum_fusion.7.refs_0_), channel_id=1, source_target_pairs={{0,16},{1,17},{2,18},{3,19},{4,20},{5,21},{6,22},{7,23},{8,24},{9,... | collective-permute-start | bytes 2064392 | tf_op jit(solution)/shard_map/ppermute | solution.py:480
  66.4 17.8 %collective-permute-start.4 = (bf16[4,112,768]{2,1,0:T(8,128)(2,1)S(1)}, bf16[4,112,768]{2,1,0:T(8,128)(2,1)S(1)}, u32[]{:S(2)}, u32[]{:S(2)}) collective-permute-start(bf16[4,112,768]{2,1,0:T(8,128)(2,1)S(1)} %pad_maximum_fusion.7.refs_0_), channel_id=1, source_target_pairs={{0,2},{1,3},{2,0},{3,1},{4,6},{5,7},{6,4},{7,5},{8,10},{9,11},{10,... | collective-permute-start | bytes 2064392 | tf_op jit(solution)/shard_map/ppermute | solution.py:480
  70.1 24.9 %collective-permute-start.8 = (bf16[4,112,768]{2,1,0:T(8,128)(2,1)S(1)}, bf16[4,112,768]{2,1,0:T(8,128)(2,1)}, u32[]{:S(2)}, u32[]{:S(2)}) collective-permute-start(bf16[4,112,768]{2,1,0:T(8,128)(2,1)S(1)} %pad_maximum_fusion.7.refs_0_), channel_id=1, source_target_pairs={{0,1},{1,0},{2,3},{3,2},{4,5},{5,4},{6,7},{7,6},{8,9},{9,8},{10,11... | collective-permute-start | bytes 2064392 | tf_op jit(solution)/shard_map/ppermute | solution.py:480
  125.8 103.4 %all-gather.9.cloned.1.call-start = ((), (), s32[]{:S(2)}) async-start(), calls=%async_computation.10 | async-start | bytes 3932160 | tf_op jit(solution)/shard_map/all_gather | solution.py:554
  125.9 19.9 %collective-permute-start.24 = (bf16[96,768]{1,0:T(8,128)(2,1)S(1)}, bf16[96,768]{1,0:T(8,128)(2,1)S(1)}, u32[]{:S(2)}, u32[]{:S(2)}) collective-permute-start(bf16[96,768]{1,0:T(8,128)(2,1)S(1)} %bitcast.218), channel_id=1, source_target_pairs={{0,4},{1,5},{2,6},{3,7},{4,8},{5,9},{6,10},{7,11},{8,12},{9,13},{1... | collective-permute-start | bytes 442376 | tf_op jit(solution)/shard_map/ppermute | solution.py:480
  125.9 19.9 %collective-permute-start.25 = (bf16[96,768]{1,0:T(8,128)(2,1)S(1)}, bf16[96,768]{1,0:T(8,128)(2,1)S(1)}, u32[]{:S(2)}, u32[]{:S(2)}) collective-permute-start(bf16[96,768]{1,0:T(8,128)(2,1)S(1)} %bitcast.219), channel_id=1, source_target_pairs={{0,8},{1,9},{2,10},{3,11},{4,12},{5,13},{6,14},{7,15},{8,0},{9,1},... | collective-permute-start | bytes 442376 | tf_op jit(solution)/shard_map/ppermute | solution.py:480
  128.6 18.3 %collective-permute-start.26 = (bf16[96,768]{1,0:T(8,128)(2,1)S(1)}, bf16[96,768]{1,0:T(8,128)(2,1)S(1)}, u32[]{:S(2)}, u32[]{:S(2)}) collective-permute-start(bf16[96,768]{1,0:T(8,128)(2,1)S(1)} %bitcast.220), channel_id=1, source_target_pairs={{0,12},{1,13},{2,14},{3,15},{4,0},{5,1},{6,2},{7,3},{8,4},{9,5},{1... | collective-permute-start | bytes 442376 | tf_op jit(solution)/shard_map/ppermute | solution.py:480
  147.0 22.0 %collective-permute-start.28 = (bf16[4,96,768]{2,1,0:T(8,128)(2,1)S(1)}, bf16[4,96,768]{2,1,0:T(8,128)(2,1)S(1)}, u32[]{:S(2)}, u32[]{:S(2)}) collective-permute-start(bf16[4,96,768]{2,1,0:T(8,128)(2,1)S(1)} %pad_maximum_fusion.8.refs_0_), channel_id=1, source_target_pairs={{0,16},{1,17},{2,18},{3,19},{4,20},{5,21},{6,22},{7,23},{8,24},{9,... | collective-permute-start | bytes 1769480 | tf_op jit(solution)/shard_map/ppermute | solution.py:480
  148.6 22.1 %collective-permute-start.27 = (bf16[4,96,768]{2,1,0:T(8,128)(2,1)S(1)}, bf16[4,96,768]{2,1,0:T(8,128)(2,1)S(1)}, u32[]{:S(2)}, u32[]{:S(2)}) collective-permute-start(bf16[4,96,768]{2,1,0:T(8,128)(2,1)S(1)} %pad_maximum_fusion.8.refs_0_), channel_id=1, source_target_pairs={{0,2},{1,3},{2,0},{3,1},{4,6},{5,7},{6,4},{7,5},{8,10},{9,11},{10,... | collective-permute-start | bytes 1769480 | tf_op jit(solution)/shard_map/ppermute | solution.py:480
  154.0 148.1 %reduce-scatter.5.cloned.1.call-start = ((), (), s32[]{:S(2)}) async-start(), calls=%async_computation.12 | async-start | bytes 1966080 | tf_op jit(solution)/shard_map/reduce_scatter | solution.py:559
  174.6 15.3 %collective-permute-start.32 = (bf16[4,96,768]{2,1,0:T(8,128)(2,1)S(1)}, bf16[4,96,768]{2,1,0:T(8,128)(2,1)}, u32[]{:S(2)}, u32[]{:S(2)}) collective-permute-start(bf16[4,96,768]{2,1,0:T(8,128)(2,1)S(1)} %collective-permute-done.27.refs_1_), channel_id=1, source_target_pairs={{0,1},{1,0},{2,3},{3,2},{4,5},{5,4},{6,7},{7,6},{8,9},{9,8},{10,11... | collective-permute-start | bytes 1769480 | tf_op jit(solution)/shard_map/ppermute | solution.py:480
  264.2 116.1 %reduce-scatter.7.cloned.1.call-start = ((), (), s32[]{:S(2)}) async-start(), calls=%async_computation.13 | async-start | bytes 3932160 | tf_op jit(solution)/shard_map/reduce_scatter | solution.py:559
  304.5 14.9 %all-to-all-start = ((bf16[4,128,768]{2,1,0:T(8,128)(2,1)}), bf16[4,128,768]{2,1,0:T(8,128)(2,1)S(1)}, u32[]{:S(2)}, u32[]{:S(2)}) async-start(bf16[4,128,768]{2,1,0:T(8,128)(2,1)} %pad_maximum_fusion.5), calls=%async_computation.1 | async-start | bytes 1572864 | tf_op jit(solution)/shard_map/all_to_all | solution.py:537
  308.2 107.9 %reduce-scatter.9.cloned.1.call-start = ((), (), s32[]{:S(2)}) async-start(), calls=%async_computation.14 | async-start | bytes 1966080 | tf_op jit(solution)/shard_map/reduce_scatter | solution.py:559
  330.1 20.7 %collective-permute-start.56 = (bf16[2,4,2,96,768]{4,3,2,1,0:T(8,128)(2,1)}, bf16[2,4,2,96,768]{4,3,2,1,0:T(8,128)(2,1)S(1)}, u32[]{:S(2)}, u32[]{:S(2)}) collective-permute-start(bf16[2,4,2,96,768]{4,3,2,1,0:T(8,128)(2,1)} %dynamic-slice_bitcast_fusion.1), channel_id=1, source_target_pairs={{0,1},{1,0},{2,3},{3,2},{4,5},{5,4},{6,7},{7,6},{8,9},{9,8},{10,11... | collective-permute-start | bytes 7077896 | tf_op jit(solution)/shard_map/ppermute | solution.py:480
  354.7 117.1 %reduce-scatter.11.cloned.1.call-start = ((), (), s32[]{:S(2)}) async-start(), calls=%async_computation.15 | async-start | bytes 3932160 | tf_op jit(solution)/shard_map/reduce_scatter | solution.py:559
  383.1 24.6 %all-to-all-start.1 = ((bf16[8,48,2048]{2,1,0:T(8,128)(2,1)}), bf16[8,48,2048]{2,1,0:T(8,128)(2,1)}, u32[]{:S(2)}, u32[]{:S(2)}) async-start(bf16[8,48,2048]{2,1,0:T(8,128)(2,1)} %pad_maximum_fusion), calls=%async_computation.3 | async-start | bytes 3145728 | tf_op jit(solution)/shard_map/all_to_all | solution.py:537
  412.6 31.5 %collective-permute-start.58 = (bf16[2,2,1,208,768]{4,3,1,0,2:T(8,128)(2,1)}, bf16[2,2,1,208,768]{4,3,1,0,2:T(8,128)(2,1)}, u32[]{:S(2)}, u32[]{:S(2)}) collective-permute-start(bf16[2,2,1,208,768]{4,3,1,0,2:T(8,128)(2,1)} %dynamic-slice_bitcast_fusion.3), channel_id=1, source_target_pairs={{0,2},{1,3},{2,0},{3,1},{4,6},{5,7},{6,4},{7,5},{8,10},{9,11},{10,... | collective-permute-start | bytes 3833864 | tf_op jit(solution)/shard_map/ppermute | solution.py:480
  415.2 32.0 %collective-permute-start.59 = (bf16[2,2,208,768]{3,2,1,0:T(8,128)(2,1)}, bf16[2,2,208,768]{3,2,1,0:T(8,128)(2,1)}, u32[]{:S(2)}, u32[]{:S(2)}) collective-permute-start(bf16[2,2,208,768]{3,2,1,0:T(8,128)(2,1)} %dynamic-slice_bitcast_fusion.2), channel_id=1, source_target_pairs={{0,16},{1,17},{2,18},{3,19},{4,20},{5,21},{6,22},{7,23},{8,24},{9,... | collective-permute-start | bytes 3833864 | tf_op jit(solution)/shard_map/ppermute | solution.py:480
  418.2 35.2 %all-to-all-start.2 = ((bf16[4,128,768]{2,1,0:T(8,128)(2,1)}), bf16[4,128,768]{2,1,0:T(8,128)(2,1)S(1)}, u32[]{:S(2)}, u32[]{:S(2)}) async-start(bf16[4,128,768]{2,1,0:T(8,128)(2,1)} %pad_maximum_fusion.6), calls=%async_computation.5 | async-start | bytes 1572864 | tf_op jit(solution)/shard_map/all_to_all | solution.py:537
  454.8 15.1 %collective-permute-start.60 = (bf16[2,208,768]{2,1,0:T(8,128)(2,1)S(1)}, bf16[2,208,768]{2,1,0:T(8,128)(2,1)S(1)}, u32[]{:S(2)}, u32[]{:S(2)}) collective-permute-start(bf16[2,208,768]{2,1,0:T(8,128)(2,1)S(1)} %dynamic-slice_bitcast_fusion.4), channel_id=1, source_target_pairs={{0,16},{1,17},{2,18},{3,19},{4,20},{5,21},{6,22},{7,23},{8,24},{9,... | collective-permute-start | bytes 1916936 | tf_op jit(solution)/shard_map/ppermute | solution.py:480
  456.8 14.7 %collective-permute-start.61 = (bf16[2,1,208,768]{3,2,1,0:T(8,128)(2,1)S(1)}, bf16[2,1,208,768]{3,2,1,0:T(8,128)(2,1)S(1)}, u32[]{:S(2)}, u32[]{:S(2)}) collective-permute-start(bf16[2,1,208,768]{3,2,1,0:T(8,128)(2,1)S(1)} %constant_dynamic-slice_fusion), channel_id=1, source_target_pairs={{0,2},{1,3},{2,0},{3,1},{4,6},{5,7},{6,4},{7,5},{8,10},{9,11},{10,... | collective-permute-start | bytes 1916936 | tf_op jit(solution)/shard_map/ppermute | solution.py:480
  474.5 38.5 %all-to-all-start.3 = ((bf16[8,48,2048]{2,1,0:T(8,128)(2,1)}), bf16[8,48,2048]{2,1,0:T(8,128)(2,1)S(1)}, u32[]{:S(2)}, u32[]{:S(2)}) async-start(bf16[8,48,2048]{2,1,0:T(8,128)(2,1)} %pad_maximum_fusion.1), calls=%async_computation.7 | async-start | bytes 3145728 | tf_op jit(solution)/shard_map/all_to_all | solution.py:537
  479.1 24.1 %collective-permute-start.62 = (bf16[208,768]{1,0:T(8,128)(2,1)}, bf16[208,768]{1,0:T(8,128)(2,1)S(1)}, u32[]{:S(2)}, u32[]{:S(2)}) collective-permute-start(bf16[208,768]{1,0:T(8,128)(2,1)} %get-tuple-element.238), channel_id=1, source_target_pairs={{0,4},{1,5},{2,6},{3,7},{4,8},{5,9},{6,10},{7,11},{8,12},{9,13},{1... | collective-permute-start | bytes 958472 | tf_op jit(solution)/shard_map/ppermute | solution.py:480
  481.4 28.1 %collective-permute-start.63 = (bf16[208,768]{1,0:T(8,128)(2,1)}, bf16[208,768]{1,0:T(8,128)(2,1)S(1)}, u32[]{:S(2)}, u32[]{:S(2)}) collective-permute-start(bf16[208,768]{1,0:T(8,128)(2,1)} %get-tuple-element.240), channel_id=1, source_target_pairs={{0,8},{1,9},{2,10},{3,11},{4,12},{5,13},{6,14},{7,15},{8,0},{9,1},... | collective-permute-start | bytes 958472 | tf_op jit(solution)/shard_map/ppermute | solution.py:480
  483.9 27.7 %collective-permute-start.64 = (bf16[208,768]{1,0:T(8,128)(2,1)}, bf16[208,768]{1,0:T(8,128)(2,1)}, u32[]{:S(2)}, u32[]{:S(2)}) collective-permute-start(bf16[208,768]{1,0:T(8,128)(2,1)} %get-tuple-element.239), channel_id=1, source_target_pairs={{0,12},{1,13},{2,14},{3,15},{4,0},{5,1},{6,2},{7,3},{8,4},{9,5},{1... | collective-permute-start | bytes 958472 | tf_op jit(solution)/shard_map/ppermute | solution.py:480
  (103 other events, 796.0 us)
Sparse Core Ops, SparseCore 0:
  16.2 42.8 all-gather.6
  65.1 62.1 all-gather.4
  128.8 37.7 all-gather.10
  168.1 61.0 all-gather.8
  264.3 35.1 reduce-scatter.4
  301.7 59.8 reduce-scatter.6
  363.9 34.6 reduce-scatter.8
  400.9 59.8 reduce-scatter.10

commit v7 on v6

--- a/solution.py
+++ b/solution.py
@@ -1033,9 +1033,8 @@
     smalls = jnp.pad(smalls, ((0, 0), (0, ROWS * features - smalls.shape[1])))
     ready = (ready[0], smalls.reshape(layout.shards, ROWS, features))
     boths[0] = layout.sum_core(dense_gradients(layout, *ready, count), j % 2)
-    boths[0], wide = join((boths[0], wide))
+    both, wide = join((jnp.concatenate(boths, axis=3), wide))
     gate_up_out = put_gate_up(wide, 1, gate_up_out)
-    both = jnp.concatenate(boths, axis=3)
     cross, gate_up_out, down = join(
         (layout.sum_cross(both, rep, j), gate_up_out, back_down(after(downs[0], both)))
     )

time: 544 us -> 543 us (level)
    unnamed x148 -> x142, local copies, waits for them, and re-layouts: 23.8 us -> 21 us
where the time goes in v7:
time: 543 us; the launch traced here: 533 us
  waiting for transfers between devices  175 us (32%)
  Pallas kernels  146 us (27%)
  starting transfers between devices  77.3 us (14%)
  local copies, waits for them, and re-layouts  57.6 us (11%)
  other arithmetic  42.3 us (8%)
  matrix products  19.3 us (4%)
  between operations  16 us (3%)
    ppermute x66, waiting for transfers between devices, send(): return lax.ppermute(x, AXES, self.pairs(move))  153 us
    pallas_call x12, Pallas kernels, call(): pl.pallas_call(kernel, out_shape=[jax.ShapeDtypeStruct(shape, dtype) for...  116 us
    ppermute x66, starting transfers between devices, send(): return lax.ppermute(x, AXES, self.pairs(move))  61.8 us
    unnamed x142, local copies, waits for them, and re-layouts  21 us
    all_to_all x4, waiting for transfers between devices, trade(): lax.all_to_all(blocks, AXES, 0, 0, axis_index_groups=groups, tiled=True)  19.7 us
    dot_general x4, matrix products, dot(): return lax.dot_general(a, b, (dims, ((), ())), preferred_element_type=F32)  19.3 us
    all_to_all x4, starting transfers between devices, trade(): lax.all_to_all(blocks, AXES, 0, 0, axis_index_groups=groups, tiled=True)  15.3 us
    pallas_call x4, Pallas kernels, store_layer(): pl.pallas_call((lambda x, o: kernel(x, o)) if held is None else lambda x,...  14.6 us
  transfers between devices with their start and end apart: 78, of which 35 were waited for; matrix products, arithmetic and copies ran while one was open for 19% of the time, Pallas kernels for 25%

profile of v7, /device:TPU:8, one launch (start us, length us, event | category | flops | bytes accessed | tf_op | source)
XLA Modules:
  0.0 533.5 jit_solution(1488904065710860034)
XLA Ops:
  21.7 13.7 %collective-permute-done = bf16[112,768]{1,0:T(8,128)(2,1)S(1)} collective-permute-done((bf16[112,768]{1,0:T(8,128)(2,1)S(1)}, bf16[112,768]{1,0:T(8,128)(2,1)S(1)}, u32[]{:S(2)}, u32[]{:S(2)}) %collective-permute-start) | collective-permute-done | bytes 172064 | tf_op jit(solution)/shard_map/ppermute | solution.py:480
  35.5 11.1 %collective-permute-done.1 = bf16[112,768]{1,0:T(8,128)(2,1)S(1)} collective-permute-done((bf16[112,768]{1,0:T(8,128)(2,1)S(1)}, bf16[112,768]{1,0:T(8,128)(2,1)S(1)}, u32[]{:S(2)}, u32[]{:S(2)}) %collective-permute-start.1) | collective-permute-done | bytes 172064 | tf_op jit(solution)/shard_map/ppermute | solution.py:480
  54.8 5.9 %collective-permute-done.18 = bf16[1,48,2048]{2,1,0:T(8,128)(2,1)S(1)} collective-permute-done((bf16[1,48,2048]{2,1,0:T(8,128)(2,1)S(1)}, bf16[1,48,2048]{2,1,0:T(8,128)(2,1)S(1)}, u32[]{:S(2)}, u32[]{:S(2)}) %collective-permute-start.18) | collective-permute-done | bytes 196640 | tf_op jit(solution)/shard_map/ppermute | solution.py:480
  70.1 12.6 %collective-permute-done.5.refs_2_ = bf16[4,112,768]{2,1,0:T(8,128)(2,1)S(1)} collective-permute-done((bf16[4,112,768]{2,1,0:T(8,128)(2,1)S(1)}, bf16[4,112,768]{2,1,0:T(8,128)(2,1)S(1)}, u32[]{:S(2)}, u32[]{:S(2)}) %collective-permute-start.5) | collective-permute-done | bytes 688160 | tf_op jit(solution)/shard_map/ppermute | solution.py:480
  96.1 5.2 shard_map.238
  105.3 12.4 %shard_map.239 = (bf16[256,768]{1,0:T(8,128)(2,1)}, bf16[256,768]{1,0:T(8,128)(2,1)}, bf16[256,768]{1,0:T(8,128)(2,1)}, bf16[256,768]{1,0:T(8,128)(2,1)}, f32[25...) custom-call(bf16[256,768]{1,0:T(8,128)(2,1)} %refs_5_.1, ...), custom_call_target="tpu_custom_call" | custom-call | bytes 43200000 | tf_op jit(solution)/shard_map/pallas_call | solution.py:451
  119.1 5.9 %collective-permute-done.43 = bf16[1,128,768]{2,1,0:T(8,128)(2,1)S(1)} collective-permute-done((bf16[1,128,768]{2,1,0:T(8,128)(2,1)S(1)}, bf16[1,128,768]{2,1,0:T(8,128)(2,1)S(1)}, u32[]{:S(2)}, u32[]{:S(2)}) %collective-permute-start.43) | collective-permute-done | bytes 196640 | tf_op jit(solution)/shard_map/ppermute | solution.py:480
  157.3 10.0 %shard_map.241 = (f32[640,2048]{1,0:T(8,128)}, bf16[640,1024]{1,0:T(8,128)(2,1)}, f32[320,768]{1,0:T(8,128)}, bf16[320,768]{1,0:T(8,128)(2,1)}) custom-call(bf16[640,768]{1,0:T(8,128)(2,1)} %bitcast.37.inputs, bf16[768,2048]{1,0:T(8,128)(2,1)} %all-gather.5.cloned.1.call-done.w_gate_up, bf16[1024,768]{1,0:T(8,128)(2,1)} %all-gather.7.cloned.1.call-done.w_down), custom_call_target="tpu_custom_call" | custom-call | bytes 36000000 | tf_op jit(solution)/shard_map/pallas_call | solution.py:451
  189.9 4.9 shard_map.242
  195.7 13.0 %shard_map.243 = (f32[256,768]{1,0:T(8,128)}, bf16[256,768]{1,0:T(8,128)(2,1)}, bf16[256,768]{1,0:T(8,128)(2,1)}, bf16[256,768]{1,0:T(8,128)(2,1)}, bf16[256,768...) custom-call(f32[256,128]{1,0:T(8,128)} %get-tuple-element.104.refs_0, ...), custom_call_target="tpu_custom_call" | custom-call | bytes 43200000 | tf_op jit(solution)/shard_map/pallas_call | solution.py:451
  220.4 4.0 collective-permute-done.38
  229.1 12.3 %shard_map.245 = (bf16[640,2048]{1,0:T(8,128)(2,1)}, bf16[640,1024]{1,0:T(8,128)(2,1)}, f32[320,1536]{1,0:T(8,128)}, bf16[320,1536]{1,0:T(8,128)(2,1)}) custom-call(bf16[640,1536]{1,0:T(8,128)(2,1)} %bitcast.197, bf16[768,2048]{1,0:T(8,128)(2,1)} %all-gather.9.cloned.1.call-done.w_gate_up, bf16[1024,768]{1,0:T(8,128)(2,1)} %all-gather.11.cloned.1.call-done.w_down), custom_call_target="tpu_custom_call" | custom-call | bytes 43200000 | tf_op jit(solution)/shard_map/pallas_call | solution.py:451
  241.4 6.5 %convolution_convert_fusion.1 = bf16[768,2048]{1,0:T(8,128)(2,1)} fusion(bf16[640,2048]{1,0:T(8,128)(2,1)} %get-tuple-element.119, bf16[640,1536]{1,0:T(8,128)(2,1)} %bitcast.198), kind=kOutput, calls=%fused_computation.6 | convolution fusion | flops 2014838784 | bytes 6750208 | tf_op jit(solution)/shard_map/dot_general | solution.py:30
  258.6 4.5 collective-permute-done.47
  268.5 5.9 %shard_map.246 = (f32[256,128]{1,0:T(8,128)}, f32[256,768]{1,0:T(8,128)}, f32[14,768]{1,0:T(8,128)}) custom-call(f32[256,128]{1,0:T(8,128)} %get-tuple-element.112.coefs, f32[256,768]{1,0:T(8,128)} %get-tuple-element.113.middle.refs_4_, f32[2,768]{1,0:T(2,128)} %bitcast.235, bf16[2,256,320]{2,1,0:T(8,128)(2,1)} %fusion.10.scatter.refs_3_, ...), custom_call_target="tpu_custom_call" | custom-call | bytes 21600000 | tf_op jit(solution)/shard_map/pallas_call | solution.py:451
  274.4 14.2 %shard_map.247 = (f32[256,768]{1,0:T(8,128)}, bf16[256,768]{1,0:T(8,128)(2,1)}, bf16[3,256,768]{2,1,0:T(8,128)(2,1)}, f32[2,768]{1,0:T(2,128)}, bf16[320,768]{1,0:T(8,128)(2,1)}) custom-call(f32[256,768]{1,0:T(8,128)} %refs_0_.3, f32[256,768]{1,0:T(8,128)} %get-tuple-element.123.refs_1_, bf16[320,1536]{1,0:T(8,128)(2,1)} %pad_maximum_fusion.5.outputs.refs_2_, ...), custom_call_target="tpu_custom_call" | custom-call | bytes 50400000 | tf_op jit(solution)/shard_map/pallas_call | solution.py:451
  293.3 5.7 %shard_map.248 = (f32[256,128]{1,0:T(8,128)}, f32[256,768]{1,0:T(8,128)}, f32[14,768]{1,0:T(8,128)}) custom-call(f32[256,128]{1,0:T(8,128)} %get-tuple-element.104.refs_0_.refs_16_.coefs, f32[256,768]{1,0:T(8,128)} %get-tuple-element.105.refs_1_.middle.refs_4_, f32[2,768]{1,0:T(2,128)} %bitcast.240, bf16[2,256,320]{2,1,0:T(8,128)(2,1)} %fusion.9.refs_3_.scatter, ...), custom_call_target="tpu_custom_call" | custom-call | bytes 21600000 | tf_op jit(solution)/shard_map/pallas_call | solution.py:451
  308.1 10.7 %shard_map.249 = (bf16[640,2048]{1,0:T(8,128)(2,1)}, f32[320,768]{1,0:T(8,128)}, bf16[320,768]{1,0:T(8,128)(2,1)}) custom-call(bf16[640,768]{1,0:T(8,128)(2,1)} %bitcast.204, bf16[768,2048]{1,0:T(8,128)(2,1)} %all-gather.5.cloned.1.call-done.w_gate_up, bf16[1024,768]{1,0:T(8,128)(2,1)} %all-gather.7.cloned.1.call-done.w_down, ...), custom_call_target="tpu_custom_call" | custom-call | bytes 36000000 | tf_op jit(solution)/shard_map/pallas_call | solution.py:451
  319.3 7.6 %shard_map.250 = bf16[2,2,4,2,96,768]{5,4,3,2,1,0:T(8,128)(2,1)} custom-call(bf16[256,768]{1,0:T(8,128)(2,1)} %get-tuple-element.148.normed, bf16[256,768]{1,0:T(8,128)(2,1)} %get-tuple-element.149.attended, bf16[3,256,768]{2,1,0:T(8,128)(2,1)} %get-tuple-element.150.d_projected, bf16[256,768]{1,0:T(8,128)(2,1)} %get-tuple-element.151.d_branch), custom_call_target="tpu_custom_call" | custom-call | bytes 28800000 | tf_op jit(solution)/shard_map/pallas_call | solution.py:451
  329.4 6.4 %convolution_convert_fusion = bf16[768,2048]{1,0:T(8,128)(2,1)} fusion(bf16[640,768]{1,0:T(8,128)(2,1)} %bitcast.37.inputs, bf16[640,2048]{1,0:T(8,128)(2,1)} %get-tuple-element.142), kind=kOutput, calls=%fused_computation.5 | convolution fusion | flops 2014838784 | bytes 6750208 | tf_op jit(solution)/shard_map/dot_general | solution.py:30
  340.8 3.8 convolution_convert_fusion.2
  352.5 13.5 %shard_map.252 = (f32[256,768]{1,0:T(8,128)}, bf16[256,768]{1,0:T(8,128)(2,1)}, bf16[3,256,768]{2,1,0:T(8,128)(2,1)}, f32[2,768]{1,0:T(2,128)}) custom-call(f32[256,768]{1,0:T(8,128)} %get-tuple-element.129.d_result.refs_0_, f32[256,768]{1,0:T(8,128)} %get-tuple-element.134.refs_1_, bf16[320,768]{1,0:T(8,128)(2,1)} %pad_maximum_fusion.13.refs_2_, ...), custom_call_target="tpu_custom_call" | custom-call | bytes 50400000 | tf_op jit(solution)/shard_map/pallas_call | solution.py:451
  368.0 7.7 %shard_map.253 = bf16[2,2,4,2,112,768]{5,4,3,2,1,0:T(8,128)(2,1)} custom-call(bf16[256,768]{1,0:T(8,128)(2,1)} %get-tuple-element.102.normed, bf16[256,768]{1,0:T(8,128)(2,1)} %get-tuple-element.103.attended, bf16[3,256,768]{2,1,0:T(8,128)(2,1)} %get-tuple-element.158.d_projected, bf16[256,768]{1,0:T(8,128)(2,1)} %get-tuple-element.159.d_branch, ...), custom_call_target="tpu_custom_call" | custom-call | bytes 28800000 | tf_op jit(solution)/shard_map/pallas_call | solution.py:451
  381.9 4.5 all-to-all-start.1
  392.4 14.1 %all-to-all-done.1 = bf16[8,48,2048]{2,1,0:T(8,128)(2,1)} async-done(((bf16[8,48,2048]{2,1,0:T(8,128)(2,1)}), bf16[8,48,2048]{2,1,0:T(8,128)(2,1)}, u32[]{:S(2)}, u32[]{:S(2)}) %all-to-all-start.1) | async-done | bytes 1572896 | tf_op jit(solution)/shard_map/all_to_all | solution.py:537
  423.4 3.9 shard_map.254.h
  427.3 15.2 %collective-permute-done.58 = bf16[2,2,1,208,768]{4,3,1,0,2:T(8,128)(2,1)} collective-permute-done((bf16[2,2,1,208,768]{4,3,1,0,2:T(8,128)(2,1)}, bf16[2,2,1,208,768]{4,3,1,0,2:T(8,128)(2,1)}, u32[]{:S(2)}, u32[]{:S(2)}) %collective-permute-start.58) | collective-permute-done | bytes 1277984 | tf_op jit(solution)/shard_map/ppermute | solution.py:480
  450.1 5.1 all-to-all-done.2
  456.3 13.9 %collective-permute-done.60 = bf16[2,208,768]{2,1,0:T(8,128)(2,1)S(1)} collective-permute-done((bf16[2,208,768]{2,1,0:T(8,128)(2,1)S(1)}, bf16[2,208,768]{2,1,0:T(8,128)(2,1)S(1)}, u32[]{:S(2)}, u32[]{:S(2)}) %collective-permute-start.60) | collective-permute-done | bytes 639008 | tf_op jit(solution)/shard_map/ppermute | solution.py:480
  489.7 13.0 %collective-permute-done.62 = bf16[208,768]{1,0:T(8,128)(2,1)S(1)} collective-permute-done((bf16[208,768]{1,0:T(8,128)(2,1)}, bf16[208,768]{1,0:T(8,128)(2,1)S(1)}, u32[]{:S(2)}, u32[]{:S(2)}) %collective-permute-start.62) | collective-permute-done | bytes 319520 | tf_op jit(solution)/shard_map/ppermute | solution.py:480
  502.7 6.3 %collective-permute-done.63 = bf16[208,768]{1,0:T(8,128)(2,1)S(1)} collective-permute-done((bf16[208,768]{1,0:T(8,128)(2,1)}, bf16[208,768]{1,0:T(8,128)(2,1)S(1)}, u32[]{:S(2)}, u32[]{:S(2)}) %collective-permute-start.63) | collective-permute-done | bytes 319520 | tf_op jit(solution)/shard_map/ppermute | solution.py:480
  517.4 3.9 shard_map.257
  (448 shorter events, 240.2 us)
Async XLA Ops:
  7.2 150.1 %all-gather.7.cloned.1.call-start = ((), (), s32[]{:S(2)}) async-start(), calls=%async_computation.9 | async-start | bytes 1966080 | tf_op jit(solution)/shard_map/all_gather | solution.py:554
  16.1 141.2 %all-gather.5.cloned.1.call-start = ((), (), s32[]{:S(2)}) async-start(), calls=%async_computation.8 | async-start | bytes 3932160 | tf_op jit(solution)/shard_map/all_gather | solution.py:554
  17.1 18.4 %collective-permute-start = (bf16[112,768]{1,0:T(8,128)(2,1)S(1)}, bf16[112,768]{1,0:T(8,128)(2,1)S(1)}, u32[]{:S(2)}, u32[]{:S(2)}) collective-permute-start(bf16[112,768]{1,0:T(8,128)(2,1)S(1)} %get-tuple-element.282), channel_id=1, source_target_pairs={{0,4},{1,5},{2,6},{3,7},{4,8},{5,9},{6,10},{7,11},{8,12},{9,13},{1... | collective-permute-start | bytes 516104 | tf_op jit(solution)/shard_map/ppermute | solution.py:480
  18.7 27.8 %collective-permute-start.1 = (bf16[112,768]{1,0:T(8,128)(2,1)S(1)}, bf16[112,768]{1,0:T(8,128)(2,1)S(1)}, u32[]{:S(2)}, u32[]{:S(2)}) collective-permute-start(bf16[112,768]{1,0:T(8,128)(2,1)S(1)} %get-tuple-element.282), channel_id=1, source_target_pairs={{0,8},{1,9},{2,10},{3,11},{4,12},{5,13},{6,14},{7,15},{8,0},{9,1},... | collective-permute-start | bytes 516104 | tf_op jit(solution)/shard_map/ppermute | solution.py:480
  19.8 28.9 %collective-permute-start.2 = (bf16[112,768]{1,0:T(8,128)(2,1)S(1)}, bf16[112,768]{1,0:T(8,128)(2,1)S(1)}, u32[]{:S(2)}, u32[]{:S(2)}) collective-permute-start(bf16[112,768]{1,0:T(8,128)(2,1)S(1)} %get-tuple-element.282), channel_id=1, source_target_pairs={{0,12},{1,13},{2,14},{3,15},{4,0},{5,1},{6,2},{7,3},{8,4},{9,5},{1... | collective-permute-start | bytes 516104 | tf_op jit(solution)/shard_map/ppermute | solution.py:480
  64.9 162.3 %all-gather.11.cloned.1.call-start = ((), (), s32[]{:S(2)}) async-start(), calls=%async_computation.11 | async-start | bytes 1966080 | tf_op jit(solution)/shard_map/all_gather | solution.py:554
  65.0 17.7 %collective-permute-start.5 = (bf16[4,112,768]{2,1,0:T(8,128)(2,1)S(1)}, bf16[4,112,768]{2,1,0:T(8,128)(2,1)S(1)}, u32[]{:S(2)}, u32[]{:S(2)}) collective-permute-start(bf16[4,112,768]{2,1,0:T(8,128)(2,1)S(1)} %pad_maximum_fusion.8.refs_0_), channel_id=1, source_target_pairs={{0,16},{1,17},{2,18},{3,19},{4,20},{5,21},{6,22},{7,23},{8,24},{9,... | collective-permute-start | bytes 2064392 | tf_op jit(solution)/shard_map/ppermute | solution.py:480
  66.4 17.8 %collective-permute-start.4 = (bf16[4,112,768]{2,1,0:T(8,128)(2,1)S(1)}, bf16[4,112,768]{2,1,0:T(8,128)(2,1)S(1)}, u32[]{:S(2)}, u32[]{:S(2)}) collective-permute-start(bf16[4,112,768]{2,1,0:T(8,128)(2,1)S(1)} %pad_maximum_fusion.8.refs_0_), channel_id=1, source_target_pairs={{0,2},{1,3},{2,0},{3,1},{4,6},{5,7},{6,4},{7,5},{8,10},{9,11},{10,... | collective-permute-start | bytes 2064392 | tf_op jit(solution)/shard_map/ppermute | solution.py:480
  70.1 24.9 %collective-permute-start.8 = (bf16[4,112,768]{2,1,0:T(8,128)(2,1)S(1)}, bf16[4,112,768]{2,1,0:T(8,128)(2,1)}, u32[]{:S(2)}, u32[]{:S(2)}) collective-permute-start(bf16[4,112,768]{2,1,0:T(8,128)(2,1)S(1)} %pad_maximum_fusion.8.refs_0_), channel_id=1, source_target_pairs={{0,1},{1,0},{2,3},{3,2},{4,5},{5,4},{6,7},{7,6},{8,9},{9,8},{10,11... | collective-permute-start | bytes 2064392 | tf_op jit(solution)/shard_map/ppermute | solution.py:480
  125.8 103.3 %all-gather.9.cloned.1.call-start = ((), (), s32[]{:S(2)}) async-start(), calls=%async_computation.10 | async-start | bytes 3932160 | tf_op jit(solution)/shard_map/all_gather | solution.py:554
  125.9 19.9 %collective-permute-start.24 = (bf16[96,768]{1,0:T(8,128)(2,1)S(1)}, bf16[96,768]{1,0:T(8,128)(2,1)S(1)}, u32[]{:S(2)}, u32[]{:S(2)}) collective-permute-start(bf16[96,768]{1,0:T(8,128)(2,1)S(1)} %bitcast.214), channel_id=1, source_target_pairs={{0,4},{1,5},{2,6},{3,7},{4,8},{5,9},{6,10},{7,11},{8,12},{9,13},{1... | collective-permute-start | bytes 442376 | tf_op jit(solution)/shard_map/ppermute | solution.py:480
  126.0 19.9 %collective-permute-start.25 = (bf16[96,768]{1,0:T(8,128)(2,1)S(1)}, bf16[96,768]{1,0:T(8,128)(2,1)S(1)}, u32[]{:S(2)}, u32[]{:S(2)}) collective-permute-start(bf16[96,768]{1,0:T(8,128)(2,1)S(1)} %bitcast.215), channel_id=1, source_target_pairs={{0,8},{1,9},{2,10},{3,11},{4,12},{5,13},{6,14},{7,15},{8,0},{9,1},... | collective-permute-start | bytes 442376 | tf_op jit(solution)/shard_map/ppermute | solution.py:480
  128.6 18.3 %collective-permute-start.26 = (bf16[96,768]{1,0:T(8,128)(2,1)S(1)}, bf16[96,768]{1,0:T(8,128)(2,1)S(1)}, u32[]{:S(2)}, u32[]{:S(2)}) collective-permute-start(bf16[96,768]{1,0:T(8,128)(2,1)S(1)} %bitcast.216), channel_id=1, source_target_pairs={{0,12},{1,13},{2,14},{3,15},{4,0},{5,1},{6,2},{7,3},{8,4},{9,5},{1... | collective-permute-start | bytes 442376 | tf_op jit(solution)/shard_map/ppermute | solution.py:480
  147.1 21.9 %collective-permute-start.28 = (bf16[4,96,768]{2,1,0:T(8,128)(2,1)S(1)}, bf16[4,96,768]{2,1,0:T(8,128)(2,1)S(1)}, u32[]{:S(2)}, u32[]{:S(2)}) collective-permute-start(bf16[4,96,768]{2,1,0:T(8,128)(2,1)S(1)} %pad_maximum_fusion.9.refs_0_), channel_id=1, source_target_pairs={{0,16},{1,17},{2,18},{3,19},{4,20},{5,21},{6,22},{7,23},{8,24},{9,... | collective-permute-start | bytes 1769480 | tf_op jit(solution)/shard_map/ppermute | solution.py:480
  148.6 22.2 %collective-permute-start.27 = (bf16[4,96,768]{2,1,0:T(8,128)(2,1)S(1)}, bf16[4,96,768]{2,1,0:T(8,128)(2,1)S(1)}, u32[]{:S(2)}, u32[]{:S(2)}) collective-permute-start(bf16[4,96,768]{2,1,0:T(8,128)(2,1)S(1)} %pad_maximum_fusion.9.refs_0_), channel_id=1, source_target_pairs={{0,2},{1,3},{2,0},{3,1},{4,6},{5,7},{6,4},{7,5},{8,10},{9,11},{10,... | collective-permute-start | bytes 1769480 | tf_op jit(solution)/shard_map/ppermute | solution.py:480
  154.1 147.9 %reduce-scatter.5.cloned.1.call-start = ((), (), s32[]{:S(2)}) async-start(), calls=%async_computation.12 | async-start | bytes 1966080 | tf_op jit(solution)/shard_map/reduce_scatter | solution.py:559
  174.6 15.3 %collective-permute-start.32 = (bf16[4,96,768]{2,1,0:T(8,128)(2,1)S(1)}, bf16[4,96,768]{2,1,0:T(8,128)(2,1)}, u32[]{:S(2)}, u32[]{:S(2)}) collective-permute-start(bf16[4,96,768]{2,1,0:T(8,128)(2,1)S(1)} %collective-permute-done.27.refs_1_), channel_id=1, source_target_pairs={{0,1},{1,0},{2,3},{3,2},{4,5},{5,4},{6,7},{7,6},{8,9},{9,8},{10,11... | collective-permute-start | bytes 1769480 | tf_op jit(solution)/shard_map/ppermute | solution.py:480
  264.2 115.0 %reduce-scatter.7.cloned.1.call-start = ((), (), s32[]{:S(2)}) async-start(), calls=%async_computation.13 | async-start | bytes 3932160 | tf_op jit(solution)/shard_map/reduce_scatter | solution.py:559
  304.4 14.9 %all-to-all-start = ((bf16[4,128,768]{2,1,0:T(8,128)(2,1)}), bf16[4,128,768]{2,1,0:T(8,128)(2,1)S(1)}, u32[]{:S(2)}, u32[]{:S(2)}) async-start(bf16[4,128,768]{2,1,0:T(8,128)(2,1)} %pad_maximum_fusion.6), calls=%async_computation.1 | async-start | bytes 1572864 | tf_op jit(solution)/shard_map/all_to_all | solution.py:537
  308.1 109.7 %reduce-scatter.9.cloned.1.call-start = ((), (), s32[]{:S(2)}) async-start(), calls=%async_computation.14 | async-start | bytes 1966080 | tf_op jit(solution)/shard_map/reduce_scatter | solution.py:559
  328.8 20.1 %collective-permute-start.56 = (bf16[2,4,2,96,768]{4,3,2,1,0:T(8,128)(2,1)S(1)}, bf16[2,4,2,96,768]{4,3,2,1,0:T(8,128)(2,1)}, u32[]{:S(2)}, u32[]{:S(2)}) collective-permute-start(bf16[2,4,2,96,768]{4,3,2,1,0:T(8,128)(2,1)S(1)} %dynamic-slice_bitcast_fusion.1), channel_id=1, source_target_pairs={{0,1},{1,0},{2,3},{3,2},{4,5},{5,4},{6,7},{7,6},{8,9},{9,8},{10,11... | collective-permute-start | bytes 7077896 | tf_op jit(solution)/shard_map/ppermute | solution.py:480
  352.0 118.7 %reduce-scatter.11.cloned.1.call-start = ((), (), s32[]{:S(2)}) async-start(), calls=%async_computation.15 | async-start | bytes 3932160 | tf_op jit(solution)/shard_map/reduce_scatter | solution.py:559
  381.9 24.6 %all-to-all-start.1 = ((bf16[8,48,2048]{2,1,0:T(8,128)(2,1)}), bf16[8,48,2048]{2,1,0:T(8,128)(2,1)}, u32[]{:S(2)}, u32[]{:S(2)}) async-start(bf16[8,48,2048]{2,1,0:T(8,128)(2,1)} %pad_maximum_fusion.1), calls=%async_computation.3 | async-start | bytes 3145728 | tf_op jit(solution)/shard_map/all_to_all | solution.py:537
  411.1 31.3 %collective-permute-start.58 = (bf16[2,2,1,208,768]{4,3,1,0,2:T(8,128)(2,1)}, bf16[2,2,1,208,768]{4,3,1,0,2:T(8,128)(2,1)}, u32[]{:S(2)}, u32[]{:S(2)}) collective-permute-start(bf16[2,2,1,208,768]{4,3,1,0,2:T(8,128)(2,1)} %constant_dynamic-slice_fusion.1), channel_id=1, source_target_pairs={{0,2},{1,3},{2,0},{3,1},{4,6},{5,7},{6,4},{7,5},{8,10},{9,11},{10,... | collective-permute-start | bytes 3833864 | tf_op jit(solution)/shard_map/ppermute | solution.py:480
  417.2 31.3 %collective-permute-start.59 = (bf16[2,2,208,768]{3,2,1,0:T(8,128)(2,1)}, bf16[2,2,208,768]{3,2,1,0:T(8,128)(2,1)}, u32[]{:S(2)}, u32[]{:S(2)}) collective-permute-start(bf16[2,2,208,768]{3,2,1,0:T(8,128)(2,1)} %dynamic-slice_bitcast_fusion.2), channel_id=1, source_target_pairs={{0,16},{1,17},{2,18},{3,19},{4,20},{5,21},{6,22},{7,23},{8,24},{9,... | collective-permute-start | bytes 3833864 | tf_op jit(solution)/shard_map/ppermute | solution.py:480
  419.9 35.4 %all-to-all-start.2 = ((bf16[4,128,768]{2,1,0:T(8,128)(2,1)}), bf16[4,128,768]{2,1,0:T(8,128)(2,1)S(1)}, u32[]{:S(2)}, u32[]{:S(2)}) async-start(bf16[4,128,768]{2,1,0:T(8,128)(2,1)} %pad_maximum_fusion.7), calls=%async_computation.5 | async-start | bytes 1572864 | tf_op jit(solution)/shard_map/all_to_all | solution.py:537
  455.3 15.0 %collective-permute-start.60 = (bf16[2,208,768]{2,1,0:T(8,128)(2,1)S(1)}, bf16[2,208,768]{2,1,0:T(8,128)(2,1)S(1)}, u32[]{:S(2)}, u32[]{:S(2)}) collective-permute-start(bf16[2,208,768]{2,1,0:T(8,128)(2,1)S(1)} %dynamic-slice_bitcast_fusion.3), channel_id=1, source_target_pairs={{0,16},{1,17},{2,18},{3,19},{4,20},{5,21},{6,22},{7,23},{8,24},{9,... | collective-permute-start | bytes 1916936 | tf_op jit(solution)/shard_map/ppermute | solution.py:480
  455.7 14.7 %collective-permute-start.61 = (bf16[2,1,208,768]{3,2,1,0:T(8,128)(2,1)S(1)}, bf16[2,1,208,768]{3,2,1,0:T(8,128)(2,1)S(1)}, u32[]{:S(2)}, u32[]{:S(2)}) collective-permute-start(bf16[2,1,208,768]{3,2,1,0:T(8,128)(2,1)S(1)} %constant_dynamic-slice_fusion), channel_id=1, source_target_pairs={{0,2},{1,3},{2,0},{3,1},{4,6},{5,7},{6,4},{7,5},{8,10},{9,11},{10,... | collective-permute-start | bytes 1916936 | tf_op jit(solution)/shard_map/ppermute | solution.py:480
  473.4 38.7 %all-to-all-start.3 = ((bf16[8,48,2048]{2,1,0:T(8,128)(2,1)}), bf16[8,48,2048]{2,1,0:T(8,128)(2,1)S(1)}, u32[]{:S(2)}, u32[]{:S(2)}) async-start(bf16[8,48,2048]{2,1,0:T(8,128)(2,1)} %pad_maximum_fusion.2), calls=%async_computation.7 | async-start | bytes 3145728 | tf_op jit(solution)/shard_map/all_to_all | solution.py:537
  478.1 24.6 %collective-permute-start.62 = (bf16[208,768]{1,0:T(8,128)(2,1)}, bf16[208,768]{1,0:T(8,128)(2,1)S(1)}, u32[]{:S(2)}, u32[]{:S(2)}) collective-permute-start(bf16[208,768]{1,0:T(8,128)(2,1)} %get-tuple-element.236), channel_id=1, source_target_pairs={{0,4},{1,5},{2,6},{3,7},{4,8},{5,9},{6,10},{7,11},{8,12},{9,13},{1... | collective-permute-start | bytes 958472 | tf_op jit(solution)/shard_map/ppermute | solution.py:480
  480.8 28.1 %collective-permute-start.63 = (bf16[208,768]{1,0:T(8,128)(2,1)}, bf16[208,768]{1,0:T(8,128)(2,1)S(1)}, u32[]{:S(2)}, u32[]{:S(2)}) collective-permute-start(bf16[208,768]{1,0:T(8,128)(2,1)} %get-tuple-element.238), channel_id=1, source_target_pairs={{0,8},{1,9},{2,10},{3,11},{4,12},{5,13},{6,14},{7,15},{8,0},{9,1},... | collective-permute-start | bytes 958472 | tf_op jit(solution)/shard_map/ppermute | solution.py:480
  483.1 27.7 %collective-permute-start.64 = (bf16[208,768]{1,0:T(8,128)(2,1)}, bf16[208,768]{1,0:T(8,128)(2,1)}, u32[]{:S(2)}, u32[]{:S(2)}) collective-permute-start(bf16[208,768]{1,0:T(8,128)(2,1)} %get-tuple-element.237), channel_id=1, source_target_pairs={{0,12},{1,13},{2,14},{3,15},{4,0},{5,1},{6,2},{7,3},{8,4},{9,5},{1... | collective-permute-start | bytes 958472 | tf_op jit(solution)/shard_map/ppermute | solution.py:480
  (101 other events, 777.6 us)
Sparse Core Ops, SparseCore 0:
  16.2 42.8 all-gather.6
  65.1 62.1 all-gather.4
  128.8 37.7 all-gather.10
  168.0 61.0 all-gather.8
  264.3 35.1 reduce-scatter.4
  301.6 59.8 reduce-scatter.6
  363.8 34.6 reduce-scatter.8
  400.9 59.8 reduce-scatter.10
